TPU v7x, 256 devices: a whole 4x4x8 slice. The times are simulated.
256 devices in a mesh: blk: 128 (over y, x_lo, z, core), rel: 2 (over x_hi).
Axes of the slice: x: 4 (x_hi: 2, x_lo: 2; x = x_hi * 2 + x_lo), y: 4, z: 8, core: 2. Of those that a mesh axis runs over, the one named last changes fastest.
Arguments:
- lhs_table: float32 [400, 32768], P(None, 'blk'), may hold values from -1.5 to 1.5
- rhs_table: float32 [400, 32768], P(None, 'blk'), may hold values from -1.5 to 1.5
- rel_table: float32 [400, 1280], P(None, 'rel'), may hold values from -2.4 to 2.4
- lhs_acc: float32 [32768], P('blk'), may hold values from 0.001 to 0.03
- rhs_acc: float32 [32768], P('blk'), may hold values from 0.001 to 0.03
- rel_acc: float32 [1280], P('rel'), may hold values from 0.003 to 3
- lhs_index: int32 [128, 2, 2, 1024], P('blk', 'rel'), may hold values from 0 to 255
- rhs_index: int32 [128, 2, 2, 1024], P('blk', 'rel'), may hold values from 0 to 255
- rel_index: int32 [128, 2, 2, 1024], P('blk', 'rel'), may hold values from 0 to 639
- bucket_ends: int32 [128, 2, 2], P('blk', 'rel'), may hold values from 1 to 1024, as said below
- neg_index: int32 [128, 2, 2, 4, 128], P('blk', 'rel'), may hold values from 0 to 255
Outputs:
- lhs_out: float32 [400, 32768], P(None, 'blk')
- lhs_acc_out: float32 [32768], P('blk')
- rhs_out: float32 [400, 32768], P(None, 'blk')
- rhs_acc_out: float32 [32768], P('blk')
- rel_out: float32 [400, 1280], P(None, 'rel')
- rel_acc_out: float32 [1280], P('rel')
Inputs may be any that keep to these rules, and one draw needn't show every extreme that they name: Only the first bucket_ends slots of a bucket are live; every other slot, and every span without a live slot, is ignored. In every round at least one bucket is full.
All inputs are finite; a program needn't handle non-finite values.
Results may differ from a plain program's by a relative error of at most 0.0003.
Values sent between devices are 32-bit elements; how exact they have to be, the bound alone decides.
No kernel may reach another device: no remote copies, remote signals or barrier semaphores. Data moves between devices by JAX's collectives and lax.ppermute only.
A program may use at most 64 MiB of HBM per device.

v0:
```python
import jax
import jax.numpy as jnp
from jax import lax
from jax.sharding import PartitionSpec as P

STEP_SIZE = 0.2


def from_behind(value, axis, steps):
    count = lax.axis_size(axis)
    pairs = [(source, (source + steps) % count) for source in range(count)]
    return lax.ppermute(value, axis, pairs)


def adagrad_rows(table, accumulator, gradient):
    grown = accumulator + jnp.mean(gradient * gradient, axis=0)
    return (table - STEP_SIZE * gradient * lax.rsqrt(grown)[None, :], grown)


def bucket_gradients(
    lhs_slab,
    context_slab,
    relation_half,
    lhs_slots,
    rhs_slots,
    relation_slots,
    live_count,
    negative_slots,
):
    edge_count = lhs_slots.shape[0]
    span_count, negative_count = negative_slots.shape
    span_width = edge_count // span_count
    feature_count = lhs_slab.shape[0]
    live = (lax.iota(jnp.int32, edge_count) < live_count).astype(jnp.float32)
    left_rows = jnp.take(lhs_slab, lhs_slots, axis=1)
    right_rows = jnp.take(context_slab, rhs_slots, axis=1)
    weights = jnp.take(relation_half, relation_slots, axis=1)
    scaled = left_rows * weights
    positive = jnp.sum(scaled * right_rows, axis=0)
    flat_negatives = negative_slots.reshape(-1)
    negative_rows = jnp.take(context_slab, flat_negatives, axis=1).reshape(
        feature_count, span_count, negative_count
    )
    scaled_blocks = scaled.reshape(feature_count, span_count, span_width)
    negative = jnp.einsum(
        "dcw,dcn->cwn", scaled_blocks, negative_rows, precision=lax.Precision.HIGHEST
    )
    positive_coef = -jax.nn.sigmoid(-positive) * live
    negative_coef = jax.nn.sigmoid(negative) * (
        live.reshape(span_count, span_width, 1) / negative_count
    )
    mixture = jnp.einsum(
        "cwn,dcn->dcw", negative_coef, negative_rows, precision=lax.Precision.HIGHEST
    ).reshape(feature_count, edge_count)
    toward = positive_coef[None, :] * right_rows + mixture
    negative_grad = jnp.einsum(
        "cwn,dcw->dcn", negative_coef, scaled_blocks, precision=lax.Precision.HIGHEST
    ).reshape(feature_count, span_count * negative_count)
    lhs_grad = jnp.zeros_like(lhs_slab).at[:, lhs_slots].add(weights * toward)
    context_grad = (
        jnp.zeros_like(context_slab).at[:, rhs_slots].add(positive_coef[None, :] * scaled)
    )
    context_grad = context_grad.at[:, flat_negatives].add(negative_grad)
    relation_grad = jnp.zeros_like(relation_half).at[:, relation_slots].add(left_rows * toward)
    return (lhs_grad, context_grad, relation_grad)


def per_device(
    lhs_table,
    rhs_table,
    rel_table,
    lhs_acc,
    rhs_acc,
    rel_acc,
    lhs_index,
    rhs_index,
    rel_index,
    bucket_ends,
    neg_index,
):
    round_count = lhs_index.shape[2]
    for t in range(round_count):
        if t > 0:
            rhs_table, rhs_acc = from_behind((rhs_table, rhs_acc), "blk", 1)
        lhs_grad, context_grad, relation_grad = bucket_gradients(
            lhs_table,
            rhs_table,
            rel_table,
            lhs_index[0, 0, t],
            rhs_index[0, 0, t],
            rel_index[0, 0, t],
            bucket_ends[0, 0, t],
            neg_index[0, 0, t],
        )
        lhs_sum, context_sum = lax.psum((lhs_grad, context_grad), "rel")
        lhs_table, lhs_acc = adagrad_rows(lhs_table, lhs_acc, lhs_sum)
        rhs_table, rhs_acc = adagrad_rows(rhs_table, rhs_acc, context_sum)
        relation_sum = lax.psum(relation_grad, "blk")
        rel_table, rel_acc = adagrad_rows(rel_table, rel_acc, relation_sum)
    return (lhs_table, lhs_acc, rhs_table, rhs_acc, rel_table, rel_acc)


def solution(mesh):
    in_specs = (
        P(None, "blk"),
        P(None, "blk"),
        P(None, "rel"),
        P("blk"),
        P("blk"),
        P("rel"),
        P("blk", "rel", None, None),
        P("blk", "rel", None, None),
        P("blk", "rel", None, None),
        P("blk", "rel", None),
        P("blk", "rel", None, None, None),
    )
    out_specs = (P(None, "blk"), P("blk"), P(None, "blk"), P("blk"), P(None, "rel"), P("rel"))
    return jax.shard_map(
        per_device, mesh=mesh, in_specs=in_specs, out_specs=out_specs, check_vma=False
    )
```

profile of v0, /device:TPU:1, one launch (start us, length us, event | category | flops | bytes accessed | tf_op | source)
XLA Modules:
  0.0 2306.6 jit_solution(12612314209476920770)
XLA Ops:
  13.4 1.3 fusion.58
  15.4 1.2 copy.37
  16.6 1.2 copy.44
  18.2 2.3 gather_fusion.3
  20.6 4.9 gather_fusion.2
  25.5 1.4 broadcast_select_fusion.1
  26.8 4.9 gather_fusion
  31.8 4.9 gather_fusion.1
  36.6 3.3 fusion.13
  40.0 2.0 fusion.27
  42.0 3.1 convolution_bitcast_fusion.1
  45.1 3.5 convolution_bitcast_fusion.3
  49.3 1.4 copy.48
  50.7 2.9 copy.69
  53.6 3.9 bitcast_add_fusion.1
  57.5 8.4 scatter_custom_fusion.2
  65.8 4.5 scatter_fusion
  70.4 9.1 scatter_custom_fusion
  79.6 9.3 scatter_custom_fusion.1
  89.7 47.2 %all-reduce.13.cloned.1.call-done = (f32[400,256]{0,1:T(8,128)}, f32[400,256]{0,1:T(8,128)}) async-done(((f32[400,256]{0,1:T(8,128)}, f32[400,256]{0,1:T(8,128)}), (f32[400,256]{0,1:T(8,128)}, f32[400,256]{0,1:T(8,128)})) %all-reduce.13.cloned.1.call-update) | async-done | bytes 819216 | tf_op jit(solution)/shard_map/psum | solution.py:95
  136.9 1.2 multiply_reduce_fusion.4
  138.1 1.2 multiply_subtract_fusion.4
  139.3 1.9 collective-permute-start
  141.5 5.1 gather_fusion.5
  146.6 1014.0 %all-reduce.7.cloned.1.call-done = f32[400,640]{0,1:T(8,128)} async-done(((f32[400,640]{0,1:T(8,128)}), f32[400,640]{0,1:T(8,128)}) %all-reduce.7.cloned.1.call-update) | async-done | bytes 1024016 | tf_op jit(solution)/shard_map/psum | solution.py:98
  1160.5 1.6 multiply_reduce_fusion.1
  1162.2 1.3 multiply_subtract_fusion.1
  1163.6 6.6 gather_fusion.4
  1170.2 2.3 gather_fusion.7
  1172.5 1.4 broadcast_select_fusion
  1173.9 4.9 gather_fusion.6
  1178.8 3.3 fusion.6
  1182.2 2.0 fusion.23
  1184.2 3.2 convolution_bitcast_fusion
  1187.3 3.5 convolution_bitcast_fusion.2
  1192.6 2.5 copy.57
  1195.1 1.9 copy.70
  1196.9 8.1 scatter_custom_fusion.5
  1205.1 3.9 bitcast_add_fusion
  1209.0 9.0 scatter_custom_fusion.4
  1218.0 3.8 scatter_fusion.1
  1222.8 9.3 scatter_custom_fusion.7
  1232.1 40.5 %all-reduce.11.cloned.1.call-done = (f32[400,256]{0,1:T(8,128)}, f32[400,256]{0,1:T(8,128)}) async-done(((f32[400,256]{0,1:T(8,128)}, f32[400,256]{0,1:T(8,128)}), (f32[400,256]{0,1:T(8,128)}, f32[400,256]{0,1:T(8,128)})) %all-reduce.11.cloned.1.call-update) | async-done | bytes 819216 | tf_op jit(solution)/shard_map/psum | solution.py:95
  1272.6 1.2 multiply_reduce_fusion.3
  1274.4 1.2 multiply_subtract_fusion.3
  1278.2 1017.8 %all-reduce.9.cloned.1.call-done = f32[400,640]{0,1:T(8,128)} async-done(((f32[400,640]{0,1:T(8,128)}), f32[400,640]{0,1:T(8,128)}) %all-reduce.9.cloned.1.call-update) | async-done | bytes 1024016 | tf_op jit(solution)/shard_map/psum | solution.py:98
  2296.1 1.6 multiply_reduce_fusion
  2298.5 1.3 copy.60
  (86 shorter events, 16.0 us)
Async XLA Ops:
  7.2 10.7 copy-start.11
  7.2 129.7 %all-reduce.13.cloned.1.call-start = ((), (), s32[]{:S(2)}) async-start(), calls=%async_computation.3 | async-start | bytes 2097152 | tf_op jit(solution)/shard_map/psum | solution.py:95
  40.0 5.1 copy-start.3
  70.3 9.1 copy-start.2
  70.3 9.2 copy-start.12
  79.5 1081.0 %all-reduce.7.cloned.1.call-start = ((), (), s32[]{:S(2)}) async-start(), calls=%async_computation | async-start | bytes 2621440 | tf_op jit(solution)/shard_map/psum | solution.py:98
  79.6 58.5 %copy-start.15 = (f32[256]{0:T(256)S(1)}, f32[256]{0:T(256)}, u32[]{:S(2)}) copy-start(f32[256]{0:T(256)} %param.21) | copy-start | bytes 3076
  88.9 52.5 %copy-start.14 = (f32[256]{0:T(256)S(1)}, f32[256]{0:T(256)}, u32[]{:S(2)}) copy-start(f32[256]{0:T(256)} %param.20) | copy-start | bytes 3076
  88.9 1183.7 %all-reduce.11.cloned.1.call-start = ((), (), s32[]{:S(2)}) async-start(), calls=%async_computation.2 | async-start | bytes 2097152 | tf_op jit(solution)/shard_map/psum | solution.py:95
  136.9 4.3 copy-start.9
  139.3 1030.9 %collective-permute-start = (f32[400,256]{0,1:T(8,128)S(1)}, f32[400,256]{0,1:T(8,128)S(1)}, u32[]{:S(2)}, u32[]{:S(2)}) collective-permute-start(f32[400,256]{0,1:T(8,128)S(1)} %multiply_subtract_fusion.4), channel_id=1, source_target_pairs={{0,2},{2,4},{4,6},{6,8},{8,10},{10,12},{12,14},{14,16},{16,18},{18... | collective-permute-start | bytes 1228808 | tf_op jit(solution)/shard_map/ppermute | solution.py:12
  141.5 1020.6 %copy-start.13 = (f32[640]{0:T(1024)S(1)}, f32[640]{0:T(1024)}, u32[]{:S(2)}) copy-start(f32[640]{0:T(1024)} %param.22) | copy-start | bytes 7684
  1160.5 1.7 copy-start.6
  1182.1 5.2 copy-start.4
  1190.8 4.3 copy-start.5
  1209.0 9.1 copy-start.8
  1221.8 0.8 copy-start.1
  1222.7 1073.4 %all-reduce.9.cloned.1.call-start = ((), (), s32[]{:S(2)}) async-start(), calls=%async_computation.1 | async-start | bytes 2621440 | tf_op jit(solution)/shard_map/psum | solution.py:98
  1222.7 53.9 %collective-permute-start.1 = (f32[256]{0:T(256)S(1)}, f32[256]{0:T(256)S(1)}, u32[]{:S(2)}, u32[]{:S(2)}) collective-permute-start(f32[256]{0:T(256)S(1)} %get-tuple-element.34), channel_id=1, source_target_pairs={{0,2},{2,4},{4,6},{6,8},{8,10},{10,12},{12,14},{14,16},{16,18},{18... | collective-permute-start | bytes 3080 | tf_op jit(solution)/shard_map/ppermute | solution.py:12
  1272.6 3.0 copy-start.10
  1276.6 1021.7 %copy-start = (f32[400,640]{0,1:T(8,128)S(1)}, f32[400,640]{0,1:T(8,128)}, u32[]{:S(2)}) copy-start(f32[400,640]{0,1:T(8,128)} %multiply_subtract_fusion.1) | copy-start | bytes 3072004
  2296.1 2.2 copy-start.7
Sparse Core Ops, SparseCore 0:
  79.6 57.2 all-reduce.12
  139.7 1020.7 all-reduce.6
  1222.8 49.7 all-reduce.10
  1275.3 1020.7 all-reduce.8
where the time goes:
time: 2320 us; the launch traced here: 2310 us
  waiting for transfers between devices  2120 us (91%)
  other arithmetic  96.3 us (4%)
  local copies, waits for them, and re-layouts  57 us (2%)
    psum x2, waiting for transfers between devices, per_device(): relation_sum = lax.psum(relation_grad, 'blk')  2030 us
    psum x2, waiting for transfers between devices, per_device(): lhs_sum, context_sum = lax.psum((lhs_grad, context_grad), 'rel')  87.7 us
  transfers between devices with their start and end apart: 6, of which 4 were waited for; matrix products, arithmetic and copies ran while one was open for 2% of the time, Pallas kernels for 0%

commit v1 on v0

v1 whole, which is shorter than its diff:
```python
import functools

import jax
import jax.numpy as jnp
from jax import lax
from jax.experimental import pallas as pl
from jax.experimental.pallas import tpu as pltpu
from jax.sharding import PartitionSpec as P

STEP_SIZE = 0.2
F32 = jnp.float32
BF16 = jnp.bfloat16
LANES = 128
VMEM_LIMIT = 48 * 1024 * 1024


def split(x):
    hi = x.astype(BF16)
    return hi, (x - hi.astype(F32)).astype(BF16)


def nn(a, b):
    return jnp.dot(a, b, preferred_element_type=F32)


def nt(a, b):
    return lax.dot_general(a, b, (((1,), (1,)), ((), ())), preferred_element_type=F32)


def one_hot(row, count):
    ids = lax.broadcasted_iota(jnp.int32, (count, row.shape[1]), 0)
    return jnp.where(ids == row, 1.0, 0.0).astype(BF16)


def adagrad(table, acc, grad):
    grown = acc + jnp.sum(grad * grad, axis=0, keepdims=True) * (1.0 / grad.shape[0])
    return table - STEP_SIZE * grad * lax.rsqrt(grown), grown


def gradients(t, refs, lhs_ref, rhs_ref, rel_ref, outs):
    (lidx, ridx, widx, nidx, ends) = refs
    (glhs_ref, gctx_ref, grel_ref) = outs
    d, rows = lhs_ref.shape
    rels = rel_ref.shape[1]
    edges = lidx.shape[1]
    neg = nidx.shape[1]
    spans = nidx.shape[0] // lidx.shape[0]
    width = edges // spans
    live_count = ends[t]
    lhi, llo = split(lhs_ref[...])
    rhi, rlo = split(rhs_ref[...])
    whi, wlo = split(rel_ref[...])
    for c in range(spans):
        at = pl.ds(c * width, width)
        hot_l = one_hot(lidx[pl.ds(t, 1), at], rows)
        hot_r = one_hot(ridx[pl.ds(t, 1), at], rows)
        hot_w = one_hot(widx[pl.ds(t, 1), at], rels)
        hot_n = one_hot(nidx[pl.ds(t * spans + c, 1), :], rows)
        left = nn(lhi, hot_l) + nn(llo, hot_l)
        right = nn(rhi, hot_r) + nn(rlo, hot_r)
        weights = nn(whi, hot_w) + nn(wlo, hot_w)
        qh32 = nn(rhi, hot_n)
        ql32 = nn(rlo, hot_n)
        qh, ql = qh32.astype(BF16), ql32.astype(BF16)
        qht, qlt = qh32.T.astype(BF16), ql32.T.astype(BF16)
        scaled = left * weights
        sh, sl = split(scaled)
        scores = nn(qht, sh) + (nn(qht, sl) + nn(qlt, sh))
        slot = lax.broadcasted_iota(jnp.int32, (1, width), 1) + c * width
        live = jnp.where(slot < live_count, 1.0, 0.0)
        coef = jax.nn.sigmoid(scores) * (live / neg)
        positive = jnp.sum(scaled * right, axis=0, keepdims=True)
        pcoef = -jax.nn.sigmoid(-positive) * live
        ch, cl = split(coef)
        toward = pcoef * right + (nn(qh, ch) + (nn(qh, cl) + nn(ql, ch)))
        ngh, ngl = split(nt(sh, ch) + (nt(sh, cl) + nt(sl, ch)))
        uh, ul = split(left * toward)
        grel = nt(uh, hot_w) + nt(ul, hot_w)
        vh, vl = split(weights * toward)
        glhs = nt(vh, hot_l) + nt(vl, hot_l)
        ph, pw = split(pcoef * scaled)
        gctx = nt(ph, hot_r) + nt(pw, hot_r) + nt(ngh, hot_n) + nt(ngl, hot_n)
        for b in range(rels // LANES):
            part = grel[:, b * LANES:(b + 1) * LANES]
            if c == 0:
                grel_ref[pl.ds(b * d, d), :] = part
            else:
                grel_ref[pl.ds(b * d, d), :] += part
        if c == 0:
            glhs_ref[...] = glhs
            gctx_ref[...] = gctx
        else:
            glhs_ref[...] += glhs
            gctx_ref[...] += gctx


def halves(core, grel_ref, keep_ref, send_ref, used):
    half = keep_ref.shape[0]
    grel_ref[pl.ds(used, grel_ref.shape[0] - used), :] = jnp.zeros(
        (grel_ref.shape[0] - used, LANES), F32
    )
    keep_ref[...] = grel_ref[pl.ds(pl.multiple_of(core * half, half), half), :]
    send_ref[...] = grel_ref[pl.ds(pl.multiple_of((1 - core) * half, half), half), :]


def first_kernel(lidx, ridx, widx, nidx, ends, core, lhs, rhs, rel,
                 glhs, gctx, keep, send, grel):
    gradients(0, (lidx, ridx, widx, nidx, ends), lhs, rhs, rel, (glhs, gctx, grel))
    halves(core[0], grel, keep, send, rel.shape[0] * (rel.shape[1] // LANES))


def join(core, mine, other, grel):
    half = mine.shape[0]
    grel[pl.ds(pl.multiple_of(core * half, half), half), :] = mine[...]
    grel[pl.ds(pl.multiple_of((1 - core) * half, half), half), :] = other[...]


def update_rel(rel, racc, grel, rel_new, racc_new):
    d = rel.shape[0]
    for b in range(rel.shape[1] // LANES):
        at = pl.ds(b * LANES, LANES)
        g = grel[pl.ds(b * d, d), :]
        rel_new[:, at], racc_new[:, at] = adagrad(rel[:, at], racc[:, at], g)


def update_pair(table, acc, one, two, table_new, acc_new):
    table_new[...], acc_new[...] = adagrad(table[...], acc[...], one[...] + two[...])


def second_kernel(lidx, ridx, widx, nidx, ends, core, lhs, rhs, rel, lacc, racc, wacc,
                  gl_a, gl_b, gc_a, gc_b, gw_mine, gw_other,
                  glhs, gctx, keep, send, lhs_new, rhs_new, rel_new,
                  lacc_new, racc_new, wacc_new, grel):
    update_pair(lhs, lacc, gl_a, gl_b, lhs_new, lacc_new)
    update_pair(rhs, racc, gc_a, gc_b, rhs_new, racc_new)
    join(core[0], gw_mine, gw_other, grel)
    update_rel(rel, wacc, grel, rel_new, wacc_new)
    gradients(1, (lidx, ridx, widx, nidx, ends), lhs_new, rhs_new, rel_new, (glhs, gctx, grel))
    halves(core[0], grel, keep, send, rel.shape[0] * (rel.shape[1] // LANES))


def pair_kernel(lhs, rhs, lacc, racc, gl_a, gl_b, gc_a, gc_b, lhs_new, rhs_new, lacc_new, racc_new):
    update_pair(lhs, lacc, gl_a, gl_b, lhs_new, lacc_new)
    update_pair(rhs, racc, gc_a, gc_b, rhs_new, racc_new)


def rel_kernel(core, rel, wacc, gw_mine, gw_other, rel_new, wacc_new, grel):
    join(core[0], gw_mine, gw_other, grel)
    update_rel(rel, wacc, grel, rel_new, wacc_new)


VM = pl.BlockSpec(memory_space=pltpu.VMEM)
SM = pl.BlockSpec(memory_space=pltpu.SMEM)


def call(kernel, ins, smem_at, outs, scratch, flops):
    return pl.pallas_call(
        kernel,
        out_shape=[jax.ShapeDtypeStruct(s, F32) for s in outs],
        in_specs=[SM if i in smem_at else VM for i in range(len(ins))],
        out_specs=[VM] * len(outs),
        scratch_shapes=[pltpu.VMEM(s, F32) for s in scratch],
        compiler_params=pltpu.CompilerParams(vmem_limit_bytes=VMEM_LIMIT),
        cost_estimate=pl.CostEstimate(
            flops=flops, bytes_accessed=8_000_000, transcendentals=0
        ),
    )(*ins)


def place(y, x, z, core):
    return y * 32 + x * 16 + z * 2 + core


def chip_chunk(y, x, z):
    return ((((y ^ (y >> 1)) & 1) * 2 + x) * 2) + ((z ^ (z >> 1)) & 1)


def cube_groups():
    groups = []
    for core in range(2):
        for yh in range(2):
            for zh in range(4):
                members = [None] * 8
                for yl in range(2):
                    for x in range(2):
                        for zl in range(2):
                            y, z = yh * 2 + yl, zh * 2 + zl
                            members[chip_chunk(y, x, z)] = place(y, x, z, core)
                groups.append(members)
    return groups


def pairs(move):
    out = []
    for y in range(4):
        for x in range(2):
            for z in range(8):
                for core in range(2):
                    a = place(y, x, z, core)
                    out.append((a, place(*move(y, x, z, core))))
    return out


CORE_PAIRS = pairs(lambda y, x, z, c: (y, x, z, 1 - c))
FAR_PAIRS = (
    pairs(lambda y, x, z, c: (3 - y, x, z, c)),
    pairs(lambda y, x, z, c: (y, x, (z + (1 if z % 2 else 7)) % 8, c)),
    pairs(lambda y, x, z, c: (y, x, z ^ (3 if z in (0, 3, 4, 7) else 7), c)),
)


def sum_over_blk(keep, send):
    part = keep + lax.ppermute(send, "blk", CORE_PAIRS)
    rows = part.shape[0] // 8
    groups = cube_groups()
    got = lax.all_to_all(
        part.reshape(8, rows, LANES), "blk", 0, 0, axis_index_groups=groups
    )
    total = jnp.sum(got, axis=0)
    for move in FAR_PAIRS:
        total = total + lax.ppermute(total, "blk", move)
    spread = jnp.broadcast_to(total[None], (8, rows, LANES))
    mine = lax.all_to_all(spread, "blk", 0, 0, axis_index_groups=groups)
    mine = mine.reshape(8 * rows, LANES)
    return mine, lax.ppermute(mine, "blk", CORE_PAIRS)


def swap(x):
    return lax.ppermute(x, "rel", [(0, 1), (1, 0)])


def onward(x, flip):
    n = lax.axis_size("blk")
    moves = [
        (2 * b + k, 2 * ((b + 1) % n) + (1 - k if flip else k)) for b in range(n) for k in range(2)
    ]
    return lax.ppermute(x, ("blk", "rel"), moves)


def per_device(lhs, rhs, rel, lacc, racc, wacc, lidx, ridx, widx, ends, nidx):
    d, rows = lhs.shape
    rels = rel.shape[1]
    rounds, edges = lidx.shape[2:]
    spans, neg = nidx.shape[3:]
    lidx, ridx, widx = (a.reshape(rounds, edges) for a in (lidx, ridx, widx))
    nidx = nidx.reshape(rounds * spans, neg)
    ends = ends.reshape(rounds)
    lacc, racc, wacc = (a.reshape(1, -1) for a in (lacc, racc, wacc))
    core = lax.rem(lax.axis_index("blk"), 2).astype(jnp.int32).reshape(1)
    used = d * (rels // LANES)
    full = -(-used // 2048) * 2048
    slab, table, state = (d, rows), (d, rels), (1, rows)
    half = (full // 2, LANES)
    index = (lidx, ridx, widx, nidx, ends, core)

    rhs_next = onward(rhs, False)
    racc_next = onward(racc, False)
    glhs, gctx, keep, send = call(
        first_kernel, index + (lhs, rhs, rel), (4, 5), [slab, slab, half, half],
        [(full, LANES)], 4_000_000_000,
    )
    gw_mine, gw_other = sum_over_blk(keep, send)
    gl_other = swap(glhs)
    gc_a = onward(gctx, False)
    gc_b = onward(gctx, True)
    glhs, gctx, keep, send, lhs, rhs, rel, lacc, racc, wacc = call(
        second_kernel,
        index + (lhs, rhs_next, rel, lacc, racc_next, wacc,
                 glhs, gl_other, gc_a, gc_b, gw_mine, gw_other),
        (4, 5),
        [slab, slab, half, half, slab, slab, table, state, state, (1, rels)],
        [(full, LANES)], 4_000_000_000,
    )
    gw_mine, gw_other = sum_over_blk(keep, send)
    gl_other = swap(glhs)
    gc_other = swap(gctx)
    lhs, rhs, lacc, racc = call(
        pair_kernel, (lhs, rhs, lacc, racc, glhs, gl_other, gctx, gc_other), (),
        [slab, slab, state, state], [], 1_000_000,
    )
    rel, wacc = call(
        rel_kernel, (core, rel, wacc, gw_mine, gw_other), (0,), [table, (1, rels)],
        [(full, LANES)], 1_000_000,
    )
    return lhs, lacc.reshape(-1), rhs, racc.reshape(-1), rel, wacc.reshape(-1)


def solution(mesh):
    in_specs = (
        P(None, "blk"),
        P(None, "blk"),
        P(None, "rel"),
        P("blk"),
        P("blk"),
        P("rel"),
        P("blk", "rel", None, None),
        P("blk", "rel", None, None),
        P("blk", "rel", None, None),
        P("blk", "rel", None),
        P("blk", "rel", None, None, None),
    )
    out_specs = (P(None, "blk"), P("blk"), P(None, "blk"), P("blk"), P(None, "rel"), P("rel"))
    return jax.shard_map(
        per_device, mesh=mesh, in_specs=in_specs, out_specs=out_specs, check_vma=False
    )
```

time: 2320 us -> 174 us (0.07)
  waiting for transfers between devices: 2120 us -> 67.2 us
  other arithmetic: 96.3 us -> 0.85 us
  local copies, waits for them, and re-layouts: 57 us -> 5.29 us
  blocking collectives: 0 us -> 43.1 us
  starting transfers between devices: 2.16 us -> 32.9 us
  Pallas kernels: 0 us -> 23.2 us
    psum x4 -> x0, waiting for transfers between devices: 2120 us -> none  [the longest x2 2030 us: per_device(): relation_sum = lax.psum(relation_grad, 'blk')]
    ppermute x2 -> x17, waiting for transfers between devices: 0.01 us -> 67.2 us  [the longest x3 37.3 us: swap(): return lax.ppermute(x, 'rel', [(0, 1), (1, 0)])]
    scatter-add x8 -> x0, other arithmetic: 61.5 us -> none  [the longest x2 18.6 us: bucket_gradients(): jnp.zeros_like(relation_half).at[:, relation_slots].add(left_rows * toward)]
    all_to_all x0 -> x4, blocking collectives: none -> 43.1 us  [the longest x2 23.7 us: sum_over_blk(): lax.all_to_all(part.reshape(8, rows, LANES), 'blk', 0, 0, axis_index_grou...]
    gather x8 -> x0, local copies, waits for them, and re-layouts: 36 us -> none  [the longest x2 11.6 us: bucket_gradients(): weights = jnp.take(relation_half, relation_slots, axis=1)]
    ppermute x2 -> x17, starting transfers between devices: 1.99 us -> 32.9 us  [the longest x2 11.6 us: sum_over_blk(): return (mine, lax.ppermute(mine, 'blk', CORE_PAIRS))]
    pallas_call x0 -> x4, Pallas kernels: none -> 23.2 us  [call(): pl.pallas_call(kernel, out_shape=[jax.ShapeDtypeStruct(s, F32) for s in o...]
  transfers between devices with their start and end apart: 6 -> 17, of which waited for: 4 -> 13; matrix products, arithmetic and copies ran while one was open for 2% -> 0% of each run, Pallas kernels for 0% -> 1%
where the time goes in v1:
time: 174 us; the launch traced here: 173 us
  waiting for transfers between devices  67.2 us (39%)
  blocking collectives  43.1 us (25%)
  starting transfers between devices  32.9 us (19%)
  Pallas kernels  23.2 us (13%)
  local copies, waits for them, and re-layouts  5.29 us (3%)
    ppermute x3, waiting for transfers between devices, swap(): return lax.ppermute(x, 'rel', [(0, 1), (1, 0)])  37.3 us
    all_to_all x2, blocking collectives, sum_over_blk(): lax.all_to_all(part.reshape(8, rows, LANES), 'blk', 0, 0, axis_index_grou...  23.7 us
    pallas_call x4, Pallas kernels, call(): pl.pallas_call(kernel, out_shape=[jax.ShapeDtypeStruct(s, F32) for s in o...  23.2 us
    ppermute x6, waiting for transfers between devices, sum_over_blk(): total = total + lax.ppermute(total, 'blk', move)  21 us
    all_to_all x2, blocking collectives, sum_over_blk(): mine = lax.all_to_all(spread, 'blk', 0, 0, axis_index_groups=groups)  19.4 us
    ppermute x2, starting transfers between devices, sum_over_blk(): return (mine, lax.ppermute(mine, 'blk', CORE_PAIRS))  11.6 us
    ppermute x6, starting transfers between devices, sum_over_blk(): total = total + lax.ppermute(total, 'blk', move)  10.3 us
    ppermute x4, waiting for transfers between devices, onward(): return lax.ppermute(x, ('blk', 'rel'), moves)  5.5 us
  transfers between devices with their start and end apart: 17, of which 13 were waited for; matrix products, arithmetic and copies ran while one was open for 0% of the time, Pallas kernels for 1%

profile of v1, /device:TPU:1, one launch (start us, length us, event | category | flops | bytes accessed | tf_op | source)
XLA Modules:
  0.0 173.4 jit_solution(759894855864720791)
XLA Ops:
  0.7 0.6 copy-done.9
  1.3 0.0 copy-done.8
  1.4 1.2 copy-done.1
  2.6 1.0 copy-done.2
  3.6 1.0 copy-done.4
  4.6 9.8 %shard_map.154 = (f32[400,256]{1,0:T(8,128)S(1)}, f32[400,256]{1,0:T(8,128)S(1)}, f32[1024,128]{1,0:T(8,128)S(1)}, f32[1024,128]{1,0:T(8,128)S(1)}) custom-call(s32[2,1024]{1,0:T(2,128)S(1)} %bitcast.18, s32[2,1024]{1,0:T(2,128)S(1)} %bitcast.20, s32[2,1024]{1,0:T(2,128)S(1)} %bitcast.22, s32[8,128]{1,0:T(8,128)S(1)} %bitcast.24, s32[2]{0:T(128)S(1)} %bitcast.27, ...), custom_call_target="tpu_custom_call" | custom-call | flops 4000000000 | bytes 8000000 | tf_op jit(solution)/shard_map/pallas_call | solution.py:157
  14.4 3.3 %collective-permute-start.5 = (f32[1024,128]{1,0:T(8,128)S(1)}, f32[1024,128]{1,0:T(8,128)S(1)}, u32[]{:S(2)}, u32[]{:S(2)}) collective-permute-start(f32[1024,128]{1,0:T(8,128)S(1)} %get-tuple-element.29), channel_id=1, source_target_pairs={{0,2},{2,0},{4,6},{6,4},{8,10},{10,8},{12,14},{14,12},{16,18},{18,... | collective-permute-start | bytes 1572872 | tf_op jit(solution)/shard_map/ppermute | solution.py:213
  17.8 1.5 collective-permute-done.5
  19.3 0.1 add.24
  19.4 11.8 %all_to_all.20 = f32[8,128,128]{2,1,0:T(8,128)S(1)} all-to-all(f32[8,128,128]{2,1,0:T(8,128)S(1)} %bitcast.29), channel_id=1, replica_groups={{0,4,32,36,64,68,96,100},{12,8,44,40,76,72,108,104},{16,20,48,52,80,84,..., dimensions={0} | all-to-all | bytes 1048576 | tf_op jit(solution)/shard_map/all_to_all | solution.py:216
  31.3 2.0 %collective-permute-start.6 = (f32[128,128]{1,0:T(8,128)S(1)}, f32[128,128]{1,0:T(8,128)S(1)}, u32[]{:S(2)}, u32[]{:S(2)}) collective-permute-start(f32[128,128]{1,0:T(8,128)S(1)} %reduce_sum.18), channel_id=1, source_target_pairs={{0,192},{2,194},{4,196},{6,198},{8,200},{10,202},{12,204},{14,206}... | collective-permute-start | bytes 196616 | tf_op jit(solution)/shard_map/ppermute | solution.py:221
  33.2 2.4 %collective-permute-done.6 = f32[128,128]{1,0:T(8,128)S(1)} collective-permute-done((f32[128,128]{1,0:T(8,128)S(1)}, f32[128,128]{1,0:T(8,128)S(1)}, u32[]{:S(2)}, u32[]{:S(2)}) %collective-permute-start.6) | collective-permute-done | bytes 65568 | tf_op jit(solution)/shard_map/ppermute | solution.py:221
  35.7 4.7 %collective-permute-start.7 = (f32[128,128]{1,0:T(8,128)S(1)}, f32[128,128]{1,0:T(8,128)S(1)}, u32[]{:S(2)}, u32[]{:S(2)}) collective-permute-start(f32[128,128]{1,0:T(8,128)S(1)} %add.25), channel_id=1, source_target_pairs={{0,28},{2,30},{4,8},{6,10},{8,4},{10,6},{12,16},{14,18},{16,12},{1... | collective-permute-start | bytes 196616 | tf_op jit(solution)/shard_map/ppermute | solution.py:221
  40.4 1.7 collective-permute-done.7
  42.1 1.7 collective-permute-start.8
  43.8 4.0 %collective-permute-done.8 = f32[128,128]{1,0:T(8,128)S(1)} collective-permute-done((f32[128,128]{1,0:T(8,128)S(1)}, f32[128,128]{1,0:T(8,128)S(1)}, u32[]{:S(2)}, u32[]{:S(2)}) %collective-permute-start.8) | collective-permute-done | bytes 65568 | tf_op jit(solution)/shard_map/ppermute | solution.py:221
  47.9 9.8 %all_to_all.21 = f32[8,128,128]{2,1,0:T(8,128)S(1)} all-to-all(f32[8,128,128]{2,1,0:T(8,128)S(1)} %broadcast_in_dim.4), channel_id=1, replica_groups={{0,4,32,36,64,68,96,100},{12,8,44,40,76,72,108,104},{16,20,48,52,80,84,..., dimensions={0} | all-to-all | bytes 1048576 | tf_op jit(solution)/shard_map/all_to_all | solution.py:223
  57.7 6.1 %collective-permute-start.9 = (f32[1024,128]{1,0:T(8,128)S(1)}, f32[1024,128]{1,0:T(8,128)S(1)}, u32[]{:S(2)}, u32[]{:S(2)}) collective-permute-start(f32[1024,128]{1,0:T(8,128)S(1)} %bitcast.16), channel_id=1, source_target_pairs={{0,2},{2,0},{4,6},{6,4},{8,10},{10,8},{12,14},{14,12},{16,18},{18,... | collective-permute-start | bytes 1572872 | tf_op jit(solution)/shard_map/ppermute | solution.py:225
  63.8 0.2 collective-permute-start.1
  64.0 0.4 collective-permute-start
  64.5 2.5 %collective-permute-start.2 = (f32[400,256]{1,0:T(8,128)S(1)}, f32[400,256]{1,0:T(8,128)S(1)}, u32[]{:S(2)}, u32[]{:S(2)}) collective-permute-start(f32[400,256]{1,0:T(8,128)S(1)} %get-tuple-element.26.gl_a), channel_id=1, source_target_pairs={{0,1},{1,0},{2,3},{3,2},{4,5},{5,4},{6,7},{7,6},{8,9},{9,8},{10,11... | collective-permute-start | bytes 1228808 | tf_op jit(solution)/shard_map/ppermute | solution.py:229
  66.9 1.2 collective-permute-start.4
  68.1 0.3 collective-permute-start.3
  68.4 0.9 collective-permute-done.rhs
  69.4 18.9 %collective-permute-done.2.gl_b = f32[400,256]{1,0:T(8,128)S(1)} collective-permute-done((f32[400,256]{1,0:T(8,128)S(1)}, f32[400,256]{1,0:T(8,128)S(1)}, u32[]{:S(2)}, u32[]{:S(2)}) %collective-permute-start.2) | collective-permute-done | bytes 409632 | tf_op jit(solution)/shard_map/ppermute | solution.py:229
  88.3 4.6 %collective-permute-done.4.gc_b = f32[400,256]{1,0:T(8,128)S(1)} collective-permute-done((f32[400,256]{1,0:T(8,128)S(1)}, f32[400,256]{1,0:T(8,128)S(1)}, u32[]{:S(2)}, u32[]{:S(2)}) %collective-permute-start.4) | collective-permute-done | bytes 409632 | tf_op jit(solution)/shard_map/ppermute | solution.py:237
  92.8 0.8 copy-done.13
  93.7 11.0 %shard_map.155 = (f32[400,256]{1,0:T(8,128)S(1)}, f32[400,256]{1,0:T(8,128)S(1)}, f32[1024,128]{1,0:T(8,128)S(1)}, f32[1024,128]{1,0:T(8,128)S(1)}, f32[400,256]...) custom-call(s32[2,1024]{1,0:T(2,128)S(1)} %bitcast.19, ...), custom_call_target="tpu_custom_call" | custom-call | flops 4000000000 | bytes 8000000 | tf_op jit(solution)/shard_map/pallas_call | solution.py:157
  104.7 0.1 collective-permute-start.12
  104.8 1.9 %collective-permute-done.12 = f32[1024,128]{1,0:T(8,128)S(1)} collective-permute-done((f32[1024,128]{1,0:T(8,128)S(1)}, f32[1024,128]{1,0:T(8,128)S(1)}, u32[]{:S(2)}, u32[]{:S(2)}) %collective-permute-start.12) | collective-permute-done | bytes 524320 | tf_op jit(solution)/shard_map/ppermute | solution.py:213
  106.7 0.1 add.28
  106.8 11.9 %all_to_all.22 = f32[8,128,128]{2,1,0:T(8,128)S(1)} all-to-all(f32[8,128,128]{2,1,0:T(8,128)S(1)} %bitcast.30), channel_id=1, replica_groups={{0,4,32,36,64,68,96,100},{12,8,44,40,76,72,108,104},{16,20,48,52,80,84,..., dimensions={0} | all-to-all | bytes 1048576 | tf_op jit(solution)/shard_map/all_to_all | solution.py:216
  118.7 1.4 collective-permute-start.13
  120.1 3.0 %collective-permute-done.13 = f32[128,128]{1,0:T(8,128)S(1)} collective-permute-done((f32[128,128]{1,0:T(8,128)S(1)}, f32[128,128]{1,0:T(8,128)S(1)}, u32[]{:S(2)}, u32[]{:S(2)}) %collective-permute-start.13) | collective-permute-done | bytes 65568 | tf_op jit(solution)/shard_map/ppermute | solution.py:221
  123.1 0.1 collective-permute-start.14
  123.2 4.3 %collective-permute-done.14 = f32[128,128]{1,0:T(8,128)S(1)} collective-permute-done((f32[128,128]{1,0:T(8,128)S(1)}, f32[128,128]{1,0:T(8,128)S(1)}, u32[]{:S(2)}, u32[]{:S(2)}) %collective-permute-start.14) | collective-permute-done | bytes 65568 | tf_op jit(solution)/shard_map/ppermute | solution.py:221
  127.6 0.3 collective-permute-start.15
  127.9 5.6 %collective-permute-done.15 = f32[128,128]{1,0:T(8,128)S(1)} collective-permute-done((f32[128,128]{1,0:T(8,128)S(1)}, f32[128,128]{1,0:T(8,128)S(1)}, u32[]{:S(2)}, u32[]{:S(2)}) %collective-permute-start.15) | collective-permute-done | bytes 65568 | tf_op jit(solution)/shard_map/ppermute | solution.py:221
  133.5 9.6 %all_to_all.23 = f32[8,128,128]{2,1,0:T(8,128)S(1)} all-to-all(f32[8,128,128]{2,1,0:T(8,128)S(1)} %broadcast_in_dim.5), channel_id=1, replica_groups={{0,4,32,36,64,68,96,100},{12,8,44,40,76,72,108,104},{16,20,48,52,80,84,..., dimensions={0} | all-to-all | bytes 1048576 | tf_op jit(solution)/shard_map/all_to_all | solution.py:223
  143.2 5.4 %collective-permute-start.16 = (f32[1024,128]{1,0:T(8,128)S(1)}, f32[1024,128]{1,0:T(8,128)S(1)}, u32[]{:S(2)}, u32[]{:S(2)}) collective-permute-start(f32[1024,128]{1,0:T(8,128)S(1)} %bitcast.14), channel_id=1, source_target_pairs={{0,2},{2,0},{4,6},{6,4},{8,10},{10,8},{12,14},{14,12},{16,18},{18,... | collective-permute-start | bytes 1572872 | tf_op jit(solution)/shard_map/ppermute | solution.py:225
  148.6 2.0 %collective-permute-start.10 = (f32[400,256]{1,0:T(8,128)S(1)}, f32[400,256]{1,0:T(8,128)S(1)}, u32[]{:S(2)}, u32[]{:S(2)}) collective-permute-start(f32[400,256]{1,0:T(8,128)S(1)} %get-tuple-element.34.gl_a), channel_id=1, source_target_pairs={{0,1},{1,0},{2,3},{3,2},{4,5},{5,4},{6,7},{7,6},{8,9},{9,8},{10,11... | collective-permute-start | bytes 1228808 | tf_op jit(solution)/shard_map/ppermute | solution.py:229
  150.6 1.0 collective-permute-start.11
  151.6 9.6 %collective-permute-done.10.gl_b = f32[400,256]{1,0:T(8,128)S(1)} collective-permute-done((f32[400,256]{1,0:T(8,128)S(1)}, f32[400,256]{1,0:T(8,128)S(1)}, u32[]{:S(2)}, u32[]{:S(2)}) %collective-permute-start.10) | collective-permute-done | bytes 409632 | tf_op jit(solution)/shard_map/ppermute | solution.py:229
  161.2 8.8 %collective-permute-done.11.gc_b = f32[400,256]{1,0:T(8,128)S(1)} collective-permute-done((f32[400,256]{1,0:T(8,128)S(1)}, f32[400,256]{1,0:T(8,128)S(1)}, u32[]{:S(2)}, u32[]{:S(2)}) %collective-permute-start.11) | collective-permute-done | bytes 409632 | tf_op jit(solution)/shard_map/ppermute | solution.py:229
  170.0 1.1 shard_map.156
  171.0 0.5 copy-done
  171.5 1.3 shard_map.157
  172.8 0.6 reduce
  (38 shorter events, 0.3 us)
Async XLA Ops:
  0.6 0.7 copy-start.9
  0.6 0.7 copy-start.8
  0.7 0.7 copy-start.7
  0.7 0.7 copy-start.6
  0.7 0.7 copy-start.11
  1.4 1.2 copy-start.1
  2.6 1.0 copy-start.2
  3.6 1.0 copy-start.4
  14.4 4.9 %collective-permute-start.5 = (f32[1024,128]{1,0:T(8,128)S(1)}, f32[1024,128]{1,0:T(8,128)S(1)}, u32[]{:S(2)}, u32[]{:S(2)}) collective-permute-start(f32[1024,128]{1,0:T(8,128)S(1)} %get-tuple-element.29), channel_id=1, source_target_pairs={{0,2},{2,0},{4,6},{6,4},{8,10},{10,8},{12,14},{14,12},{16,18},{18,... | collective-permute-start | bytes 1572872 | tf_op jit(solution)/shard_map/ppermute | solution.py:213
  31.3 4.4 %collective-permute-start.6 = (f32[128,128]{1,0:T(8,128)S(1)}, f32[128,128]{1,0:T(8,128)S(1)}, u32[]{:S(2)}, u32[]{:S(2)}) collective-permute-start(f32[128,128]{1,0:T(8,128)S(1)} %reduce_sum.18), channel_id=1, source_target_pairs={{0,192},{2,194},{4,196},{6,198},{8,200},{10,202},{12,204},{14,206}... | collective-permute-start | bytes 196616 | tf_op jit(solution)/shard_map/ppermute | solution.py:221
  35.7 6.4 %collective-permute-start.7 = (f32[128,128]{1,0:T(8,128)S(1)}, f32[128,128]{1,0:T(8,128)S(1)}, u32[]{:S(2)}, u32[]{:S(2)}) collective-permute-start(f32[128,128]{1,0:T(8,128)S(1)} %add.25), channel_id=1, source_target_pairs={{0,28},{2,30},{4,8},{6,10},{8,4},{10,6},{12,16},{14,18},{16,12},{1... | collective-permute-start | bytes 196616 | tf_op jit(solution)/shard_map/ppermute | solution.py:221
  42.1 5.7 %collective-permute-start.8 = (f32[128,128]{1,0:T(8,128)S(1)}, f32[128,128]{1,0:T(8,128)S(1)}, u32[]{:S(2)}, u32[]{:S(2)}) collective-permute-start(f32[128,128]{1,0:T(8,128)S(1)} %add.26), channel_id=1, source_target_pairs={{0,12},{2,14},{4,24},{6,26},{8,20},{10,22},{12,0},{14,2},{16,28},{... | collective-permute-start | bytes 196616 | tf_op jit(solution)/shard_map/ppermute | solution.py:221
  47.9 15.9 %copy-start.14 = (f32[256]{0:T(256)S(1)}, f32[256]{0:T(256)}, u32[]{:S(2)}) copy-start(f32[256]{0:T(256)} %param.15) | copy-start | bytes 3076
  47.9 16.2 %copy-start.3 = (f32[400,256]{1,0:T(8,128)S(1)}, f32[400,256]{1,0:T(8,128)}, u32[]{:S(2)}) copy-start(f32[400,256]{1,0:T(8,128)} %rhs.2) | copy-start | bytes 1228804
  47.9 45.8 %copy-start.5 = (f32[400,256]{1,0:T(8,128)S(1)}, f32[400,256]{1,0:T(8,128)}, u32[]{:S(2)}) copy-start(f32[400,256]{1,0:T(8,128)} %lhs.4) | copy-start | bytes 1228804
  57.7 10.8 %copy-start.12 = (f32[640]{0:T(1024)S(1)}, f32[640]{0:T(1024)}, u32[]{:S(2)}) copy-start(f32[640]{0:T(1024)} %param.16) | copy-start | bytes 7684
  57.7 35.2 %collective-permute-start.9 = (f32[1024,128]{1,0:T(8,128)S(1)}, f32[1024,128]{1,0:T(8,128)S(1)}, u32[]{:S(2)}, u32[]{:S(2)}) collective-permute-start(f32[1024,128]{1,0:T(8,128)S(1)} %bitcast.16), channel_id=1, source_target_pairs={{0,2},{2,0},{4,6},{6,4},{8,10},{10,8},{12,14},{14,12},{16,18},{18,... | collective-permute-start | bytes 1572872 | tf_op jit(solution)/shard_map/ppermute | solution.py:225
  63.8 4.3 %collective-permute-start.1 = (f32[1,256]{1,0:T(1,128)S(1)}, f32[1,256]{1,0:T(1,128)S(1)}, u32[]{:S(2)}, u32[]{:S(2)}) collective-permute-start(f32[1,256]{1,0:T(1,128)S(1)} %bitcast.31), channel_id=1, source_target_pairs={{0,2},{1,3},{2,4},{3,5},{4,6},{5,7},{6,8},{7,9},{8,10},{9,11},{10,... | collective-permute-start | bytes 3080 | tf_op jit(solution)/shard_map/ppermute | solution.py:237
  64.0 5.3 %collective-permute-start = (f32[400,256]{1,0:T(8,128)S(1)}, f32[400,256]{1,0:T(8,128)S(1)}, u32[]{:S(2)}, u32[]{:S(2)}) collective-permute-start(f32[400,256]{1,0:T(8,128)S(1)} %copy-done.3), channel_id=1, source_target_pairs={{0,2},{1,3},{2,4},{3,5},{4,6},{5,7},{6,8},{7,9},{8,10},{9,11},{10,... | collective-permute-start | bytes 1228808 | tf_op jit(solution)/shard_map/ppermute | solution.py:237
  64.5 23.8 %collective-permute-start.2 = (f32[400,256]{1,0:T(8,128)S(1)}, f32[400,256]{1,0:T(8,128)S(1)}, u32[]{:S(2)}, u32[]{:S(2)}) collective-permute-start(f32[400,256]{1,0:T(8,128)S(1)} %get-tuple-element.26.gl_a), channel_id=1, source_target_pairs={{0,1},{1,0},{2,3},{3,2},{4,5},{5,4},{6,7},{7,6},{8,9},{9,8},{10,11... | collective-permute-start | bytes 1228808 | tf_op jit(solution)/shard_map/ppermute | solution.py:229
  66.9 25.9 %collective-permute-start.4 = (f32[400,256]{1,0:T(8,128)S(1)}, f32[400,256]{1,0:T(8,128)S(1)}, u32[]{:S(2)}, u32[]{:S(2)}) collective-permute-start(f32[400,256]{1,0:T(8,128)S(1)} %get-tuple-element.27), channel_id=1, source_target_pairs={{0,3},{1,2},{2,5},{3,4},{4,7},{5,6},{6,9},{7,8},{8,11},{9,10},{10,... | collective-permute-start | bytes 1228808 | tf_op jit(solution)/shard_map/ppermute | solution.py:237
  68.1 24.7 %collective-permute-start.3 = (f32[400,256]{1,0:T(8,128)S(1)}, f32[400,256]{1,0:T(8,128)S(1)}, u32[]{:S(2)}, u32[]{:S(2)}) collective-permute-start(f32[400,256]{1,0:T(8,128)S(1)} %get-tuple-element.27), channel_id=1, source_target_pairs={{0,2},{1,3},{2,4},{3,5},{4,6},{5,7},{6,8},{7,9},{8,10},{9,11},{10,... | collective-permute-start | bytes 1228808 | tf_op jit(solution)/shard_map/ppermute | solution.py:237
  68.4 25.2 %copy-start.10 = (f32[256]{0:T(256)S(1)}, f32[256]{0:T(256)}, u32[]{:S(2)}) copy-start(f32[256]{0:T(256)} %param.14) | copy-start | bytes 3076
  92.8 0.8 copy-start.13
  104.7 2.0 %collective-permute-start.12 = (f32[1024,128]{1,0:T(8,128)S(1)}, f32[1024,128]{1,0:T(8,128)S(1)}, u32[]{:S(2)}, u32[]{:S(2)}) collective-permute-start(f32[1024,128]{1,0:T(8,128)S(1)} %get-tuple-element.43), channel_id=1, source_target_pairs={{0,2},{2,0},{4,6},{6,4},{8,10},{10,8},{12,14},{14,12},{16,18},{18,... | collective-permute-start | bytes 1572872 | tf_op jit(solution)/shard_map/ppermute | solution.py:213
  118.7 4.4 %collective-permute-start.13 = (f32[128,128]{1,0:T(8,128)S(1)}, f32[128,128]{1,0:T(8,128)S(1)}, u32[]{:S(2)}, u32[]{:S(2)}) collective-permute-start(f32[128,128]{1,0:T(8,128)S(1)} %reduce_sum.19), channel_id=1, source_target_pairs={{0,192},{2,194},{4,196},{6,198},{8,200},{10,202},{12,204},{14,206}... | collective-permute-start | bytes 196616 | tf_op jit(solution)/shard_map/ppermute | solution.py:221
  123.1 4.4 %collective-permute-start.14 = (f32[128,128]{1,0:T(8,128)S(1)}, f32[128,128]{1,0:T(8,128)S(1)}, u32[]{:S(2)}, u32[]{:S(2)}) collective-permute-start(f32[128,128]{1,0:T(8,128)S(1)} %add.29), channel_id=1, source_target_pairs={{0,28},{2,30},{4,8},{6,10},{8,4},{10,6},{12,16},{14,18},{16,12},{1... | collective-permute-start | bytes 196616 | tf_op jit(solution)/shard_map/ppermute | solution.py:221
  127.6 5.9 %collective-permute-start.15 = (f32[128,128]{1,0:T(8,128)S(1)}, f32[128,128]{1,0:T(8,128)S(1)}, u32[]{:S(2)}, u32[]{:S(2)}) collective-permute-start(f32[128,128]{1,0:T(8,128)S(1)} %add.30), channel_id=1, source_target_pairs={{0,12},{2,14},{4,24},{6,26},{8,20},{10,22},{12,0},{14,2},{16,28},{... | collective-permute-start | bytes 196616 | tf_op jit(solution)/shard_map/ppermute | solution.py:221
  143.2 27.9 %collective-permute-start.16 = (f32[1024,128]{1,0:T(8,128)S(1)}, f32[1024,128]{1,0:T(8,128)S(1)}, u32[]{:S(2)}, u32[]{:S(2)}) collective-permute-start(f32[1024,128]{1,0:T(8,128)S(1)} %bitcast.14), channel_id=1, source_target_pairs={{0,2},{2,0},{4,6},{6,4},{8,10},{10,8},{12,14},{14,12},{16,18},{18,... | collective-permute-start | bytes 1572872 | tf_op jit(solution)/shard_map/ppermute | solution.py:225
  148.6 12.6 %collective-permute-start.10 = (f32[400,256]{1,0:T(8,128)S(1)}, f32[400,256]{1,0:T(8,128)S(1)}, u32[]{:S(2)}, u32[]{:S(2)}) collective-permute-start(f32[400,256]{1,0:T(8,128)S(1)} %get-tuple-element.34.gl_a), channel_id=1, source_target_pairs={{0,1},{1,0},{2,3},{3,2},{4,5},{5,4},{6,7},{7,6},{8,9},{9,8},{10,11... | collective-permute-start | bytes 1228808 | tf_op jit(solution)/shard_map/ppermute | solution.py:229
  150.6 19.4 %collective-permute-start.11 = (f32[400,256]{1,0:T(8,128)S(1)}, f32[400,256]{1,0:T(8,128)S(1)}, u32[]{:S(2)}, u32[]{:S(2)}) collective-permute-start(f32[400,256]{1,0:T(8,128)S(1)} %get-tuple-element.35.gc_a), channel_id=1, source_target_pairs={{0,1},{1,0},{2,3},{3,2},{4,5},{5,4},{6,7},{7,6},{8,9},{9,8},{10,11... | collective-permute-start | bytes 1228808 | tf_op jit(solution)/shard_map/ppermute | solution.py:229
  170.0 1.5 copy-start

commit v2 on v1

v2 whole, which is shorter than its diff:
```python
import functools

import jax
import jax.numpy as jnp
from jax import lax
from jax.experimental import pallas as pl
from jax.experimental.pallas import tpu as pltpu
from jax.sharding import PartitionSpec as P

STEP_SIZE = 0.2
F32 = jnp.float32
BF16 = jnp.bfloat16
LANES = 128


def split(x):
    hi = x.astype(BF16)
    return hi, (x - hi.astype(F32)).astype(BF16)


def nn(a, b):
    return jnp.dot(a, b, preferred_element_type=F32)


def nt(a, b):
    return lax.dot_general(a, b, (((1,), (1,)), ((), ())), preferred_element_type=F32)


def one_hot(row, count):
    ids = lax.broadcasted_iota(jnp.int32, (count, row.shape[1]), 0)
    return jnp.where(ids == row, 1.0, 0.0).astype(BF16)


def adagrad(table, acc, grad):
    grown = acc + jnp.sum(grad * grad, axis=0, keepdims=True) * (1.0 / grad.shape[0])
    return table - STEP_SIZE * grad * lax.rsqrt(grown), grown


def bucket(t, spans, idx, ends, tables, outs, work):
    (lidx, ridx, widx, nidx) = idx
    (lhs, rhs, rel) = tables
    (glhs, gctx, grel) = outs
    (left, right, wts, hot_w, qh, ql, qht, qlt, sh, sl, uh, ul, vh, vl, ph, pw, nh, nl) = work
    d, rows = lhs.shape
    rels = rel.shape[1]
    edges = lidx.shape[1]
    neg = nidx.shape[1]
    width = edges // spans
    ats = [pl.ds(c * width, width) for c in range(spans)]
    nats = [pl.ds(c * neg, neg) for c in range(spans)]

    def hot_neg(c):
        return one_hot(nidx[pl.ds(t * spans + c, 1), :], rows)

    rh, rl = split(rhs[...])
    for c in range(spans):
        hot_n = hot_neg(c)
        q = nn(rh, hot_n)
        qh[:, nats[c]] = q.astype(BF16)
        qht[nats[c], :] = q.T.astype(BF16)
        q = nn(rl, hot_n)
        ql[:, nats[c]] = q.astype(BF16)
        qlt[nats[c], :] = q.T.astype(BF16)
    for c in range(spans):
        hot = one_hot(ridx[pl.ds(t, 1), ats[c]], rows)
        right[:, ats[c]] = nn(rh, hot) + nn(rl, hot)
    rh, rl = split(lhs[...])
    for c in range(spans):
        hot = one_hot(lidx[pl.ds(t, 1), ats[c]], rows)
        left[:, ats[c]] = nn(rh, hot) + nn(rl, hot)
    rh, rl = split(rel[...])
    pcoefs, lives = [], []
    for c in range(spans):
        hot = one_hot(widx[pl.ds(t, 1), ats[c]], rels)
        hot_w[:, ats[c]] = hot
        weights = nn(rh, hot) + nn(rl, hot)
        wts[:, ats[c]] = weights
        scaled = left[:, ats[c]] * weights
        high, low = split(scaled)
        sh[:, ats[c]] = high
        sl[:, ats[c]] = low
        slot = lax.broadcasted_iota(jnp.int32, (1, width), 1) + c * width
        live = jnp.where(slot < ends[t], 1.0, 0.0)
        positive = jnp.sum(scaled * right[:, ats[c]], axis=0, keepdims=True)
        pcoef = -jax.nn.sigmoid(-positive) * live
        ph[:, ats[c]], pw[:, ats[c]] = split(pcoef * scaled)
        pcoefs.append(pcoef)
        lives.append(live)
    coefs = []
    for c in range(spans):
        scores = nn(qht[nats[c], :], sh[:, ats[c]]) + (
            nn(qht[nats[c], :], sl[:, ats[c]]) + nn(qlt[nats[c], :], sh[:, ats[c]])
        )
        coefs.append(split(jax.nn.sigmoid(scores) * (lives[c] / neg)))
    for c in range(spans):
        ch, cl = coefs[c]
        mixture = nn(qh[:, nats[c]], ch) + (nn(qh[:, nats[c]], cl) + nn(ql[:, nats[c]], ch))
        toward = pcoefs[c] * right[:, ats[c]] + mixture
        uh[:, ats[c]], ul[:, ats[c]] = split(left[:, ats[c]] * toward)
        vh[:, ats[c]], vl[:, ats[c]] = split(wts[:, ats[c]] * toward)
    for c in range(spans):
        ch, cl = coefs[c]
        ngrad = nt(sh[:, ats[c]], ch) + (nt(sh[:, ats[c]], cl) + nt(sl[:, ats[c]], ch))
        nh[:, nats[c]], nl[:, nats[c]] = split(ngrad)
    total = nt(uh[...], hot_w[...]) + nt(ul[...], hot_w[...])
    for b in range(rels // LANES):
        grel[pl.ds(b * d, d), :] = total[:, b * LANES:(b + 1) * LANES]
    hot = one_hot(lidx[pl.ds(t, 1), :], rows)
    glhs[...] = nt(vh[...], hot) + nt(vl[...], hot)
    hot = one_hot(ridx[pl.ds(t, 1), :], rows)
    total = nt(ph[...], hot) + nt(pw[...], hot)
    hot = jnp.concatenate([hot_neg(c) for c in range(spans)], axis=1)
    gctx[...] = total + (nt(nh[...], hot) + nt(nl[...], hot))


def work_shapes(d, edges, negs, rels):
    f32 = [pltpu.VMEM((d, edges), F32)] * 3
    bf = lambda *shape: pltpu.VMEM(shape, BF16)
    return f32 + [bf(rels, edges)] + [bf(d, negs)] * 2 + [bf(negs, d)] * 2 + [bf(d, edges)] * 8 + [
        bf(d, negs)
    ] * 2


def halves(core, grel_ref, keep_ref, send_ref, used):
    half = keep_ref.shape[0]
    grel_ref[pl.ds(used, grel_ref.shape[0] - used), :] = jnp.zeros(
        (grel_ref.shape[0] - used, LANES), F32
    )
    keep_ref[...] = grel_ref[pl.ds(pl.multiple_of(core * half, half), half), :]
    send_ref[...] = grel_ref[pl.ds(pl.multiple_of((1 - core) * half, half), half), :]


def first_kernel(spans, core, lidx_hbm, ridx_hbm, nidx_hbm, widx_hbm, ends_hbm, rhs_hbm, lhs_hbm,
                 rel_hbm, glhs, gctx, keep, send, grel,
                 lidx, ridx, nidx, widx, ends, rhs, lhs, rel, sems, *work):
    sources = (lidx_hbm, ridx_hbm, nidx_hbm, widx_hbm, ends_hbm, rhs_hbm, lhs_hbm, rel_hbm)
    targets = (lidx, ridx, nidx, widx, ends, rhs, lhs, rel)
    copies = [
        pltpu.make_async_copy(source, target, sems.at[i])
        for i, (source, target) in enumerate(zip(sources, targets))
    ]
    for copy in copies:
        copy.start()
    for copy in copies:
        copy.wait()
    bucket(0, spans, (lidx, ridx, widx, nidx), ends, (lhs, rhs, rel), (glhs, gctx, grel), work)
    halves(core[0], grel, keep, send, rel.shape[0] * (rel.shape[1] // LANES))


def join(core, mine, other, grel):
    half = mine.shape[0]
    grel[pl.ds(pl.multiple_of(core * half, half), half), :] = mine[...]
    grel[pl.ds(pl.multiple_of((1 - core) * half, half), half), :] = other[...]


def update_rel(rel, racc, grel, rel_new, racc_new):
    d = rel.shape[0]
    for b in range(rel.shape[1] // LANES):
        at = pl.ds(b * LANES, LANES)
        g = grel[pl.ds(b * d, d), :]
        rel_new[:, at], racc_new[:, at] = adagrad(rel[:, at], racc[:, at], g)


def update_pair(table, acc, one, two, table_new, acc_new):
    table_new[...], acc_new[...] = adagrad(table[...], acc[...], one[...] + two[...])


def second_kernel(spans, lidx, ridx, widx, nidx, ends, core, lhs, rhs, rel, wacc,
                  gw_mine, gw_other, glhs, gctx, keep, send, rel_out, wacc_new,
                  grel, rel_new, sem, *work):
    join(core[0], gw_mine, gw_other, grel)
    update_rel(rel, wacc, grel, rel_new, wacc_new)
    copy = pltpu.make_async_copy(rel_new, rel_out, sem)
    copy.start()
    bucket(1, spans, (lidx, ridx, widx, nidx), ends, (lhs, rhs, rel_new), (glhs, gctx, grel), work)
    halves(core[0], grel, keep, send, rel.shape[0] * (rel.shape[1] // LANES))
    copy.wait()


def pair_kernel(lhs, rhs, lacc, racc, gl_a, gl_b, gc_a, gc_b, lhs_new, rhs_new, lacc_new, racc_new):
    update_pair(lhs, lacc, gl_a, gl_b, lhs_new, lacc_new)
    update_pair(rhs, racc, gc_a, gc_b, rhs_new, racc_new)


def rel_kernel(core, rel, wacc, gw_mine, gw_other, rel_new, wacc_new, grel):
    join(core[0], gw_mine, gw_other, grel)
    update_rel(rel, wacc, grel, rel_new, wacc_new)


def add_kernel(one, two, out):
    out[...] = one[...] + two[...]


def spread_kernel(one, two, *rest):
    out = rest[-1]
    out[...] = jnp.broadcast_to((one[...] + two[...])[None], out.shape)


def follow(value, others):
    return pl.pallas_call(
        lambda *refs: None,
        out_shape=jax.ShapeDtypeStruct(value.shape, value.dtype),
        in_specs=[AN] * (1 + len(others)),
        out_specs=AN,
        input_output_aliases={0: 0},
        compiler_params=pltpu.CompilerParams(vmem_limit_bytes=1 << 20),
    )(value, *others)


VM = pl.BlockSpec(memory_space=pltpu.VMEM)
SM = pl.BlockSpec(memory_space=pltpu.SMEM)
HB = pl.BlockSpec(memory_space=pltpu.HBM)
AN = pl.BlockSpec(memory_space=pl.ANY)


def call(kernel, ins, specs, outs, scratch, flops, mib=4, out_specs={}):
    return pl.pallas_call(
        kernel,
        out_shape=[jax.ShapeDtypeStruct(o, F32) if isinstance(o, tuple) else o for o in outs],
        in_specs=[specs.get(i, VM) for i in range(len(ins))],
        out_specs=[out_specs.get(i, VM) for i in range(len(outs))],
        scratch_shapes=[pltpu.VMEM(s, F32) if isinstance(s, tuple) else s for s in scratch],
        compiler_params=pltpu.CompilerParams(vmem_limit_bytes=mib << 20),
        cost_estimate=pl.CostEstimate(
            flops=flops, bytes_accessed=8_000_000, transcendentals=0
        ),
    )(*ins)


def place(y, x, z, core):
    return y * 32 + x * 16 + z * 2 + core


def near_groups():
    groups = []
    for core in range(2):
        for zh in range(4):
            members = [None] * 16
            for y in range(4):
                for x in range(2):
                    for zl in range(2):
                        z = zh * 2 + zl
                        members[(y * 2 + x) * 2 + ((z ^ (z >> 1)) & 1)] = place(y, x, z, core)
            groups.append(members)
    return groups


def pairs(move):
    out = []
    for y in range(4):
        for x in range(2):
            for z in range(8):
                for core in range(2):
                    a = place(y, x, z, core)
                    out.append((a, place(*move(y, x, z, core))))
    return out


CORE_PAIRS = pairs(lambda y, x, z, c: (y, x, z, 1 - c))
FAR_PAIRS = (
    pairs(lambda y, x, z, c: (y, x, (z + (1 if z % 2 else 7)) % 8, c)),
    pairs(lambda y, x, z, c: (y, x, z ^ (3 if z in (0, 3, 4, 7) else 7), c)),
)


def sum_over_blk(keep, send, exchange, after, wait_for):
    got = lax.ppermute(send, "blk", CORE_PAIRS)
    half = keep.shape
    (part,) = call(add_kernel, (keep, got), {}, [half], [], 1_000_000)
    beside = exchange()
    groups = near_groups()
    n = len(groups[0])
    rows = half[0] // n
    got = lax.all_to_all(
        part.reshape(n, rows, LANES), "blk", 0, 0, axis_index_groups=groups
    )
    total = jnp.sum(got, axis=0)
    total = total + lax.ppermute(total, "blk", FAR_PAIRS[0])
    got = lax.ppermute(total, "blk", FAR_PAIRS[1])
    ended = tuple(beside[1:])
    (spread,) = call(
        spread_kernel, (total, got) + ended, {2 + i: AN for i in range(len(ended))},
        [(n, rows, LANES)], [], 1_000_000,
    )
    mine = lax.all_to_all(spread, "blk", 0, 0, axis_index_groups=groups)
    beside = after(beside)
    mine = mine.reshape(n * rows, LANES)
    if wait_for:
        mine = follow(mine, tuple(beside[:1]))
    return mine, lax.ppermute(mine, "blk", CORE_PAIRS), beside


def swap(x):
    return lax.ppermute(x, "rel", [(0, 1), (1, 0)])


def onward(x, flip):
    n = lax.axis_size("blk")
    moves = [
        (2 * b + k, 2 * ((b + 1) % n) + (1 - k if flip else k)) for b in range(n) for k in range(2)
    ]
    return lax.ppermute(x, ("blk", "rel"), moves)


def per_device(lhs, rhs, rel, lacc, racc, wacc, lidx, ridx, widx, ends, nidx):
    d, rows = lhs.shape
    rels = rel.shape[1]
    rounds, edges = lidx.shape[2:]
    spans, neg = nidx.shape[3:]
    lidx, ridx, widx = (a.reshape(rounds, edges) for a in (lidx, ridx, widx))
    nidx = nidx.reshape(rounds * spans, neg)
    ends = ends.reshape(rounds)
    lacc, racc, wacc = (a.reshape(1, -1) for a in (lacc, racc, wacc))
    core = lax.rem(lax.axis_index("blk"), 2).astype(jnp.int32).reshape(1)
    used = d * (rels // LANES)
    full = -(-used // 2048) * 2048
    slab, table, state = (d, rows), (d, rels), (1, rows)
    half = (full // 2, LANES)
    work = work_shapes(d, edges, spans * neg, rels)
    sources = tuple(
        pltpu.with_memory_space_constraint(a, pltpu.HBM)
        for a in (lidx, ridx, nidx, widx, ends, rhs, lhs, rel)
    )
    glhs, gctx, keep, send = call(
        functools.partial(first_kernel, spans), (core,) + sources,
        {0: SM} | {1 + i: HB for i in range(8)},
        [slab, slab, half, half],
        [(full, LANES)]
        + [pltpu.VMEM(a.shape, a.dtype) for a in (lidx, ridx, nidx, widx)]
        + [pltpu.SMEM(ends.shape, ends.dtype), slab, slab, table, pltpu.SemaphoreType.DMA((8,))]
        + work,
        4_000_000_000, 40,
    )

    def exchange_first():
        return (glhs, swap(glhs), onward(gctx, False), onward(gctx, True),
                onward(rhs, False), onward(racc, False))

    def update_first(arrived):
        gl_a, gl_b, gc_a, gc_b, rhs_in, racc_in = arrived
        return call(
            pair_kernel, (lhs, rhs_in, lacc, racc_in, gl_a, gl_b, gc_a, gc_b), {},
            [slab, slab, state, state], [], 1_000_000, 2,
        )

    gw_mine, gw_other, (lhs1, rhs1, lacc1, racc1) = sum_over_blk(
        keep, send, exchange_first, update_first, True
    )
    glhs1, gctx1, keep, send, rel, wacc = call(
        functools.partial(second_kernel, spans),
        (lidx, ridx, widx, nidx, ends, core, lhs1, rhs1, rel, wacc, gw_mine, gw_other),
        {4: SM, 5: SM},
        [slab, slab, half, half, pltpu.HBM(table, F32), (1, rels)],
        [(full, LANES), table, pltpu.SemaphoreType.DMA] + work, 4_000_000_000, 40, {4: HB},
    )

    def exchange_last():
        return glhs1, swap(glhs1), gctx1, swap(gctx1)

    def update_last(arrived):
        return call(
            pair_kernel, (lhs1, rhs1, lacc1, racc1) + tuple(arrived), {},
            [slab, slab, state, state], [], 1_000_000, 2,
        )

    gw_mine, gw_other, (lhs, rhs, lacc, racc) = sum_over_blk(
        keep, send, exchange_last, update_last, False
    )
    rel, wacc = call(
        rel_kernel, (core, rel, wacc, gw_mine, gw_other), {0: SM}, [table, (1, rels)],
        [(full, LANES)], 1_000_000, 4,
    )
    return lhs, lacc.reshape(-1), rhs, racc.reshape(-1), rel, wacc.reshape(-1)


def solution(mesh):
    in_specs = (
        P(None, "blk"),
        P(None, "blk"),
        P(None, "rel"),
        P("blk"),
        P("blk"),
        P("rel"),
        P("blk", "rel", None, None),
        P("blk", "rel", None, None),
        P("blk", "rel", None, None),
        P("blk", "rel", None),
        P("blk", "rel", None, None, None),
    )
    out_specs = (P(None, "blk"), P("blk"), P(None, "blk"), P("blk"), P(None, "rel"), P("rel"))
    return jax.shard_map(
        per_device, mesh=mesh, in_specs=in_specs, out_specs=out_specs, check_vma=False
    )
```

time: 174 us -> 133 us (0.76)
  blocking collectives: 43.1 us -> 12.8 us
  waiting for transfers between devices: 67.2 us -> 53 us
  starting transfers between devices: 32.9 us -> 40.7 us
  local copies, waits for them, and re-layouts: 5.29 us -> 1.72 us
    all_to_all x2 -> x0, blocking collectives: 23.7 us -> none  [sum_over_blk(): lax.all_to_all(part.reshape(8, rows, LANES), 'blk', 0, 0, axis_index_grou...]
    ppermute x3, waiting for transfers between devices: 37.3 us -> 17 us  [swap(): return lax.ppermute(x, 'rel', [(0, 1), (1, 0)])]
    all_to_all x0 -> x3, starting transfers between devices: none -> 14.2 us  [the longest x2 8.99 us: sum_over_blk(): lax.all_to_all(part.reshape(n, rows, LANES), 'blk', 0, 0, axis_index_grou...]
    all_to_all x0 -> x3, waiting for transfers between devices: none -> 12.1 us  [the longest x1 6.3 us: sum_over_blk(): mine = lax.all_to_all(spread, 'blk', 0, 0, axis_index_groups=groups)]
    ppermute x10 -> x8, starting transfers between devices: 25.3 us -> 16 us  [the longest x2 5.88 us: sum_over_blk(): return (mine, lax.ppermute(mine, 'blk', CORE_PAIRS), beside)]
    all_to_all x2 -> x1, blocking collectives: 19.4 us -> 12.8 us  [sum_over_blk(): mine = lax.all_to_all(spread, 'blk', 0, 0, axis_index_groups=groups)]
    ppermute x10 -> x8, waiting for transfers between devices: 24.4 us -> 17.9 us  [the longest x2 12.8 us: sum_over_blk(): total = total + lax.ppermute(total, 'blk', FAR_PAIRS[0])]
    unnamed x30 -> x26, local copies, waits for them, and re-layouts: 5.22 us -> 1.72 us
  transfers between devices with their start and end apart: 17 -> 18, of which waited for: 13 -> 14; matrix products, arithmetic and copies ran while one was open for 0% -> 0% of each run, Pallas kernels for 1% -> 1%
where the time goes in v2:
time: 133 us; the launch traced here: 132 us
  waiting for transfers between devices  53 us (40%)
  starting transfers between devices  40.7 us (31%)
  Pallas kernels  22.4 us (17%)
  blocking collectives  12.8 us (10%)
  local copies, waits for them, and re-layouts  1.72 us (1%)
    pallas_call x9, Pallas kernels, call(): pl.pallas_call(kernel, out_shape=[jax.ShapeDtypeStruct(o, F32) if isinsta...  22.4 us
    ppermute x3, waiting for transfers between devices, swap(): return lax.ppermute(x, 'rel', [(0, 1), (1, 0)])  17 us
    ppermute x2, waiting for transfers between devices, sum_over_blk(): total = total + lax.ppermute(total, 'blk', FAR_PAIRS[0])  12.8 us
    all_to_all x1, blocking collectives, sum_over_blk(): mine = lax.all_to_all(spread, 'blk', 0, 0, axis_index_groups=groups)  12.8 us
    all_to_all x2, starting transfers between devices, sum_over_blk(): lax.all_to_all(part.reshape(n, rows, LANES), 'blk', 0, 0, axis_index_grou...  8.99 us
    all_to_all x1, waiting for transfers between devices, sum_over_blk(): mine = lax.all_to_all(spread, 'blk', 0, 0, axis_index_groups=groups)  6.3 us
    ppermute x4, waiting for transfers between devices, onward(): return lax.ppermute(x, ('blk', 'rel'), moves)  6.03 us
    ppermute x2, starting transfers between devices, sum_over_blk(): return (mine, lax.ppermute(mine, 'blk', CORE_PAIRS), beside)  5.88 us
  transfers between devices with their start and end apart: 18, of which 14 were waited for; matrix products, arithmetic and copies ran while one was open for 0% of the time, Pallas kernels for 1%

profile of v2, /device:TPU:1, one launch (start us, length us, event | category | flops | bytes accessed | tf_op | source)
XLA Modules:
  0.0 132.1 jit_solution(9965709405887930420)
XLA Ops:
  0.6 9.1 %shard_map.154 = (f32[400,256]{1,0:T(8,128)S(1)}, f32[400,256]{1,0:T(8,128)S(1)}, f32[1024,128]{1,0:T(8,128)S(1)}, f32[1024,128]{1,0:T(8,128)S(1)}) custom-call(s32[1]{0:T(128)} %bitcast.2.core, s32[2,1024]{1,0:T(2,128)} %bitcast.18, s32[2,1024]{1,0:T(2,128)} %bitcast.20, s32[8,128]{1,0:T(8,128)} %bitcast.24, s32[2,1024]{1,0:T(2,128)} %bitcast.22, ...), custom_call_target="tpu_custom_call" | custom-call | flops 4000000000 | bytes 8000000 | tf_op jit(solution)/shard_map/pallas_call | solution.py:217
  9.7 0.0 copy-start.2
  9.7 3.3 %collective-permute-start.5 = (f32[1024,128]{1,0:T(8,128)S(1)}, f32[1024,128]{1,0:T(8,128)S(1)}, u32[]{:S(2)}, u32[]{:S(2)}) collective-permute-start(f32[1024,128]{1,0:T(8,128)S(1)} %get-tuple-element.33), channel_id=1, source_target_pairs={{0,2},{2,0},{4,6},{6,4},{8,10},{10,8},{12,14},{14,12},{16,18},{18,... | collective-permute-start | bytes 1572872 | tf_op jit(solution)/shard_map/ppermute | solution.py:267
  13.1 1.5 %collective-permute-done.5.two = f32[1024,128]{1,0:T(8,128)S(1)} collective-permute-done((f32[1024,128]{1,0:T(8,128)S(1)}, f32[1024,128]{1,0:T(8,128)S(1)}, u32[]{:S(2)}, u32[]{:S(2)}) %collective-permute-start.5) | collective-permute-done | bytes 524320 | tf_op jit(solution)/shard_map/ppermute | solution.py:267
  14.6 0.8 shard_map.156
  15.5 4.8 %all-to-all-start = ((f32[16,64,128]{2,1,0:T(8,128)}), f32[16,64,128]{2,1,0:T(8,128)S(1)}, u32[]{:S(2)}, u32[]{:S(2)}) async-start(f32[16,64,128]{2,1,0:T(8,128)} %bitcast.8), calls=%async_computation | async-start | bytes 1048576 | tf_op jit(solution)/shard_map/all_to_all | solution.py:274
  20.3 2.2 %collective-permute-start = (f32[400,256]{1,0:T(8,128)}, f32[400,256]{1,0:T(8,128)S(1)}, u32[]{:S(2)}, u32[]{:S(2)}) collective-permute-start(f32[400,256]{1,0:T(8,128)} %rhs_hbm.1), channel_id=1, source_target_pairs={{0,2},{1,3},{2,4},{3,5},{4,6},{5,7},{6,8},{7,9},{8,10},{9,11},{10,... | collective-permute-start | bytes 1228808 | tf_op jit(solution)/shard_map/ppermute | solution.py:302
  22.5 2.4 %collective-permute-start.2 = (f32[400,256]{1,0:T(8,128)S(1)}, f32[400,256]{1,0:T(8,128)S(1)}, u32[]{:S(2)}, u32[]{:S(2)}) collective-permute-start(f32[400,256]{1,0:T(8,128)S(1)} %get-tuple-element.26.gl_a), channel_id=1, source_target_pairs={{0,1},{1,0},{2,3},{3,2},{4,5},{5,4},{6,7},{7,6},{8,9},{9,8},{10,11... | collective-permute-start | bytes 1228808 | tf_op jit(solution)/shard_map/ppermute | solution.py:294
  24.9 0.6 collective-permute-start.4
  25.6 2.3 %collective-permute-start.3 = (f32[400,256]{1,0:T(8,128)S(1)}, f32[400,256]{1,0:T(8,128)S(1)}, u32[]{:S(2)}, u32[]{:S(2)}) collective-permute-start(f32[400,256]{1,0:T(8,128)S(1)} %get-tuple-element.27), channel_id=1, source_target_pairs={{0,2},{1,3},{2,4},{3,5},{4,6},{5,7},{6,8},{7,9},{8,10},{9,11},{10,... | collective-permute-start | bytes 1228808 | tf_op jit(solution)/shard_map/ppermute | solution.py:302
  27.8 0.7 all-to-all-done
  28.5 0.0 copy-start.12
  28.5 4.8 %collective-permute-start.6 = (f32[64,128]{1,0:T(8,128)S(1)}, f32[64,128]{1,0:T(8,128)S(1)}, u32[]{:S(2)}, u32[]{:S(2)}) collective-permute-start(f32[64,128]{1,0:T(8,128)S(1)} %reduce_sum.18), channel_id=1, source_target_pairs={{0,28},{2,30},{4,8},{6,10},{8,4},{10,6},{12,16},{14,18},{16,12},{1... | collective-permute-start | bytes 98312 | tf_op jit(solution)/shard_map/ppermute | solution.py:278
  33.3 8.5 %collective-permute-done.6 = f32[64,128]{1,0:T(8,128)S(1)} collective-permute-done((f32[64,128]{1,0:T(8,128)S(1)}, f32[64,128]{1,0:T(8,128)S(1)}, u32[]{:S(2)}, u32[]{:S(2)}) %collective-permute-start.6) | collective-permute-done | bytes 32800 | tf_op jit(solution)/shard_map/ppermute | solution.py:278
  41.8 1.1 collective-permute-done.1.racc.rest_4_
  42.9 1.5 %collective-permute-start.7 = (f32[64,128]{1,0:T(8,128)S(1)}, f32[64,128]{1,0:T(8,128)S(1)}, u32[]{:S(2)}, u32[]{:S(2)}) collective-permute-start(f32[64,128]{1,0:T(8,128)S(1)} %add.6.one), channel_id=1, source_target_pairs={{0,12},{2,14},{4,24},{6,26},{8,20},{10,22},{12,0},{14,2},{16,28},{... | collective-permute-start | bytes 98312 | tf_op jit(solution)/shard_map/ppermute | solution.py:279
  44.4 4.0 %collective-permute-done.2.gl_b.rest_0_ = f32[400,256]{1,0:T(8,128)S(1)} collective-permute-done((f32[400,256]{1,0:T(8,128)S(1)}, f32[400,256]{1,0:T(8,128)S(1)}, u32[]{:S(2)}, u32[]{:S(2)}) %collective-permute-start.2) | collective-permute-done | bytes 409632 | tf_op jit(solution)/shard_map/ppermute | solution.py:294
  48.4 4.9 %collective-permute-done.4.gc_b.rest_2_ = f32[400,256]{1,0:T(8,128)S(1)} collective-permute-done((f32[400,256]{1,0:T(8,128)S(1)}, f32[400,256]{1,0:T(8,128)S(1)}, u32[]{:S(2)}, u32[]{:S(2)}) %collective-permute-start.4) | collective-permute-done | bytes 409632 | tf_op jit(solution)/shard_map/ppermute | solution.py:302
  53.3 0.8 shard_map.157
  54.2 5.2 %all-to-all-start.1 = ((f32[16,64,128]{2,1,0:T(8,128)}), f32[16,64,128]{2,1,0:T(8,128)S(1)}, u32[]{:S(2)}, u32[]{:S(2)}) async-start(f32[16,64,128]{2,1,0:T(8,128)} %shard_map.157), calls=%async_computation.1 | async-start | bytes 1048576 | tf_op jit(solution)/shard_map/all_to_all | solution.py:285
  59.3 0.0 copy-start.4
  59.3 0.7 copy-done.4
  60.0 1.0 copy-done.3
  61.0 0.2 shard_map.155
  61.3 6.3 %all-to-all-done.1 = f32[16,64,128]{2,1,0:T(8,128)S(1)} async-done(((f32[16,64,128]{2,1,0:T(8,128)}), f32[16,64,128]{2,1,0:T(8,128)S(1)}, u32[]{:S(2)}, u32[]{:S(2)}) %all-to-all-start.1) | async-done | bytes 524320 | tf_op jit(solution)/shard_map/all_to_all | solution.py:285
  67.6 0.0 copy-start.9
  67.6 0.0 copy-start.10
  67.6 0.0 copy-start.6
  67.6 2.4 %collective-permute-start.8 = (f32[1024,128]{1,0:T(8,128)S(1)}, f32[1024,128]{1,0:T(8,128)S(1)}, u32[]{:S(2)}, u32[]{:S(2)}) collective-permute-start(f32[1024,128]{1,0:T(8,128)S(1)} %shard_map.158.gw_mine), channel_id=1, source_target_pairs={{0,2},{2,0},{4,6},{6,4},{8,10},{10,8},{12,14},{14,12},{16,18},{18,... | collective-permute-start | bytes 1572872 | tf_op jit(solution)/shard_map/ppermute | solution.py:290
  70.1 1.5 %collective-permute-done.8.gw_other = f32[1024,128]{1,0:T(8,128)S(1)} collective-permute-done((f32[1024,128]{1,0:T(8,128)S(1)}, f32[1024,128]{1,0:T(8,128)S(1)}, u32[]{:S(2)}, u32[]{:S(2)}) %collective-permute-start.8) | collective-permute-done | bytes 524320 | tf_op jit(solution)/shard_map/ppermute | solution.py:290
  71.6 8.1 %shard_map.159 = (f32[400,256]{1,0:T(8,128)S(1)}, f32[400,256]{1,0:T(8,128)S(1)}, f32[1024,128]{1,0:T(8,128)S(1)}, f32[1024,128]{1,0:T(8,128)S(1)}, f32[400,640]{1,0:T(8,128)}, /*index=5*/f32[1,640]{1,0:T(1,128)S(1)}) custom-call(s32[2,1024]{1,0:T(2,128)S(1)} %bitcast.19, s32[2,1024]{1,0:T(2,128)S(1)} %bitcast.21, s32[2,1024]{1,0:T(2,128)S(1)} %bitcast.23, ...), custom_call_target="tpu_custom_call" | custom-call | flops 4000000000 | bytes 8000000 | tf_op jit(solution)/shard_map/pallas_call | solution.py:217
  79.8 0.5 collective-permute-start.11
  80.2 1.5 %collective-permute-done.11.two = f32[1024,128]{1,0:T(8,128)S(1)} collective-permute-done((f32[1024,128]{1,0:T(8,128)S(1)}, f32[1024,128]{1,0:T(8,128)S(1)}, u32[]{:S(2)}, u32[]{:S(2)}) %collective-permute-start.11) | collective-permute-done | bytes 524320 | tf_op jit(solution)/shard_map/ppermute | solution.py:267
  81.8 0.9 shard_map.161
  82.7 4.2 %all-to-all-start.2 = ((f32[16,64,128]{2,1,0:T(8,128)}), f32[16,64,128]{2,1,0:T(8,128)S(1)}, u32[]{:S(2)}, u32[]{:S(2)}) async-start(f32[16,64,128]{2,1,0:T(8,128)} %bitcast.12), calls=%async_computation.2 | async-start | bytes 1048576 | tf_op jit(solution)/shard_map/all_to_all | solution.py:274
  86.8 2.0 %collective-permute-start.9 = (f32[400,256]{1,0:T(8,128)S(1)}, f32[400,256]{1,0:T(8,128)S(1)}, u32[]{:S(2)}, u32[]{:S(2)}) collective-permute-start(f32[400,256]{1,0:T(8,128)S(1)} %get-tuple-element.34.gl_a), channel_id=1, source_target_pairs={{0,1},{1,0},{2,3},{3,2},{4,5},{5,4},{6,7},{7,6},{8,9},{9,8},{10,11... | collective-permute-start | bytes 1228808 | tf_op jit(solution)/shard_map/ppermute | solution.py:294
  88.8 1.1 collective-permute-start.10
  89.9 5.1 %all-to-all-done.2 = f32[16,64,128]{2,1,0:T(8,128)S(1)} async-done(((f32[16,64,128]{2,1,0:T(8,128)}), f32[16,64,128]{2,1,0:T(8,128)S(1)}, u32[]{:S(2)}, u32[]{:S(2)}) %all-to-all-start.2) | async-done | bytes 524320 | tf_op jit(solution)/shard_map/all_to_all | solution.py:274
  95.0 0.1 collective-permute-start.12
  95.1 4.3 %collective-permute-done.12 = f32[64,128]{1,0:T(8,128)S(1)} collective-permute-done((f32[64,128]{1,0:T(8,128)S(1)}, f32[64,128]{1,0:T(8,128)S(1)}, u32[]{:S(2)}, u32[]{:S(2)}) %collective-permute-start.12) | collective-permute-done | bytes 32800 | tf_op jit(solution)/shard_map/ppermute | solution.py:278
  99.4 4.2 %collective-permute-done.9.gl_b.rest_0_ = f32[400,256]{1,0:T(8,128)S(1)} collective-permute-done((f32[400,256]{1,0:T(8,128)S(1)}, f32[400,256]{1,0:T(8,128)S(1)}, u32[]{:S(2)}, u32[]{:S(2)}) %collective-permute-start.9) | collective-permute-done | bytes 409632 | tf_op jit(solution)/shard_map/ppermute | solution.py:294
  103.6 8.8 %collective-permute-done.10.gc_b.rest_2_ = f32[400,256]{1,0:T(8,128)S(1)} collective-permute-done((f32[400,256]{1,0:T(8,128)S(1)}, f32[400,256]{1,0:T(8,128)S(1)}, u32[]{:S(2)}, u32[]{:S(2)}) %collective-permute-start.10) | collective-permute-done | bytes 409632 | tf_op jit(solution)/shard_map/ppermute | solution.py:294
  112.5 12.8 %all_to_all.20 = f32[16,64,128]{2,1,0:T(8,128)S(1)} all-to-all(f32[16,64,128]{2,1,0:T(8,128)S(1)} %shard_map.162), channel_id=1, replica_groups={{0,4,32,36,64,68,96,100,128,132,160,164,192,196,224,228},{12,8,44,40,76..., dimensions={0} | all-to-all | bytes 1048576 | tf_op jit(solution)/shard_map/all_to_all | solution.py:285
  125.2 3.4 %collective-permute-start.14 = (f32[1024,128]{1,0:T(8,128)S(1)}, f32[1024,128]{1,0:T(8,128)S(1)}, u32[]{:S(2)}, u32[]{:S(2)}) collective-permute-start(f32[1024,128]{1,0:T(8,128)S(1)} %bitcast.14), channel_id=1, source_target_pairs={{0,2},{2,0},{4,6},{6,4},{8,10},{10,8},{12,14},{14,12},{16,18},{18,... | collective-permute-start | bytes 1572872 | tf_op jit(solution)/shard_map/ppermute | solution.py:290
  128.7 1.0 shard_map.160
  129.7 0.5 collective-permute-done.14.gw_other
  130.2 1.3 shard_map.163
  131.5 0.6 reduce
  (31 shorter events, 0.2 us)
Async XLA Ops:
  9.7 12.8 %copy-start.2 = (f32[400,256]{1,0:T(8,128)}, f32[400,256]{1,0:T(8,128)S(1)}, u32[]{:S(2)}) copy-start(f32[400,256]{1,0:T(8,128)S(1)} %get-tuple-element.26.gl_a) | copy-start | bytes 1228804
  9.7 4.9 %collective-permute-start.5 = (f32[1024,128]{1,0:T(8,128)S(1)}, f32[1024,128]{1,0:T(8,128)S(1)}, u32[]{:S(2)}, u32[]{:S(2)}) collective-permute-start(f32[1024,128]{1,0:T(8,128)S(1)} %get-tuple-element.33), channel_id=1, source_target_pairs={{0,2},{2,0},{4,6},{6,4},{8,10},{10,8},{12,14},{14,12},{16,18},{18,... | collective-permute-start | bytes 1572872 | tf_op jit(solution)/shard_map/ppermute | solution.py:267
  15.5 13.0 %all-to-all-start = ((f32[16,64,128]{2,1,0:T(8,128)}), f32[16,64,128]{2,1,0:T(8,128)S(1)}, u32[]{:S(2)}, u32[]{:S(2)}) async-start(f32[16,64,128]{2,1,0:T(8,128)} %bitcast.8), calls=%async_computation | async-start | bytes 1048576 | tf_op jit(solution)/shard_map/all_to_all | solution.py:274
  20.3 24.1 %collective-permute-start = (f32[400,256]{1,0:T(8,128)}, f32[400,256]{1,0:T(8,128)S(1)}, u32[]{:S(2)}, u32[]{:S(2)}) collective-permute-start(f32[400,256]{1,0:T(8,128)} %rhs_hbm.1), channel_id=1, source_target_pairs={{0,2},{1,3},{2,4},{3,5},{4,6},{5,7},{6,8},{7,9},{8,10},{9,11},{10,... | collective-permute-start | bytes 1228808 | tf_op jit(solution)/shard_map/ppermute | solution.py:302
  22.5 25.9 %collective-permute-start.2 = (f32[400,256]{1,0:T(8,128)S(1)}, f32[400,256]{1,0:T(8,128)S(1)}, u32[]{:S(2)}, u32[]{:S(2)}) collective-permute-start(f32[400,256]{1,0:T(8,128)S(1)} %get-tuple-element.26.gl_a), channel_id=1, source_target_pairs={{0,1},{1,0},{2,3},{3,2},{4,5},{5,4},{6,7},{7,6},{8,9},{9,8},{10,11... | collective-permute-start | bytes 1228808 | tf_op jit(solution)/shard_map/ppermute | solution.py:294
  24.9 28.4 %collective-permute-start.4 = (f32[400,256]{1,0:T(8,128)S(1)}, f32[400,256]{1,0:T(8,128)S(1)}, u32[]{:S(2)}, u32[]{:S(2)}) collective-permute-start(f32[400,256]{1,0:T(8,128)S(1)} %get-tuple-element.27), channel_id=1, source_target_pairs={{0,3},{1,2},{2,5},{3,4},{4,7},{5,6},{6,9},{7,8},{8,11},{9,10},{10,... | collective-permute-start | bytes 1228808 | tf_op jit(solution)/shard_map/ppermute | solution.py:302
  25.6 27.7 %collective-permute-start.3 = (f32[400,256]{1,0:T(8,128)S(1)}, f32[400,256]{1,0:T(8,128)S(1)}, u32[]{:S(2)}, u32[]{:S(2)}) collective-permute-start(f32[400,256]{1,0:T(8,128)S(1)} %get-tuple-element.27), channel_id=1, source_target_pairs={{0,2},{1,3},{2,4},{3,5},{4,6},{5,7},{6,8},{7,9},{8,10},{9,11},{10,... | collective-permute-start | bytes 1228808 | tf_op jit(solution)/shard_map/ppermute | solution.py:302
  28.5 13.3 %copy-start.12 = (f32[256]{0:T(256)S(1)}, f32[256]{0:T(256)}, u32[]{:S(2)}) copy-start(f32[256]{0:T(256)} %param.15) | copy-start | bytes 3076
  28.5 13.3 %collective-permute-start.6 = (f32[64,128]{1,0:T(8,128)S(1)}, f32[64,128]{1,0:T(8,128)S(1)}, u32[]{:S(2)}, u32[]{:S(2)}) collective-permute-start(f32[64,128]{1,0:T(8,128)S(1)} %reduce_sum.18), channel_id=1, source_target_pairs={{0,28},{2,30},{4,8},{6,10},{8,4},{10,6},{12,16},{14,18},{16,12},{1... | collective-permute-start | bytes 98312 | tf_op jit(solution)/shard_map/ppermute | solution.py:278
  41.8 1.1 collective-permute-start.1
  42.9 10.3 %collective-permute-start.7 = (f32[64,128]{1,0:T(8,128)S(1)}, f32[64,128]{1,0:T(8,128)S(1)}, u32[]{:S(2)}, u32[]{:S(2)}) collective-permute-start(f32[64,128]{1,0:T(8,128)S(1)} %add.6.one), channel_id=1, source_target_pairs={{0,12},{2,14},{4,24},{6,26},{8,20},{10,22},{12,0},{14,2},{16,28},{... | collective-permute-start | bytes 98312 | tf_op jit(solution)/shard_map/ppermute | solution.py:279
  54.1 5.2 %copy-start.1 = (f32[400,256]{1,0:T(8,128)S(1)}, f32[400,256]{1,0:T(8,128)}, u32[]{:S(2)}) copy-start(f32[400,256]{1,0:T(8,128)} %lhs.2) | copy-start | bytes 1228804
  54.2 13.4 %all-to-all-start.1 = ((f32[16,64,128]{2,1,0:T(8,128)}), f32[16,64,128]{2,1,0:T(8,128)S(1)}, u32[]{:S(2)}, u32[]{:S(2)}) async-start(f32[16,64,128]{2,1,0:T(8,128)} %shard_map.157), calls=%async_computation.1 | async-start | bytes 1048576 | tf_op jit(solution)/shard_map/all_to_all | solution.py:285
  59.3 0.7 copy-start.4
  60.0 1.0 copy-start.3
  67.6 4.0 %copy-start.5 = (f32[400,640]{1,0:T(8,128)S(1)}, f32[400,640]{1,0:T(8,128)}, u32[]{:S(2)}) copy-start(f32[400,640]{1,0:T(8,128)} %rel.1) | copy-start | bytes 3072004
  67.6 2.5 %copy-start.11 = (f32[640]{0:T(1024)S(1)}, f32[640]{0:T(1024)}, u32[]{:S(2)}) copy-start(f32[640]{0:T(1024)} %param.16) | copy-start | bytes 7684
  67.6 4.0 %copy-start.7 = (s32[1,1,2,1024]{3,2,1,0:T(2,128)S(1)}, s32[1,1,2,1024]{3,2,1,0:T(2,128)}, u32[]{:S(2)}) copy-start(s32[1,1,2,1024]{3,2,1,0:T(2,128)} %param.18) | copy-start | bytes 24580
  67.6 4.0 %copy-start.8 = (s32[1,1,2,1024]{3,2,1,0:T(2,128)S(1)}, s32[1,1,2,1024]{3,2,1,0:T(2,128)}, u32[]{:S(2)}) copy-start(s32[1,1,2,1024]{3,2,1,0:T(2,128)} %param.19) | copy-start | bytes 24580
  67.6 4.0 %copy-start.9 = (s32[1,1,2,4,128]{4,3,2,1,0:T(4,128)S(1)}, s32[1,1,2,4,128]{4,3,2,1,0:T(4,128)}, u32[]{:S(2)}) copy-start(s32[1,1,2,4,128]{4,3,2,1,0:T(4,128)} %param.21) | copy-start | bytes 12292
  67.6 4.0 %copy-start.10 = (s32[1,1,2]{2,1,0:T(1,128)S(1)}, s32[1,1,2]{2,1,0:T(1,128)}, u32[]{:S(2)}) copy-start(s32[1,1,2]{2,1,0:T(1,128)} %param.20) | copy-start | bytes 28
  67.6 4.0 %copy-start.6 = (s32[1,1,2,1024]{3,2,1,0:T(2,128)S(1)}, s32[1,1,2,1024]{3,2,1,0:T(2,128)}, u32[]{:S(2)}) copy-start(s32[1,1,2,1024]{3,2,1,0:T(2,128)} %param.17) | copy-start | bytes 24580
  67.6 4.0 %collective-permute-start.8 = (f32[1024,128]{1,0:T(8,128)S(1)}, f32[1024,128]{1,0:T(8,128)S(1)}, u32[]{:S(2)}, u32[]{:S(2)}) collective-permute-start(f32[1024,128]{1,0:T(8,128)S(1)} %shard_map.158.gw_mine), channel_id=1, source_target_pairs={{0,2},{2,0},{4,6},{6,4},{8,10},{10,8},{12,14},{14,12},{16,18},{18,... | collective-permute-start | bytes 1572872 | tf_op jit(solution)/shard_map/ppermute | solution.py:290
  79.8 2.0 %collective-permute-start.11 = (f32[1024,128]{1,0:T(8,128)S(1)}, f32[1024,128]{1,0:T(8,128)S(1)}, u32[]{:S(2)}, u32[]{:S(2)}) collective-permute-start(f32[1024,128]{1,0:T(8,128)S(1)} %get-tuple-element.43), channel_id=1, source_target_pairs={{0,2},{2,0},{4,6},{6,4},{8,10},{10,8},{12,14},{14,12},{16,18},{18,... | collective-permute-start | bytes 1572872 | tf_op jit(solution)/shard_map/ppermute | solution.py:267
  82.7 12.4 %all-to-all-start.2 = ((f32[16,64,128]{2,1,0:T(8,128)}), f32[16,64,128]{2,1,0:T(8,128)S(1)}, u32[]{:S(2)}, u32[]{:S(2)}) async-start(f32[16,64,128]{2,1,0:T(8,128)} %bitcast.12), calls=%async_computation.2 | async-start | bytes 1048576 | tf_op jit(solution)/shard_map/all_to_all | solution.py:274
  86.8 16.8 %collective-permute-start.9 = (f32[400,256]{1,0:T(8,128)S(1)}, f32[400,256]{1,0:T(8,128)S(1)}, u32[]{:S(2)}, u32[]{:S(2)}) collective-permute-start(f32[400,256]{1,0:T(8,128)S(1)} %get-tuple-element.34.gl_a), channel_id=1, source_target_pairs={{0,1},{1,0},{2,3},{3,2},{4,5},{5,4},{6,7},{7,6},{8,9},{9,8},{10,11... | collective-permute-start | bytes 1228808 | tf_op jit(solution)/shard_map/ppermute | solution.py:294
  88.8 23.6 %collective-permute-start.10 = (f32[400,256]{1,0:T(8,128)S(1)}, f32[400,256]{1,0:T(8,128)S(1)}, u32[]{:S(2)}, u32[]{:S(2)}) collective-permute-start(f32[400,256]{1,0:T(8,128)S(1)} %get-tuple-element.35.gc_a.rest_1_), channel_id=1, source_target_pairs={{0,1},{1,0},{2,3},{3,2},{4,5},{5,4},{6,7},{7,6},{8,9},{9,8},{10,11... | collective-permute-start | bytes 1228808 | tf_op jit(solution)/shard_map/ppermute | solution.py:294
  95.0 4.4 %collective-permute-start.12 = (f32[64,128]{1,0:T(8,128)S(1)}, f32[64,128]{1,0:T(8,128)S(1)}, u32[]{:S(2)}, u32[]{:S(2)}) collective-permute-start(f32[64,128]{1,0:T(8,128)S(1)} %reduce_sum.19), channel_id=1, source_target_pairs={{0,28},{2,30},{4,8},{6,10},{8,4},{10,6},{12,16},{14,18},{16,12},{1... | collective-permute-start | bytes 98312 | tf_op jit(solution)/shard_map/ppermute | solution.py:278
  99.4 13.0 %collective-permute-start.13 = (f32[64,128]{1,0:T(8,128)S(1)}, f32[64,128]{1,0:T(8,128)S(1)}, u32[]{:S(2)}, u32[]{:S(2)}) collective-permute-start(f32[64,128]{1,0:T(8,128)S(1)} %add.7.one), channel_id=1, source_target_pairs={{0,12},{2,14},{4,24},{6,26},{8,20},{10,22},{12,0},{14,2},{16,28},{... | collective-permute-start | bytes 98312 | tf_op jit(solution)/shard_map/ppermute | solution.py:279
  125.2 5.0 %collective-permute-start.14 = (f32[1024,128]{1,0:T(8,128)S(1)}, f32[1024,128]{1,0:T(8,128)S(1)}, u32[]{:S(2)}, u32[]{:S(2)}) collective-permute-start(f32[1024,128]{1,0:T(8,128)S(1)} %bitcast.14), channel_id=1, source_target_pairs={{0,2},{2,0},{4,6},{6,4},{8,10},{10,8},{12,14},{14,12},{16,18},{18,... | collective-permute-start | bytes 1572872 | tf_op jit(solution)/shard_map/ppermute | solution.py:290
  128.7 1.5 %copy-start = (f32[400,640]{1,0:T(8,128)S(1)}, f32[400,640]{1,0:T(8,128)}, u32[]{:S(2)}) copy-start(f32[400,640]{1,0:T(8,128)} %get-tuple-element.40.rel) | copy-start | bytes 3072004

commit v3 on v2

--- a/solution.py
+++ b/solution.py
@@ -110,7 +110,7 @@
     hot = one_hot(ridx[pl.ds(t, 1), :], rows)
     total = nt(ph[...], hot) + nt(pw[...], hot)
     hot = jnp.concatenate([hot_neg(c) for c in range(spans)], axis=1)
-    gctx[...] = total + (nt(nh[...], hot) + nt(nl[...], hot))
+    gctx[pl.ds(0, d), :] = total + (nt(nh[...], hot) + nt(nl[...], hot))
 
 
 def work_shapes(d, edges, negs, rels):
@@ -131,10 +131,10 @@
 
 
 def first_kernel(spans, core, lidx_hbm, ridx_hbm, nidx_hbm, widx_hbm, ends_hbm, rhs_hbm, lhs_hbm,
-                 rel_hbm, glhs, gctx, keep, send, grel,
-                 lidx, ridx, nidx, widx, ends, rhs, lhs, rel, sems, *work):
-    sources = (lidx_hbm, ridx_hbm, nidx_hbm, widx_hbm, ends_hbm, rhs_hbm, lhs_hbm, rel_hbm)
-    targets = (lidx, ridx, nidx, widx, ends, rhs, lhs, rel)
+                 rel_hbm, racc_hbm, glhs, gctx, keep, send, grel,
+                 lidx, ridx, nidx, widx, ends, rhs, lhs, rel, racc, sems, *work):
+    sources = (lidx_hbm, ridx_hbm, nidx_hbm, widx_hbm, ends_hbm, rhs_hbm, lhs_hbm, rel_hbm, racc_hbm)
+    targets = (lidx, ridx, nidx, widx, ends, rhs, lhs, rel, racc)
     copies = [
         pltpu.make_async_copy(source, target, sems.at[i])
         for i, (source, target) in enumerate(zip(sources, targets))
@@ -144,6 +144,8 @@
     for copy in copies:
         copy.wait()
     bucket(0, spans, (lidx, ridx, widx, nidx), ends, (lhs, rhs, rel), (glhs, gctx, grel), work)
+    tail = gctx.shape[0] - lhs.shape[0]
+    gctx[pl.ds(lhs.shape[0], tail), :] = jnp.broadcast_to(racc[...], (tail, racc.shape[1]))
     halves(core[0], grel, keep, send, rel.shape[0] * (rel.shape[1] // LANES))
 
 
@@ -175,6 +177,14 @@
     bucket(1, spans, (lidx, ridx, widx, nidx), ends, (lhs, rhs, rel_new), (glhs, gctx, grel), work)
     halves(core[0], grel, keep, send, rel.shape[0] * (rel.shape[1] // LANES))
     copy.wait()
+
+
+def moved_kernel(lhs, rhs, lacc, gl_a, gl_b, gc_a, gc_b, lhs_new, rhs_new, lacc_new, racc_new):
+    d = lhs.shape[0]
+    update_pair(lhs, lacc, gl_a, gl_b, lhs_new, lacc_new)
+    update_pair(
+        rhs, gc_a.at[pl.ds(d, 1)], gc_a.at[pl.ds(0, d)], gc_b.at[pl.ds(0, d)], rhs_new, racc_new
+    )
 
 
 def pair_kernel(lhs, rhs, lacc, racc, gl_a, gl_b, gc_a, gc_b, lhs_new, rhs_new, lacc_new, racc_new):
@@ -234,14 +244,14 @@
 def near_groups():
     groups = []
     for core in range(2):
-        for zh in range(4):
-            members = [None] * 16
-            for y in range(4):
-                for x in range(2):
+        for x in range(2):
+            for zh in range(4):
+                members = [None] * 8
+                for y in range(4):
                     for zl in range(2):
                         z = zh * 2 + zl
-                        members[(y * 2 + x) * 2 + ((z ^ (z >> 1)) & 1)] = place(y, x, z, core)
-            groups.append(members)
+                        members[y * 2 + ((z ^ (z >> 1)) & 1)] = place(y, x, z, core)
+                groups.append(members)
     return groups
 
 
@@ -260,6 +270,7 @@
 FAR_PAIRS = (
     pairs(lambda y, x, z, c: (y, x, (z + (1 if z % 2 else 7)) % 8, c)),
     pairs(lambda y, x, z, c: (y, x, z ^ (3 if z in (0, 3, 4, 7) else 7), c)),
+    pairs(lambda y, x, z, c: (y, 1 - x, z, c)),
 )
 
 
@@ -275,8 +286,9 @@
         part.reshape(n, rows, LANES), "blk", 0, 0, axis_index_groups=groups
     )
     total = jnp.sum(got, axis=0)
-    total = total + lax.ppermute(total, "blk", FAR_PAIRS[0])
-    got = lax.ppermute(total, "blk", FAR_PAIRS[1])
+    for move in FAR_PAIRS[:-1]:
+        total = total + lax.ppermute(total, "blk", move)
+    got = lax.ppermute(total, "blk", FAR_PAIRS[-1])
     ended = tuple(beside[1:])
     (spread,) = call(
         spread_kernel, (total, got) + ended, {2 + i: AN for i in range(len(ended))},
@@ -319,27 +331,28 @@
     work = work_shapes(d, edges, spans * neg, rels)
     sources = tuple(
         pltpu.with_memory_space_constraint(a, pltpu.HBM)
-        for a in (lidx, ridx, nidx, widx, ends, rhs, lhs, rel)
+        for a in (lidx, ridx, nidx, widx, ends, rhs, lhs, rel, racc)
     )
     glhs, gctx, keep, send = call(
         functools.partial(first_kernel, spans), (core,) + sources,
-        {0: SM} | {1 + i: HB for i in range(8)},
-        [slab, slab, half, half],
+        {0: SM} | {1 + i: HB for i in range(9)},
+        [slab, (d + 8, rows), half, half],
         [(full, LANES)]
         + [pltpu.VMEM(a.shape, a.dtype) for a in (lidx, ridx, nidx, widx)]
-        + [pltpu.SMEM(ends.shape, ends.dtype), slab, slab, table, pltpu.SemaphoreType.DMA((8,))]
+        + [pltpu.SMEM(ends.shape, ends.dtype), slab, slab, table, state, pltpu.SemaphoreType.DMA((9,))]
         + work,
         4_000_000_000, 40,
     )
 
+    rhs_in = onward(rhs, False)
+
     def exchange_first():
-        return (glhs, swap(glhs), onward(gctx, False), onward(gctx, True),
-                onward(rhs, False), onward(racc, False))
+        return glhs, swap(glhs), onward(gctx, False), onward(gctx, True), rhs_in
 
     def update_first(arrived):
-        gl_a, gl_b, gc_a, gc_b, rhs_in, racc_in = arrived
+        gl_a, gl_b, gc_a, gc_b, rhs_in = arrived
         return call(
-            pair_kernel, (lhs, rhs_in, lacc, racc_in, gl_a, gl_b, gc_a, gc_b), {},
+            moved_kernel, (lhs, rhs_in, lacc, gl_a, gl_b, gc_a, gc_b), {},
             [slab, slab, state, state], [], 1_000_000, 2,
         )
 

time: 133 us -> 126 us (0.947)
  waiting for transfers between devices: 53 us -> 46.4 us
  blocking collectives: 12.8 us -> 10 us
  starting transfers between devices: 40.7 us -> 42.9 us
    ppermute x3, waiting for transfers between devices: 17 us -> 0.01 us  [swap(): return lax.ppermute(x, 'rel', [(0, 1), (1, 0)])]
    ppermute x4 -> x6, waiting for transfers between devices: 12.8 us -> 25 us  [the longest x4 21.4 us: sum_over_blk(): total = total + lax.ppermute(total, 'blk', move)]
    ppermute x4 -> x6, starting transfers between devices: 6.32 us -> 12.5 us  [the longest x4 8.74 us: sum_over_blk(): total = total + lax.ppermute(total, 'blk', move)]
    ppermute x4 -> x3, waiting for transfers between devices: 6.03 us -> 0.01 us  [onward(): return lax.ppermute(x, ('blk', 'rel'), moves)]
    all_to_all x2, waiting for transfers between devices: 5.79 us -> 8.8 us  [sum_over_blk(): lax.all_to_all(part.reshape(n, rows, LANES), 'blk', 0, 0, axis_index_grou...]
    all_to_all x1, blocking collectives: 12.8 us -> 10 us  [sum_over_blk(): mine = lax.all_to_all(spread, 'blk', 0, 0, axis_index_groups=groups)]
    ppermute x3, starting transfers between devices: 5.5 us -> 3.28 us  [swap(): return lax.ppermute(x, 'rel', [(0, 1), (1, 0)])]
    ppermute x4 -> x3, starting transfers between devices: 5.09 us -> 7.22 us  [onward(): return lax.ppermute(x, ('blk', 'rel'), moves)]
  transfers between devices with their start and end apart: 18 -> 19, of which waited for: 14 -> 13; matrix products, arithmetic and copies ran while one was open for 0% -> 0% of each run, Pallas kernels for 1% -> 1%
where the time goes in v3:
time: 126 us
  waiting for transfers between devices  46.4 us (37%)
  starting transfers between devices  42.9 us (34%)
  Pallas kernels  22.5 us (18%)
  blocking collectives  10 us (8%)
  local copies, waits for them, and re-layouts  2.34 us (2%)
    pallas_call x9, Pallas kernels, call(): pl.pallas_call(kernel, out_shape=[jax.ShapeDtypeStruct(o, F32) if isinsta...  22.4 us
    ppermute x4, waiting for transfers between devices, sum_over_blk(): total = total + lax.ppermute(total, 'blk', move)  21.4 us
    all_to_all x1, blocking collectives, sum_over_blk(): mine = lax.all_to_all(spread, 'blk', 0, 0, axis_index_groups=groups)  10 us
    all_to_all x2, waiting for transfers between devices, sum_over_blk(): lax.all_to_all(part.reshape(n, rows, LANES), 'blk', 0, 0, axis_index_grou...  8.8 us
    ppermute x4, starting transfers between devices, sum_over_blk(): total = total + lax.ppermute(total, 'blk', move)  8.74 us
    all_to_all x2, starting transfers between devices, sum_over_blk(): lax.all_to_all(part.reshape(n, rows, LANES), 'blk', 0, 0, axis_index_grou...  7.43 us
    all_to_all x1, waiting for transfers between devices, sum_over_blk(): mine = lax.all_to_all(spread, 'blk', 0, 0, axis_index_groups=groups)  7.42 us
    ppermute x3, starting transfers between devices, onward(): return lax.ppermute(x, ('blk', 'rel'), moves)  7.22 us
  transfers between devices with their start and end apart: 19, of which 13 were waited for; matrix products, arithmetic and copies ran while one was open for 0% of the time, Pallas kernels for 1%

profile of v3, /device:TPU:1, one launch (start us, length us, event | category | flops | bytes accessed | tf_op | source)
XLA Modules:
  0.0 125.6 jit_solution(9439542982664562897)
XLA Ops:
  0.6 9.1 %shard_map.154 = (f32[400,256]{1,0:T(8,128)S(1)}, f32[408,256]{1,0:T(8,128)S(1)}, f32[1024,128]{1,0:T(8,128)S(1)}, f32[1024,128]{1,0:T(8,128)S(1)}) custom-call(s32[1]{0:T(128)} %bitcast.1.core, s32[2,1024]{1,0:T(2,128)} %bitcast.18, s32[2,1024]{1,0:T(2,128)} %bitcast.20, s32[8,128]{1,0:T(8,128)} %bitcast.24, s32[2,1024]{1,0:T(2,128)} %bitcast.22, ...), custom_call_target="tpu_custom_call" | custom-call | flops 4000000000 | bytes 8000000 | tf_op jit(solution)/shard_map/pallas_call | solution.py:227
  9.7 0.0 copy-start.2
  9.7 3.3 %collective-permute-start.4 = (f32[1024,128]{1,0:T(8,128)S(1)}, f32[1024,128]{1,0:T(8,128)S(1)}, u32[]{:S(2)}, u32[]{:S(2)}) collective-permute-start(f32[1024,128]{1,0:T(8,128)S(1)} %get-tuple-element.33), channel_id=1, source_target_pairs={{0,2},{2,0},{4,6},{6,4},{8,10},{10,8},{12,14},{14,12},{16,18},{18,... | collective-permute-start | bytes 1572872 | tf_op jit(solution)/shard_map/ppermute | solution.py:278
  13.1 1.5 %collective-permute-done.4.two = f32[1024,128]{1,0:T(8,128)S(1)} collective-permute-done((f32[1024,128]{1,0:T(8,128)S(1)}, f32[1024,128]{1,0:T(8,128)S(1)}, u32[]{:S(2)}, u32[]{:S(2)}) %collective-permute-start.4) | collective-permute-done | bytes 524320 | tf_op jit(solution)/shard_map/ppermute | solution.py:278
  14.6 0.9 shard_map.156
  15.5 3.9 %all-to-all-start = ((f32[8,128,128]{2,1,0:T(8,128)}), f32[8,128,128]{2,1,0:T(8,128)S(1)}, u32[]{:S(2)}, u32[]{:S(2)}) async-start(f32[8,128,128]{2,1,0:T(8,128)} %bitcast.8), calls=%async_computation | async-start | bytes 1048576 | tf_op jit(solution)/shard_map/all_to_all | solution.py:285
  19.4 4.7 %collective-permute-start.3 = (f32[408,256]{1,0:T(8,128)S(1)}, f32[408,256]{1,0:T(8,128)S(1)}, u32[]{:S(2)}, u32[]{:S(2)}) collective-permute-start(f32[408,256]{1,0:T(8,128)S(1)} %get-tuple-element.27), channel_id=1, source_target_pairs={{0,3},{1,2},{2,5},{3,4},{4,7},{5,6},{6,9},{7,8},{8,11},{9,10},{10,... | collective-permute-start | bytes 1253384 | tf_op jit(solution)/shard_map/ppermute | solution.py:314
  24.2 2.5 %collective-permute-start = (f32[400,256]{1,0:T(8,128)S(1)}, f32[400,256]{1,0:T(8,128)S(1)}, u32[]{:S(2)}, u32[]{:S(2)}) collective-permute-start(f32[400,256]{1,0:T(8,128)S(1)} %copy-done.12), channel_id=1, source_target_pairs={{0,2},{1,3},{2,4},{3,5},{4,6},{5,7},{6,8},{7,9},{8,10},{9,11},{10,... | collective-permute-start | bytes 1228808 | tf_op jit(solution)/shard_map/ppermute | solution.py:314
  26.7 0.2 collective-permute-start.1
  26.9 1.8 %all-to-all-done = f32[8,128,128]{2,1,0:T(8,128)S(1)} async-done(((f32[8,128,128]{2,1,0:T(8,128)}), f32[8,128,128]{2,1,0:T(8,128)S(1)}, u32[]{:S(2)}, u32[]{:S(2)}) %all-to-all-start) | async-done | bytes 524320 | tf_op jit(solution)/shard_map/all_to_all | solution.py:285
  28.7 4.7 %collective-permute-start.5 = (f32[128,128]{1,0:T(8,128)S(1)}, f32[128,128]{1,0:T(8,128)S(1)}, u32[]{:S(2)}, u32[]{:S(2)}) collective-permute-start(f32[128,128]{1,0:T(8,128)S(1)} %reduce_sum.18), channel_id=1, source_target_pairs={{0,28},{2,30},{4,8},{6,10},{8,4},{10,6},{12,16},{14,18},{16,12},{1... | collective-permute-start | bytes 196616 | tf_op jit(solution)/shard_map/ppermute | solution.py:290
  33.5 9.4 %collective-permute-done.5 = f32[128,128]{1,0:T(8,128)S(1)} collective-permute-done((f32[128,128]{1,0:T(8,128)S(1)}, f32[128,128]{1,0:T(8,128)S(1)}, u32[]{:S(2)}, u32[]{:S(2)}) %collective-permute-start.5) | collective-permute-done | bytes 65568 | tf_op jit(solution)/shard_map/ppermute | solution.py:290
  42.9 2.0 %collective-permute-start.6 = (f32[128,128]{1,0:T(8,128)S(1)}, f32[128,128]{1,0:T(8,128)S(1)}, u32[]{:S(2)}, u32[]{:S(2)}) collective-permute-start(f32[128,128]{1,0:T(8,128)S(1)} %add.12), channel_id=1, source_target_pairs={{0,12},{2,14},{4,24},{6,26},{8,20},{10,22},{12,0},{14,2},{16,28},{... | collective-permute-start | bytes 196616 | tf_op jit(solution)/shard_map/ppermute | solution.py:290
  44.8 3.3 %collective-permute-done.6 = f32[128,128]{1,0:T(8,128)S(1)} collective-permute-done((f32[128,128]{1,0:T(8,128)S(1)}, f32[128,128]{1,0:T(8,128)S(1)}, u32[]{:S(2)}, u32[]{:S(2)}) %collective-permute-start.6) | collective-permute-done | bytes 65568 | tf_op jit(solution)/shard_map/ppermute | solution.py:290
  48.2 2.6 %collective-permute-start.7 = (f32[128,128]{1,0:T(8,128)S(1)}, f32[128,128]{1,0:T(8,128)S(1)}, u32[]{:S(2)}, u32[]{:S(2)}) collective-permute-start(f32[128,128]{1,0:T(8,128)S(1)} %add.13.one), channel_id=1, source_target_pairs={{0,32},{2,34},{4,36},{6,38},{8,40},{10,42},{12,44},{14,46},{16,48}... | collective-permute-start | bytes 196616 | tf_op jit(solution)/shard_map/ppermute | solution.py:291
  50.8 1.6 %collective-permute-done.7.two = f32[128,128]{1,0:T(8,128)S(1)} collective-permute-done((f32[128,128]{1,0:T(8,128)S(1)}, f32[128,128]{1,0:T(8,128)S(1)}, u32[]{:S(2)}, u32[]{:S(2)}) %collective-permute-start.7) | collective-permute-done | bytes 65568 | tf_op jit(solution)/shard_map/ppermute | solution.py:291
  52.4 0.8 shard_map.157
  53.2 4.3 %all-to-all-start.1 = ((f32[8,128,128]{2,1,0:T(8,128)}), f32[8,128,128]{2,1,0:T(8,128)S(1)}, u32[]{:S(2)}, u32[]{:S(2)}) async-start(f32[8,128,128]{2,1,0:T(8,128)} %shard_map.157), calls=%async_computation.1 | async-start | bytes 1048576 | tf_op jit(solution)/shard_map/all_to_all | solution.py:297
  57.5 0.7 copy-done.4
  58.2 1.0 copy-done.3
  59.2 0.3 shard_map.155
  59.5 7.4 %all-to-all-done.1 = f32[8,128,128]{2,1,0:T(8,128)S(1)} async-done(((f32[8,128,128]{2,1,0:T(8,128)}), f32[8,128,128]{2,1,0:T(8,128)S(1)}, u32[]{:S(2)}, u32[]{:S(2)}) %all-to-all-start.1) | async-done | bytes 524320 | tf_op jit(solution)/shard_map/all_to_all | solution.py:297
  66.9 0.0 copy-start.9
  66.9 0.0 copy-start.10
  66.9 0.0 copy-start.6
  67.0 0.1 collective-permute-start.8
  67.1 0.6 copy-done.11
  67.7 1.3 %collective-permute-done.8.gw_other = f32[1024,128]{1,0:T(8,128)S(1)} collective-permute-done((f32[1024,128]{1,0:T(8,128)S(1)}, f32[1024,128]{1,0:T(8,128)S(1)}, u32[]{:S(2)}, u32[]{:S(2)}) %collective-permute-start.8) | collective-permute-done | bytes 524320 | tf_op jit(solution)/shard_map/ppermute | solution.py:302
  69.0 8.1 %shard_map.159 = (f32[400,256]{1,0:T(8,128)S(1)}, f32[400,256]{1,0:T(8,128)S(1)}, f32[1024,128]{1,0:T(8,128)S(1)}, f32[1024,128]{1,0:T(8,128)S(1)}, f32[400,640]{1,0:T(8,128)}, /*index=5*/f32[1,640]{1,0:T(1,128)S(1)}) custom-call(s32[2,1024]{1,0:T(2,128)S(1)} %bitcast.19, s32[2,1024]{1,0:T(2,128)S(1)} %bitcast.21, s32[2,1024]{1,0:T(2,128)S(1)} %bitcast.23, ...), custom_call_target="tpu_custom_call" | custom-call | flops 4000000000 | bytes 8000000 | tf_op jit(solution)/shard_map/pallas_call | solution.py:227
  77.1 0.2 collective-permute-start.11
  77.3 1.8 %collective-permute-done.11.two = f32[1024,128]{1,0:T(8,128)S(1)} collective-permute-done((f32[1024,128]{1,0:T(8,128)S(1)}, f32[1024,128]{1,0:T(8,128)S(1)}, u32[]{:S(2)}, u32[]{:S(2)}) %collective-permute-start.11) | collective-permute-done | bytes 524320 | tf_op jit(solution)/shard_map/ppermute | solution.py:278
  79.1 0.9 shard_map.161
  80.0 3.5 %all-to-all-start.2 = ((f32[8,128,128]{2,1,0:T(8,128)}), f32[8,128,128]{2,1,0:T(8,128)S(1)}, u32[]{:S(2)}, u32[]{:S(2)}) async-start(f32[8,128,128]{2,1,0:T(8,128)} %bitcast.12), calls=%async_computation.2 | async-start | bytes 1048576 | tf_op jit(solution)/shard_map/all_to_all | solution.py:285
  83.5 2.3 %collective-permute-start.9 = (f32[400,256]{1,0:T(8,128)S(1)}, f32[400,256]{1,0:T(8,128)S(1)}, u32[]{:S(2)}, u32[]{:S(2)}) collective-permute-start(f32[400,256]{1,0:T(8,128)S(1)} %get-tuple-element.34.gl_a), channel_id=1, source_target_pairs={{0,1},{1,0},{2,3},{3,2},{4,5},{5,4},{6,7},{7,6},{8,9},{9,8},{10,11... | collective-permute-start | bytes 1228808 | tf_op jit(solution)/shard_map/ppermute | solution.py:306
  85.8 0.8 collective-permute-start.10
  86.6 7.0 %all-to-all-done.2 = f32[8,128,128]{2,1,0:T(8,128)S(1)} async-done(((f32[8,128,128]{2,1,0:T(8,128)}), f32[8,128,128]{2,1,0:T(8,128)S(1)}, u32[]{:S(2)}, u32[]{:S(2)}) %all-to-all-start.2) | async-done | bytes 524320 | tf_op jit(solution)/shard_map/all_to_all | solution.py:285
  93.6 1.8 %collective-permute-start.12 = (f32[128,128]{1,0:T(8,128)S(1)}, f32[128,128]{1,0:T(8,128)S(1)}, u32[]{:S(2)}, u32[]{:S(2)}) collective-permute-start(f32[128,128]{1,0:T(8,128)S(1)} %reduce_sum.19), channel_id=1, source_target_pairs={{0,28},{2,30},{4,8},{6,10},{8,4},{10,6},{12,16},{14,18},{16,12},{1... | collective-permute-start | bytes 196616 | tf_op jit(solution)/shard_map/ppermute | solution.py:290
  95.4 2.9 %collective-permute-done.12 = f32[128,128]{1,0:T(8,128)S(1)} collective-permute-done((f32[128,128]{1,0:T(8,128)S(1)}, f32[128,128]{1,0:T(8,128)S(1)}, u32[]{:S(2)}, u32[]{:S(2)}) %collective-permute-start.12) | collective-permute-done | bytes 65568 | tf_op jit(solution)/shard_map/ppermute | solution.py:290
  98.3 0.2 collective-permute-start.13
  98.5 5.7 %collective-permute-done.13 = f32[128,128]{1,0:T(8,128)S(1)} collective-permute-done((f32[128,128]{1,0:T(8,128)S(1)}, f32[128,128]{1,0:T(8,128)S(1)}, u32[]{:S(2)}, u32[]{:S(2)}) %collective-permute-start.13) | collective-permute-done | bytes 65568 | tf_op jit(solution)/shard_map/ppermute | solution.py:290
  104.3 1.2 collective-permute-start.14
  105.5 2.0 %collective-permute-done.14.two = f32[128,128]{1,0:T(8,128)S(1)} collective-permute-done((f32[128,128]{1,0:T(8,128)S(1)}, f32[128,128]{1,0:T(8,128)S(1)}, u32[]{:S(2)}, u32[]{:S(2)}) %collective-permute-start.14) | collective-permute-done | bytes 65568 | tf_op jit(solution)/shard_map/ppermute | solution.py:291
  107.5 10.0 %all_to_all.20 = f32[8,128,128]{2,1,0:T(8,128)S(1)} all-to-all(f32[8,128,128]{2,1,0:T(8,128)S(1)} %shard_map.162), channel_id=1, replica_groups={{0,4,64,68,128,132,192,196},{12,8,76,72,140,136,204,200},{16,20,80,84,1..., dimensions={0} | all-to-all | bytes 1048576 | tf_op jit(solution)/shard_map/all_to_all | solution.py:297
  117.5 4.6 %collective-permute-start.15 = (f32[1024,128]{1,0:T(8,128)S(1)}, f32[1024,128]{1,0:T(8,128)S(1)}, u32[]{:S(2)}, u32[]{:S(2)}) collective-permute-start(f32[1024,128]{1,0:T(8,128)S(1)} %bitcast.14), channel_id=1, source_target_pairs={{0,2},{2,0},{4,6},{6,4},{8,10},{10,8},{12,14},{14,12},{16,18},{18,... | collective-permute-start | bytes 1572872 | tf_op jit(solution)/shard_map/ppermute | solution.py:302
  122.2 1.0 shard_map.160
  123.2 0.5 collective-permute-done.15.gw_other
  123.7 1.3 %shard_map.163 = (f32[400,640]{1,0:T(8,128)}, f32[1,640]{1,0:T(1,128)S(1)}) custom-call(s32[1]{0:T(128)} %bitcast.1.core, f32[400,640]{1,0:T(8,128)S(1)} %copy-done, f32[1,640]{1,0:T(1,128)S(1)} %get-tuple-element.41.wacc, f32[1024,128]{1,0:T(8,128)S(1)} %bitcast.15, f32[1024,128]{1,0:T(8,128)S(1)} %collective-permute-done.15.gw_other), custom_call_target="tpu_custom_call" | custom-call | flops 1000000 | bytes 8000000 | tf_op jit(solution)/shard_map/pallas_call | solution.py:227
  125.0 0.6 reduce
  (35 shorter events, 0.2 us)
Async XLA Ops:
  9.7 16.9 %copy-start.2 = (f32[400,256]{1,0:T(8,128)}, f32[400,256]{1,0:T(8,128)S(1)}, u32[]{:S(2)}) copy-start(f32[400,256]{1,0:T(8,128)S(1)} %get-tuple-element.26.gl_a) | copy-start | bytes 1228804
  9.7 4.9 %collective-permute-start.4 = (f32[1024,128]{1,0:T(8,128)S(1)}, f32[1024,128]{1,0:T(8,128)S(1)}, u32[]{:S(2)}, u32[]{:S(2)}) collective-permute-start(f32[1024,128]{1,0:T(8,128)S(1)} %get-tuple-element.33), channel_id=1, source_target_pairs={{0,2},{2,0},{4,6},{6,4},{8,10},{10,8},{12,14},{14,12},{16,18},{18,... | collective-permute-start | bytes 1572872 | tf_op jit(solution)/shard_map/ppermute | solution.py:278
  15.5 8.7 %copy-start.12 = (f32[400,256]{1,0:T(8,128)S(1)}, f32[400,256]{1,0:T(8,128)}, u32[]{:S(2)}) copy-start(f32[400,256]{1,0:T(8,128)} %rhs_hbm.1) | copy-start | bytes 1228804
  15.5 13.2 %all-to-all-start = ((f32[8,128,128]{2,1,0:T(8,128)}), f32[8,128,128]{2,1,0:T(8,128)S(1)}, u32[]{:S(2)}, u32[]{:S(2)}) async-start(f32[8,128,128]{2,1,0:T(8,128)} %bitcast.8), calls=%async_computation | async-start | bytes 1048576 | tf_op jit(solution)/shard_map/all_to_all | solution.py:285
  19.4 31.3 %collective-permute-start.3 = (f32[408,256]{1,0:T(8,128)S(1)}, f32[408,256]{1,0:T(8,128)S(1)}, u32[]{:S(2)}, u32[]{:S(2)}) collective-permute-start(f32[408,256]{1,0:T(8,128)S(1)} %get-tuple-element.27), channel_id=1, source_target_pairs={{0,3},{1,2},{2,5},{3,4},{4,7},{5,6},{6,9},{7,8},{8,11},{9,10},{10,... | collective-permute-start | bytes 1253384 | tf_op jit(solution)/shard_map/ppermute | solution.py:314
  24.2 26.6 %collective-permute-start.2 = (f32[408,256]{1,0:T(8,128)S(1)}, f32[408,256]{1,0:T(8,128)S(1)}, u32[]{:S(2)}, u32[]{:S(2)}) collective-permute-start(f32[408,256]{1,0:T(8,128)S(1)} %get-tuple-element.27), channel_id=1, source_target_pairs={{0,2},{1,3},{2,4},{3,5},{4,6},{5,7},{6,8},{7,9},{8,10},{9,11},{10,... | collective-permute-start | bytes 1253384 | tf_op jit(solution)/shard_map/ppermute | solution.py:314
  24.2 26.6 %collective-permute-start = (f32[400,256]{1,0:T(8,128)S(1)}, f32[400,256]{1,0:T(8,128)S(1)}, u32[]{:S(2)}, u32[]{:S(2)}) collective-permute-start(f32[400,256]{1,0:T(8,128)S(1)} %copy-done.12), channel_id=1, source_target_pairs={{0,2},{1,3},{2,4},{3,5},{4,6},{5,7},{6,8},{7,9},{8,10},{9,11},{10,... | collective-permute-start | bytes 1228808 | tf_op jit(solution)/shard_map/ppermute | solution.py:314
  26.7 24.1 %collective-permute-start.1 = (f32[400,256]{1,0:T(8,128)S(1)}, f32[400,256]{1,0:T(8,128)S(1)}, u32[]{:S(2)}, u32[]{:S(2)}) collective-permute-start(f32[400,256]{1,0:T(8,128)S(1)} %get-tuple-element.26.gl_a), channel_id=1, source_target_pairs={{0,1},{1,0},{2,3},{3,2},{4,5},{5,4},{6,7},{7,6},{8,9},{9,8},{10,11... | collective-permute-start | bytes 1228808 | tf_op jit(solution)/shard_map/ppermute | solution.py:306
  28.7 14.1 %collective-permute-start.5 = (f32[128,128]{1,0:T(8,128)S(1)}, f32[128,128]{1,0:T(8,128)S(1)}, u32[]{:S(2)}, u32[]{:S(2)}) collective-permute-start(f32[128,128]{1,0:T(8,128)S(1)} %reduce_sum.18), channel_id=1, source_target_pairs={{0,28},{2,30},{4,8},{6,10},{8,4},{10,6},{12,16},{14,18},{16,12},{1... | collective-permute-start | bytes 196616 | tf_op jit(solution)/shard_map/ppermute | solution.py:290
  42.9 5.3 %collective-permute-start.6 = (f32[128,128]{1,0:T(8,128)S(1)}, f32[128,128]{1,0:T(8,128)S(1)}, u32[]{:S(2)}, u32[]{:S(2)}) collective-permute-start(f32[128,128]{1,0:T(8,128)S(1)} %add.12), channel_id=1, source_target_pairs={{0,12},{2,14},{4,24},{6,26},{8,20},{10,22},{12,0},{14,2},{16,28},{... | collective-permute-start | bytes 196616 | tf_op jit(solution)/shard_map/ppermute | solution.py:290
  48.2 4.2 %collective-permute-start.7 = (f32[128,128]{1,0:T(8,128)S(1)}, f32[128,128]{1,0:T(8,128)S(1)}, u32[]{:S(2)}, u32[]{:S(2)}) collective-permute-start(f32[128,128]{1,0:T(8,128)S(1)} %add.13.one), channel_id=1, source_target_pairs={{0,32},{2,34},{4,36},{6,38},{8,40},{10,42},{12,44},{14,46},{16,48}... | collective-permute-start | bytes 196616 | tf_op jit(solution)/shard_map/ppermute | solution.py:291
  53.2 4.3 %copy-start.1 = (f32[400,256]{1,0:T(8,128)S(1)}, f32[400,256]{1,0:T(8,128)}, u32[]{:S(2)}) copy-start(f32[400,256]{1,0:T(8,128)} %lhs.2) | copy-start | bytes 1228804
  53.2 13.7 %all-to-all-start.1 = ((f32[8,128,128]{2,1,0:T(8,128)}), f32[8,128,128]{2,1,0:T(8,128)S(1)}, u32[]{:S(2)}, u32[]{:S(2)}) async-start(f32[8,128,128]{2,1,0:T(8,128)} %shard_map.157), calls=%async_computation.1 | async-start | bytes 1048576 | tf_op jit(solution)/shard_map/all_to_all | solution.py:297
  57.5 0.7 copy-start.4
  58.2 1.0 copy-start.3
  66.9 2.1 %copy-start.5 = (f32[400,640]{1,0:T(8,128)S(1)}, f32[400,640]{1,0:T(8,128)}, u32[]{:S(2)}) copy-start(f32[400,640]{1,0:T(8,128)} %rel.1) | copy-start | bytes 3072004
  66.9 0.8 copy-start.11
  66.9 2.1 %copy-start.7 = (s32[1,1,2,1024]{3,2,1,0:T(2,128)S(1)}, s32[1,1,2,1024]{3,2,1,0:T(2,128)}, u32[]{:S(2)}) copy-start(s32[1,1,2,1024]{3,2,1,0:T(2,128)} %param.18) | copy-start | bytes 24580
  66.9 2.1 %copy-start.8 = (s32[1,1,2,1024]{3,2,1,0:T(2,128)S(1)}, s32[1,1,2,1024]{3,2,1,0:T(2,128)}, u32[]{:S(2)}) copy-start(s32[1,1,2,1024]{3,2,1,0:T(2,128)} %param.19) | copy-start | bytes 24580
  66.9 2.1 %copy-start.9 = (s32[1,1,2,4,128]{4,3,2,1,0:T(4,128)S(1)}, s32[1,1,2,4,128]{4,3,2,1,0:T(4,128)}, u32[]{:S(2)}) copy-start(s32[1,1,2,4,128]{4,3,2,1,0:T(4,128)} %param.21) | copy-start | bytes 12292
  66.9 2.1 %copy-start.10 = (s32[1,1,2]{2,1,0:T(1,128)S(1)}, s32[1,1,2]{2,1,0:T(1,128)}, u32[]{:S(2)}) copy-start(s32[1,1,2]{2,1,0:T(1,128)} %param.20) | copy-start | bytes 28
  66.9 2.0 %copy-start.6 = (s32[1,1,2,1024]{3,2,1,0:T(2,128)S(1)}, s32[1,1,2,1024]{3,2,1,0:T(2,128)}, u32[]{:S(2)}) copy-start(s32[1,1,2,1024]{3,2,1,0:T(2,128)} %param.17) | copy-start | bytes 24580
  67.0 2.0 %collective-permute-start.8 = (f32[1024,128]{1,0:T(8,128)S(1)}, f32[1024,128]{1,0:T(8,128)S(1)}, u32[]{:S(2)}, u32[]{:S(2)}) collective-permute-start(f32[1024,128]{1,0:T(8,128)S(1)} %shard_map.158.gw_mine), channel_id=1, source_target_pairs={{0,2},{2,0},{4,6},{6,4},{8,10},{10,8},{12,14},{14,12},{16,18},{18,... | collective-permute-start | bytes 1572872 | tf_op jit(solution)/shard_map/ppermute | solution.py:302
  77.1 2.0 %collective-permute-start.11 = (f32[1024,128]{1,0:T(8,128)S(1)}, f32[1024,128]{1,0:T(8,128)S(1)}, u32[]{:S(2)}, u32[]{:S(2)}) collective-permute-start(f32[1024,128]{1,0:T(8,128)S(1)} %get-tuple-element.43), channel_id=1, source_target_pairs={{0,2},{2,0},{4,6},{6,4},{8,10},{10,8},{12,14},{14,12},{16,18},{18,... | collective-permute-start | bytes 1572872 | tf_op jit(solution)/shard_map/ppermute | solution.py:278
  80.0 13.6 %all-to-all-start.2 = ((f32[8,128,128]{2,1,0:T(8,128)}), f32[8,128,128]{2,1,0:T(8,128)S(1)}, u32[]{:S(2)}, u32[]{:S(2)}) async-start(f32[8,128,128]{2,1,0:T(8,128)} %bitcast.12), calls=%async_computation.2 | async-start | bytes 1048576 | tf_op jit(solution)/shard_map/all_to_all | solution.py:285
  83.5 22.0 %collective-permute-start.9 = (f32[400,256]{1,0:T(8,128)S(1)}, f32[400,256]{1,0:T(8,128)S(1)}, u32[]{:S(2)}, u32[]{:S(2)}) collective-permute-start(f32[400,256]{1,0:T(8,128)S(1)} %get-tuple-element.34.gl_a), channel_id=1, source_target_pairs={{0,1},{1,0},{2,3},{3,2},{4,5},{5,4},{6,7},{7,6},{8,9},{9,8},{10,11... | collective-permute-start | bytes 1228808 | tf_op jit(solution)/shard_map/ppermute | solution.py:306
  85.8 19.7 %collective-permute-start.10 = (f32[400,256]{1,0:T(8,128)S(1)}, f32[400,256]{1,0:T(8,128)S(1)}, u32[]{:S(2)}, u32[]{:S(2)}) collective-permute-start(f32[400,256]{1,0:T(8,128)S(1)} %get-tuple-element.35.gc_a.rest_1_), channel_id=1, source_target_pairs={{0,1},{1,0},{2,3},{3,2},{4,5},{5,4},{6,7},{7,6},{8,9},{9,8},{10,11... | collective-permute-start | bytes 1228808 | tf_op jit(solution)/shard_map/ppermute | solution.py:306
  93.6 4.7 %collective-permute-start.12 = (f32[128,128]{1,0:T(8,128)S(1)}, f32[128,128]{1,0:T(8,128)S(1)}, u32[]{:S(2)}, u32[]{:S(2)}) collective-permute-start(f32[128,128]{1,0:T(8,128)S(1)} %reduce_sum.19), channel_id=1, source_target_pairs={{0,28},{2,30},{4,8},{6,10},{8,4},{10,6},{12,16},{14,18},{16,12},{1... | collective-permute-start | bytes 196616 | tf_op jit(solution)/shard_map/ppermute | solution.py:290
  98.3 6.0 %collective-permute-start.13 = (f32[128,128]{1,0:T(8,128)S(1)}, f32[128,128]{1,0:T(8,128)S(1)}, u32[]{:S(2)}, u32[]{:S(2)}) collective-permute-start(f32[128,128]{1,0:T(8,128)S(1)} %add.14), channel_id=1, source_target_pairs={{0,12},{2,14},{4,24},{6,26},{8,20},{10,22},{12,0},{14,2},{16,28},{... | collective-permute-start | bytes 196616 | tf_op jit(solution)/shard_map/ppermute | solution.py:290
  104.3 3.2 %collective-permute-start.14 = (f32[128,128]{1,0:T(8,128)S(1)}, f32[128,128]{1,0:T(8,128)S(1)}, u32[]{:S(2)}, u32[]{:S(2)}) collective-permute-start(f32[128,128]{1,0:T(8,128)S(1)} %add.15.one), channel_id=1, source_target_pairs={{0,32},{2,34},{4,36},{6,38},{8,40},{10,42},{12,44},{14,46},{16,48}... | collective-permute-start | bytes 196616 | tf_op jit(solution)/shard_map/ppermute | solution.py:291
  117.5 6.2 %collective-permute-start.15 = (f32[1024,128]{1,0:T(8,128)S(1)}, f32[1024,128]{1,0:T(8,128)S(1)}, u32[]{:S(2)}, u32[]{:S(2)}) collective-permute-start(f32[1024,128]{1,0:T(8,128)S(1)} %bitcast.14), channel_id=1, source_target_pairs={{0,2},{2,0},{4,6},{6,4},{8,10},{10,8},{12,14},{14,12},{16,18},{18,... | collective-permute-start | bytes 1572872 | tf_op jit(solution)/shard_map/ppermute | solution.py:302
  122.2 1.5 %copy-start = (f32[400,640]{1,0:T(8,128)S(1)}, f32[400,640]{1,0:T(8,128)}, u32[]{:S(2)}) copy-start(f32[400,640]{1,0:T(8,128)} %get-tuple-element.40.rel) | copy-start | bytes 3072004

commit v4 on v3

--- a/solution.py
+++ b/solution.py
@@ -168,8 +168,10 @@
 
 
 def second_kernel(spans, lidx, ridx, widx, nidx, ends, core, lhs, rhs, rel, wacc,
-                  gw_mine, gw_other, glhs, gctx, keep, send, rel_out, wacc_new,
+                  gw_mine, gw_other, both, keep, send, rel_out, wacc_new,
                   grel, rel_new, sem, *work):
+    d = lhs.shape[0]
+    glhs, gctx = both.at[pl.ds(0, d)], both.at[pl.ds(d, d)]
     join(core[0], gw_mine, gw_other, grel)
     update_rel(rel, wacc, grel, rel_new, wacc_new)
     copy = pltpu.make_async_copy(rel_new, rel_out, sem)
@@ -187,9 +189,11 @@
     )
 
 
-def pair_kernel(lhs, rhs, lacc, racc, gl_a, gl_b, gc_a, gc_b, lhs_new, rhs_new, lacc_new, racc_new):
-    update_pair(lhs, lacc, gl_a, gl_b, lhs_new, lacc_new)
-    update_pair(rhs, racc, gc_a, gc_b, rhs_new, racc_new)
+def pair_kernel(lhs, rhs, lacc, racc, one, two, lhs_new, rhs_new, lacc_new, racc_new):
+    d = lhs.shape[0]
+    first, last = pl.ds(0, d), pl.ds(d, d)
+    update_pair(lhs, lacc, one.at[first], two.at[first], lhs_new, lacc_new)
+    update_pair(rhs, racc, one.at[last], two.at[last], rhs_new, racc_new)
 
 
 def rel_kernel(core, rel, wacc, gw_mine, gw_other, rel_new, wacc_new, grel):
@@ -359,16 +363,16 @@
     gw_mine, gw_other, (lhs1, rhs1, lacc1, racc1) = sum_over_blk(
         keep, send, exchange_first, update_first, True
     )
-    glhs1, gctx1, keep, send, rel, wacc = call(
+    grads, keep, send, rel, wacc = call(
         functools.partial(second_kernel, spans),
         (lidx, ridx, widx, nidx, ends, core, lhs1, rhs1, rel, wacc, gw_mine, gw_other),
         {4: SM, 5: SM},
-        [slab, slab, half, half, pltpu.HBM(table, F32), (1, rels)],
-        [(full, LANES), table, pltpu.SemaphoreType.DMA] + work, 4_000_000_000, 40, {4: HB},
+        [(2 * d, rows), half, half, pltpu.HBM(table, F32), (1, rels)],
+        [(full, LANES), table, pltpu.SemaphoreType.DMA] + work, 4_000_000_000, 40, {3: HB},
     )
 
     def exchange_last():
-        return glhs1, swap(glhs1), gctx1, swap(gctx1)
+        return grads, swap(grads)
 
     def update_last(arrived):
         return call(

time: 126 us -> 126 us (level)
    ppermute x3 -> x2, starting transfers between devices: 3.28 us -> 2.52 us  [swap(): return lax.ppermute(x, 'rel', [(0, 1), (1, 0)])]
  transfers between devices with their start and end apart: 19 -> 18, of which waited for: 13 -> 13; matrix products, arithmetic and copies ran while one was open for 0% -> 0% of each run, Pallas kernels for 1% -> 1%
where the time goes in v4:
time: 126 us
  waiting for transfers between devices  47.1 us (37%)
  starting transfers between devices  42.2 us (33%)
  Pallas kernels  22.5 us (18%)
  blocking collectives  10 us (8%)
  local copies, waits for them, and re-layouts  2.34 us (2%)
    pallas_call x9, Pallas kernels, call(): pl.pallas_call(kernel, out_shape=[jax.ShapeDtypeStruct(o, F32) if isinsta...  22.5 us
    ppermute x4, waiting for transfers between devices, sum_over_blk(): total = total + lax.ppermute(total, 'blk', move)  21.4 us
    all_to_all x1, blocking collectives, sum_over_blk(): mine = lax.all_to_all(spread, 'blk', 0, 0, axis_index_groups=groups)  10 us
    all_to_all x2, waiting for transfers between devices, sum_over_blk(): lax.all_to_all(part.reshape(n, rows, LANES), 'blk', 0, 0, axis_index_grou...  9.56 us
    ppermute x4, starting transfers between devices, sum_over_blk(): total = total + lax.ppermute(total, 'blk', move)  8.73 us
    all_to_all x2, starting transfers between devices, sum_over_blk(): lax.all_to_all(part.reshape(n, rows, LANES), 'blk', 0, 0, axis_index_grou...  7.43 us
    all_to_all x1, waiting for transfers between devices, sum_over_blk(): mine = lax.all_to_all(spread, 'blk', 0, 0, axis_index_groups=groups)  7.42 us
    ppermute x3, starting transfers between devices, onward(): return lax.ppermute(x, ('blk', 'rel'), moves)  7.22 us
  transfers between devices with their start and end apart: 18, of which 13 were waited for; matrix products, arithmetic and copies ran while one was open for 0% of the time, Pallas kernels for 1%

profile of v4, /device:TPU:1, one launch (start us, length us, event | category | flops | bytes accessed | tf_op | source)
XLA Modules:
  0.0 125.6 jit_solution(5919033671260657922)
XLA Ops:
  0.6 9.1 %shard_map.154 = (f32[400,256]{1,0:T(8,128)S(1)}, f32[408,256]{1,0:T(8,128)S(1)}, f32[1024,128]{1,0:T(8,128)S(1)}, f32[1024,128]{1,0:T(8,128)S(1)}) custom-call(s32[1]{0:T(128)} %bitcast.1.core, s32[2,1024]{1,0:T(2,128)} %bitcast.18, s32[2,1024]{1,0:T(2,128)} %bitcast.20, s32[8,128]{1,0:T(8,128)} %bitcast.24, s32[2,1024]{1,0:T(2,128)} %bitcast.22, ...), custom_call_target="tpu_custom_call" | custom-call | flops 4000000000 | bytes 8000000 | tf_op jit(solution)/shard_map/pallas_call | solution.py:231
  9.7 0.0 copy-start.2
  9.7 3.3 %collective-permute-start.4 = (f32[1024,128]{1,0:T(8,128)S(1)}, f32[1024,128]{1,0:T(8,128)S(1)}, u32[]{:S(2)}, u32[]{:S(2)}) collective-permute-start(f32[1024,128]{1,0:T(8,128)S(1)} %get-tuple-element.32), channel_id=1, source_target_pairs={{0,2},{2,0},{4,6},{6,4},{8,10},{10,8},{12,14},{14,12},{16,18},{18,... | collective-permute-start | bytes 1572872 | tf_op jit(solution)/shard_map/ppermute | solution.py:282
  13.1 1.5 %collective-permute-done.4.two = f32[1024,128]{1,0:T(8,128)S(1)} collective-permute-done((f32[1024,128]{1,0:T(8,128)S(1)}, f32[1024,128]{1,0:T(8,128)S(1)}, u32[]{:S(2)}, u32[]{:S(2)}) %collective-permute-start.4) | collective-permute-done | bytes 524320 | tf_op jit(solution)/shard_map/ppermute | solution.py:282
  14.6 0.9 shard_map.156
  15.5 3.9 %all-to-all-start = ((f32[8,128,128]{2,1,0:T(8,128)}), f32[8,128,128]{2,1,0:T(8,128)S(1)}, u32[]{:S(2)}, u32[]{:S(2)}) async-start(f32[8,128,128]{2,1,0:T(8,128)} %bitcast.8), calls=%async_computation | async-start | bytes 1048576 | tf_op jit(solution)/shard_map/all_to_all | solution.py:289
  19.4 4.7 %collective-permute-start.3 = (f32[408,256]{1,0:T(8,128)S(1)}, f32[408,256]{1,0:T(8,128)S(1)}, u32[]{:S(2)}, u32[]{:S(2)}) collective-permute-start(f32[408,256]{1,0:T(8,128)S(1)} %get-tuple-element.26), channel_id=1, source_target_pairs={{0,3},{1,2},{2,5},{3,4},{4,7},{5,6},{6,9},{7,8},{8,11},{9,10},{10,... | collective-permute-start | bytes 1253384 | tf_op jit(solution)/shard_map/ppermute | solution.py:318
  24.2 2.5 %collective-permute-start = (f32[400,256]{1,0:T(8,128)S(1)}, f32[400,256]{1,0:T(8,128)S(1)}, u32[]{:S(2)}, u32[]{:S(2)}) collective-permute-start(f32[400,256]{1,0:T(8,128)S(1)} %copy-done.12), channel_id=1, source_target_pairs={{0,2},{1,3},{2,4},{3,5},{4,6},{5,7},{6,8},{7,9},{8,10},{9,11},{10,... | collective-permute-start | bytes 1228808 | tf_op jit(solution)/shard_map/ppermute | solution.py:318
  26.7 0.2 collective-permute-start.1
  26.9 1.8 %all-to-all-done = f32[8,128,128]{2,1,0:T(8,128)S(1)} async-done(((f32[8,128,128]{2,1,0:T(8,128)}), f32[8,128,128]{2,1,0:T(8,128)S(1)}, u32[]{:S(2)}, u32[]{:S(2)}) %all-to-all-start) | async-done | bytes 524320 | tf_op jit(solution)/shard_map/all_to_all | solution.py:289
  28.7 4.7 %collective-permute-start.5 = (f32[128,128]{1,0:T(8,128)S(1)}, f32[128,128]{1,0:T(8,128)S(1)}, u32[]{:S(2)}, u32[]{:S(2)}) collective-permute-start(f32[128,128]{1,0:T(8,128)S(1)} %reduce_sum.18), channel_id=1, source_target_pairs={{0,28},{2,30},{4,8},{6,10},{8,4},{10,6},{12,16},{14,18},{16,12},{1... | collective-permute-start | bytes 196616 | tf_op jit(solution)/shard_map/ppermute | solution.py:294
  33.5 9.4 %collective-permute-done.5 = f32[128,128]{1,0:T(8,128)S(1)} collective-permute-done((f32[128,128]{1,0:T(8,128)S(1)}, f32[128,128]{1,0:T(8,128)S(1)}, u32[]{:S(2)}, u32[]{:S(2)}) %collective-permute-start.5) | collective-permute-done | bytes 65568 | tf_op jit(solution)/shard_map/ppermute | solution.py:294
  42.9 2.0 %collective-permute-start.6 = (f32[128,128]{1,0:T(8,128)S(1)}, f32[128,128]{1,0:T(8,128)S(1)}, u32[]{:S(2)}, u32[]{:S(2)}) collective-permute-start(f32[128,128]{1,0:T(8,128)S(1)} %add.12), channel_id=1, source_target_pairs={{0,12},{2,14},{4,24},{6,26},{8,20},{10,22},{12,0},{14,2},{16,28},{... | collective-permute-start | bytes 196616 | tf_op jit(solution)/shard_map/ppermute | solution.py:294
  44.8 3.3 %collective-permute-done.6 = f32[128,128]{1,0:T(8,128)S(1)} collective-permute-done((f32[128,128]{1,0:T(8,128)S(1)}, f32[128,128]{1,0:T(8,128)S(1)}, u32[]{:S(2)}, u32[]{:S(2)}) %collective-permute-start.6) | collective-permute-done | bytes 65568 | tf_op jit(solution)/shard_map/ppermute | solution.py:294
  48.2 2.6 %collective-permute-start.7 = (f32[128,128]{1,0:T(8,128)S(1)}, f32[128,128]{1,0:T(8,128)S(1)}, u32[]{:S(2)}, u32[]{:S(2)}) collective-permute-start(f32[128,128]{1,0:T(8,128)S(1)} %add.13.one), channel_id=1, source_target_pairs={{0,32},{2,34},{4,36},{6,38},{8,40},{10,42},{12,44},{14,46},{16,48}... | collective-permute-start | bytes 196616 | tf_op jit(solution)/shard_map/ppermute | solution.py:295
  50.7 0.0 collective-permute-done.rhs.rest_3_
  50.8 1.6 %collective-permute-done.7.two = f32[128,128]{1,0:T(8,128)S(1)} collective-permute-done((f32[128,128]{1,0:T(8,128)S(1)}, f32[128,128]{1,0:T(8,128)S(1)}, u32[]{:S(2)}, u32[]{:S(2)}) %collective-permute-start.7) | collective-permute-done | bytes 65568 | tf_op jit(solution)/shard_map/ppermute | solution.py:295
  52.4 0.8 shard_map.157
  53.2 4.3 %all-to-all-start.1 = ((f32[8,128,128]{2,1,0:T(8,128)}), f32[8,128,128]{2,1,0:T(8,128)S(1)}, u32[]{:S(2)}, u32[]{:S(2)}) async-start(f32[8,128,128]{2,1,0:T(8,128)} %shard_map.157), calls=%async_computation.1 | async-start | bytes 1048576 | tf_op jit(solution)/shard_map/all_to_all | solution.py:301
  57.5 0.7 copy-done.4
  58.2 1.0 copy-done.3
  59.2 0.3 shard_map.155
  59.5 7.4 %all-to-all-done.1 = f32[8,128,128]{2,1,0:T(8,128)S(1)} async-done(((f32[8,128,128]{2,1,0:T(8,128)}), f32[8,128,128]{2,1,0:T(8,128)S(1)}, u32[]{:S(2)}, u32[]{:S(2)}) %all-to-all-start.1) | async-done | bytes 524320 | tf_op jit(solution)/shard_map/all_to_all | solution.py:301
  66.9 0.0 copy-start.9
  66.9 0.0 copy-start.10
  66.9 0.0 copy-start.6
  67.0 0.1 collective-permute-start.8
  67.1 0.6 copy-done.11
  67.7 1.3 %collective-permute-done.8.gw_other = f32[1024,128]{1,0:T(8,128)S(1)} collective-permute-done((f32[1024,128]{1,0:T(8,128)S(1)}, f32[1024,128]{1,0:T(8,128)S(1)}, u32[]{:S(2)}, u32[]{:S(2)}) %collective-permute-start.8) | collective-permute-done | bytes 524320 | tf_op jit(solution)/shard_map/ppermute | solution.py:306
  69.0 8.1 %shard_map.159 = (f32[800,256]{1,0:T(8,128)S(1)}, f32[1024,128]{1,0:T(8,128)S(1)}, f32[1024,128]{1,0:T(8,128)S(1)}, f32[400,640]{1,0:T(8,128)}, f32[1,640]{1,0:T(1,128)S(1)}) custom-call(s32[2,1024]{1,0:T(2,128)S(1)} %bitcast.19, s32[2,1024]{1,0:T(2,128)S(1)} %bitcast.21, s32[2,1024]{1,0:T(2,128)S(1)} %bitcast.23, s32[8,128]{1,0:T(8,128)S(1)} %bitcast.25, ...), custom_call_target="tpu_custom_call" | custom-call | flops 4000000000 | bytes 8000000 | tf_op jit(solution)/shard_map/pallas_call | solution.py:231
  77.1 0.2 collective-permute-start.10
  77.3 1.8 %collective-permute-done.10.two = f32[1024,128]{1,0:T(8,128)S(1)} collective-permute-done((f32[1024,128]{1,0:T(8,128)S(1)}, f32[1024,128]{1,0:T(8,128)S(1)}, u32[]{:S(2)}, u32[]{:S(2)}) %collective-permute-start.10) | collective-permute-done | bytes 524320 | tf_op jit(solution)/shard_map/ppermute | solution.py:282
  79.1 0.9 shard_map.161
  80.0 3.5 %all-to-all-start.2 = ((f32[8,128,128]{2,1,0:T(8,128)}), f32[8,128,128]{2,1,0:T(8,128)S(1)}, u32[]{:S(2)}, u32[]{:S(2)}) async-start(f32[8,128,128]{2,1,0:T(8,128)} %bitcast.12), calls=%async_computation.2 | async-start | bytes 1048576 | tf_op jit(solution)/shard_map/all_to_all | solution.py:289
  83.5 2.3 %collective-permute-start.9 = (f32[800,256]{1,0:T(8,128)S(1)}, f32[800,256]{1,0:T(8,128)S(1)}, u32[]{:S(2)}, u32[]{:S(2)}) collective-permute-start(f32[800,256]{1,0:T(8,128)S(1)} %get-tuple-element.33.one), channel_id=1, source_target_pairs={{0,1},{1,0},{2,3},{3,2},{4,5},{5,4},{6,7},{7,6},{8,9},{9,8},{10,11... | collective-permute-start | bytes 2457608 | tf_op jit(solution)/shard_map/ppermute | solution.py:310
  85.8 7.8 %all-to-all-done.2 = f32[8,128,128]{2,1,0:T(8,128)S(1)} async-done(((f32[8,128,128]{2,1,0:T(8,128)}), f32[8,128,128]{2,1,0:T(8,128)S(1)}, u32[]{:S(2)}, u32[]{:S(2)}) %all-to-all-start.2) | async-done | bytes 524320 | tf_op jit(solution)/shard_map/all_to_all | solution.py:289
  93.6 1.8 %collective-permute-start.11 = (f32[128,128]{1,0:T(8,128)S(1)}, f32[128,128]{1,0:T(8,128)S(1)}, u32[]{:S(2)}, u32[]{:S(2)}) collective-permute-start(f32[128,128]{1,0:T(8,128)S(1)} %reduce_sum.19), channel_id=1, source_target_pairs={{0,28},{2,30},{4,8},{6,10},{8,4},{10,6},{12,16},{14,18},{16,12},{1... | collective-permute-start | bytes 196616 | tf_op jit(solution)/shard_map/ppermute | solution.py:294
  95.4 2.9 %collective-permute-done.11 = f32[128,128]{1,0:T(8,128)S(1)} collective-permute-done((f32[128,128]{1,0:T(8,128)S(1)}, f32[128,128]{1,0:T(8,128)S(1)}, u32[]{:S(2)}, u32[]{:S(2)}) %collective-permute-start.11) | collective-permute-done | bytes 65568 | tf_op jit(solution)/shard_map/ppermute | solution.py:294
  98.3 0.2 collective-permute-start.12
  98.6 5.7 %collective-permute-done.12 = f32[128,128]{1,0:T(8,128)S(1)} collective-permute-done((f32[128,128]{1,0:T(8,128)S(1)}, f32[128,128]{1,0:T(8,128)S(1)}, u32[]{:S(2)}, u32[]{:S(2)}) %collective-permute-start.12) | collective-permute-done | bytes 65568 | tf_op jit(solution)/shard_map/ppermute | solution.py:294
  104.3 1.2 collective-permute-start.13
  105.5 2.0 %collective-permute-done.13.two = f32[128,128]{1,0:T(8,128)S(1)} collective-permute-done((f32[128,128]{1,0:T(8,128)S(1)}, f32[128,128]{1,0:T(8,128)S(1)}, u32[]{:S(2)}, u32[]{:S(2)}) %collective-permute-start.13) | collective-permute-done | bytes 65568 | tf_op jit(solution)/shard_map/ppermute | solution.py:295
  107.5 10.0 %all_to_all.20 = f32[8,128,128]{2,1,0:T(8,128)S(1)} all-to-all(f32[8,128,128]{2,1,0:T(8,128)S(1)} %shard_map.162), channel_id=1, replica_groups={{0,4,64,68,128,132,192,196},{12,8,76,72,140,136,204,200},{16,20,80,84,1..., dimensions={0} | all-to-all | bytes 1048576 | tf_op jit(solution)/shard_map/all_to_all | solution.py:301
  117.6 4.6 %collective-permute-start.14 = (f32[1024,128]{1,0:T(8,128)S(1)}, f32[1024,128]{1,0:T(8,128)S(1)}, u32[]{:S(2)}, u32[]{:S(2)}) collective-permute-start(f32[1024,128]{1,0:T(8,128)S(1)} %bitcast.14), channel_id=1, source_target_pairs={{0,2},{2,0},{4,6},{6,4},{8,10},{10,8},{12,14},{14,12},{16,18},{18,... | collective-permute-start | bytes 1572872 | tf_op jit(solution)/shard_map/ppermute | solution.py:306
  122.2 1.0 shard_map.160
  123.2 0.5 collective-permute-done.14.gw_other
  123.7 1.3 %shard_map.163 = (f32[400,640]{1,0:T(8,128)}, f32[1,640]{1,0:T(1,128)S(1)}) custom-call(s32[1]{0:T(128)} %bitcast.1.core, f32[400,640]{1,0:T(8,128)S(1)} %copy-done, f32[1,640]{1,0:T(1,128)S(1)} %get-tuple-element.39.wacc, f32[1024,128]{1,0:T(8,128)S(1)} %bitcast.15, f32[1024,128]{1,0:T(8,128)S(1)} %collective-permute-done.14.gw_other), custom_call_target="tpu_custom_call" | custom-call | flops 1000000 | bytes 8000000 | tf_op jit(solution)/shard_map/pallas_call | solution.py:231
  125.0 0.6 reduce
  (33 shorter events, 0.2 us)
Async XLA Ops:
  9.7 16.9 %copy-start.2 = (f32[400,256]{1,0:T(8,128)}, f32[400,256]{1,0:T(8,128)S(1)}, u32[]{:S(2)}) copy-start(f32[400,256]{1,0:T(8,128)S(1)} %get-tuple-element.25.gl_a) | copy-start | bytes 1228804
  9.7 4.9 %collective-permute-start.4 = (f32[1024,128]{1,0:T(8,128)S(1)}, f32[1024,128]{1,0:T(8,128)S(1)}, u32[]{:S(2)}, u32[]{:S(2)}) collective-permute-start(f32[1024,128]{1,0:T(8,128)S(1)} %get-tuple-element.32), channel_id=1, source_target_pairs={{0,2},{2,0},{4,6},{6,4},{8,10},{10,8},{12,14},{14,12},{16,18},{18,... | collective-permute-start | bytes 1572872 | tf_op jit(solution)/shard_map/ppermute | solution.py:282
  15.5 8.7 %copy-start.12 = (f32[400,256]{1,0:T(8,128)S(1)}, f32[400,256]{1,0:T(8,128)}, u32[]{:S(2)}) copy-start(f32[400,256]{1,0:T(8,128)} %rhs_hbm.1) | copy-start | bytes 1228804
  15.5 13.2 %all-to-all-start = ((f32[8,128,128]{2,1,0:T(8,128)}), f32[8,128,128]{2,1,0:T(8,128)S(1)}, u32[]{:S(2)}, u32[]{:S(2)}) async-start(f32[8,128,128]{2,1,0:T(8,128)} %bitcast.8), calls=%async_computation | async-start | bytes 1048576 | tf_op jit(solution)/shard_map/all_to_all | solution.py:289
  19.4 31.3 %collective-permute-start.3 = (f32[408,256]{1,0:T(8,128)S(1)}, f32[408,256]{1,0:T(8,128)S(1)}, u32[]{:S(2)}, u32[]{:S(2)}) collective-permute-start(f32[408,256]{1,0:T(8,128)S(1)} %get-tuple-element.26), channel_id=1, source_target_pairs={{0,3},{1,2},{2,5},{3,4},{4,7},{5,6},{6,9},{7,8},{8,11},{9,10},{10,... | collective-permute-start | bytes 1253384 | tf_op jit(solution)/shard_map/ppermute | solution.py:318
  24.2 26.6 %collective-permute-start.2 = (f32[408,256]{1,0:T(8,128)S(1)}, f32[408,256]{1,0:T(8,128)S(1)}, u32[]{:S(2)}, u32[]{:S(2)}) collective-permute-start(f32[408,256]{1,0:T(8,128)S(1)} %get-tuple-element.26), channel_id=1, source_target_pairs={{0,2},{1,3},{2,4},{3,5},{4,6},{5,7},{6,8},{7,9},{8,10},{9,11},{10,... | collective-permute-start | bytes 1253384 | tf_op jit(solution)/shard_map/ppermute | solution.py:318
  24.2 26.6 %collective-permute-start = (f32[400,256]{1,0:T(8,128)S(1)}, f32[400,256]{1,0:T(8,128)S(1)}, u32[]{:S(2)}, u32[]{:S(2)}) collective-permute-start(f32[400,256]{1,0:T(8,128)S(1)} %copy-done.12), channel_id=1, source_target_pairs={{0,2},{1,3},{2,4},{3,5},{4,6},{5,7},{6,8},{7,9},{8,10},{9,11},{10,... | collective-permute-start | bytes 1228808 | tf_op jit(solution)/shard_map/ppermute | solution.py:318
  26.7 24.1 %collective-permute-start.1 = (f32[400,256]{1,0:T(8,128)S(1)}, f32[400,256]{1,0:T(8,128)S(1)}, u32[]{:S(2)}, u32[]{:S(2)}) collective-permute-start(f32[400,256]{1,0:T(8,128)S(1)} %get-tuple-element.25.gl_a), channel_id=1, source_target_pairs={{0,1},{1,0},{2,3},{3,2},{4,5},{5,4},{6,7},{7,6},{8,9},{9,8},{10,11... | collective-permute-start | bytes 1228808 | tf_op jit(solution)/shard_map/ppermute | solution.py:310
  28.7 14.1 %collective-permute-start.5 = (f32[128,128]{1,0:T(8,128)S(1)}, f32[128,128]{1,0:T(8,128)S(1)}, u32[]{:S(2)}, u32[]{:S(2)}) collective-permute-start(f32[128,128]{1,0:T(8,128)S(1)} %reduce_sum.18), channel_id=1, source_target_pairs={{0,28},{2,30},{4,8},{6,10},{8,4},{10,6},{12,16},{14,18},{16,12},{1... | collective-permute-start | bytes 196616 | tf_op jit(solution)/shard_map/ppermute | solution.py:294
  42.9 5.3 %collective-permute-start.6 = (f32[128,128]{1,0:T(8,128)S(1)}, f32[128,128]{1,0:T(8,128)S(1)}, u32[]{:S(2)}, u32[]{:S(2)}) collective-permute-start(f32[128,128]{1,0:T(8,128)S(1)} %add.12), channel_id=1, source_target_pairs={{0,12},{2,14},{4,24},{6,26},{8,20},{10,22},{12,0},{14,2},{16,28},{... | collective-permute-start | bytes 196616 | tf_op jit(solution)/shard_map/ppermute | solution.py:294
  48.2 4.2 %collective-permute-start.7 = (f32[128,128]{1,0:T(8,128)S(1)}, f32[128,128]{1,0:T(8,128)S(1)}, u32[]{:S(2)}, u32[]{:S(2)}) collective-permute-start(f32[128,128]{1,0:T(8,128)S(1)} %add.13.one), channel_id=1, source_target_pairs={{0,32},{2,34},{4,36},{6,38},{8,40},{10,42},{12,44},{14,46},{16,48}... | collective-permute-start | bytes 196616 | tf_op jit(solution)/shard_map/ppermute | solution.py:295
  53.2 4.3 %copy-start.1 = (f32[400,256]{1,0:T(8,128)S(1)}, f32[400,256]{1,0:T(8,128)}, u32[]{:S(2)}) copy-start(f32[400,256]{1,0:T(8,128)} %lhs.2) | copy-start | bytes 1228804
  53.2 13.7 %all-to-all-start.1 = ((f32[8,128,128]{2,1,0:T(8,128)}), f32[8,128,128]{2,1,0:T(8,128)S(1)}, u32[]{:S(2)}, u32[]{:S(2)}) async-start(f32[8,128,128]{2,1,0:T(8,128)} %shard_map.157), calls=%async_computation.1 | async-start | bytes 1048576 | tf_op jit(solution)/shard_map/all_to_all | solution.py:301
  57.5 0.7 copy-start.4
  58.2 1.0 copy-start.3
  66.9 2.1 %copy-start.5 = (f32[400,640]{1,0:T(8,128)S(1)}, f32[400,640]{1,0:T(8,128)}, u32[]{:S(2)}) copy-start(f32[400,640]{1,0:T(8,128)} %rel.1) | copy-start | bytes 3072004
  66.9 0.8 copy-start.11
  66.9 2.1 %copy-start.7 = (s32[1,1,2,1024]{3,2,1,0:T(2,128)S(1)}, s32[1,1,2,1024]{3,2,1,0:T(2,128)}, u32[]{:S(2)}) copy-start(s32[1,1,2,1024]{3,2,1,0:T(2,128)} %param.18) | copy-start | bytes 24580
  66.9 2.1 %copy-start.8 = (s32[1,1,2,1024]{3,2,1,0:T(2,128)S(1)}, s32[1,1,2,1024]{3,2,1,0:T(2,128)}, u32[]{:S(2)}) copy-start(s32[1,1,2,1024]{3,2,1,0:T(2,128)} %param.19) | copy-start | bytes 24580
  66.9 2.1 %copy-start.9 = (s32[1,1,2,4,128]{4,3,2,1,0:T(4,128)S(1)}, s32[1,1,2,4,128]{4,3,2,1,0:T(4,128)}, u32[]{:S(2)}) copy-start(s32[1,1,2,4,128]{4,3,2,1,0:T(4,128)} %param.21) | copy-start | bytes 12292
  66.9 2.1 %copy-start.10 = (s32[1,1,2]{2,1,0:T(1,128)S(1)}, s32[1,1,2]{2,1,0:T(1,128)}, u32[]{:S(2)}) copy-start(s32[1,1,2]{2,1,0:T(1,128)} %param.20) | copy-start | bytes 28
  66.9 2.0 %copy-start.6 = (s32[1,1,2,1024]{3,2,1,0:T(2,128)S(1)}, s32[1,1,2,1024]{3,2,1,0:T(2,128)}, u32[]{:S(2)}) copy-start(s32[1,1,2,1024]{3,2,1,0:T(2,128)} %param.17) | copy-start | bytes 24580
  67.0 2.0 %collective-permute-start.8 = (f32[1024,128]{1,0:T(8,128)S(1)}, f32[1024,128]{1,0:T(8,128)S(1)}, u32[]{:S(2)}, u32[]{:S(2)}) collective-permute-start(f32[1024,128]{1,0:T(8,128)S(1)} %shard_map.158.gw_mine), channel_id=1, source_target_pairs={{0,2},{2,0},{4,6},{6,4},{8,10},{10,8},{12,14},{14,12},{16,18},{18,... | collective-permute-start | bytes 1572872 | tf_op jit(solution)/shard_map/ppermute | solution.py:306
  77.1 2.0 %collective-permute-start.10 = (f32[1024,128]{1,0:T(8,128)S(1)}, f32[1024,128]{1,0:T(8,128)S(1)}, u32[]{:S(2)}, u32[]{:S(2)}) collective-permute-start(f32[1024,128]{1,0:T(8,128)S(1)} %get-tuple-element.41), channel_id=1, source_target_pairs={{0,2},{2,0},{4,6},{6,4},{8,10},{10,8},{12,14},{14,12},{16,18},{18,... | collective-permute-start | bytes 1572872 | tf_op jit(solution)/shard_map/ppermute | solution.py:282
  80.0 13.6 %all-to-all-start.2 = ((f32[8,128,128]{2,1,0:T(8,128)}), f32[8,128,128]{2,1,0:T(8,128)S(1)}, u32[]{:S(2)}, u32[]{:S(2)}) async-start(f32[8,128,128]{2,1,0:T(8,128)} %bitcast.12), calls=%async_computation.2 | async-start | bytes 1048576 | tf_op jit(solution)/shard_map/all_to_all | solution.py:289
  83.5 22.0 %collective-permute-start.9 = (f32[800,256]{1,0:T(8,128)S(1)}, f32[800,256]{1,0:T(8,128)S(1)}, u32[]{:S(2)}, u32[]{:S(2)}) collective-permute-start(f32[800,256]{1,0:T(8,128)S(1)} %get-tuple-element.33.one), channel_id=1, source_target_pairs={{0,1},{1,0},{2,3},{3,2},{4,5},{5,4},{6,7},{7,6},{8,9},{9,8},{10,11... | collective-permute-start | bytes 2457608 | tf_op jit(solution)/shard_map/ppermute | solution.py:310
  93.6 4.7 %collective-permute-start.11 = (f32[128,128]{1,0:T(8,128)S(1)}, f32[128,128]{1,0:T(8,128)S(1)}, u32[]{:S(2)}, u32[]{:S(2)}) collective-permute-start(f32[128,128]{1,0:T(8,128)S(1)} %reduce_sum.19), channel_id=1, source_target_pairs={{0,28},{2,30},{4,8},{6,10},{8,4},{10,6},{12,16},{14,18},{16,12},{1... | collective-permute-start | bytes 196616 | tf_op jit(solution)/shard_map/ppermute | solution.py:294
  98.3 6.0 %collective-permute-start.12 = (f32[128,128]{1,0:T(8,128)S(1)}, f32[128,128]{1,0:T(8,128)S(1)}, u32[]{:S(2)}, u32[]{:S(2)}) collective-permute-start(f32[128,128]{1,0:T(8,128)S(1)} %add.14), channel_id=1, source_target_pairs={{0,12},{2,14},{4,24},{6,26},{8,20},{10,22},{12,0},{14,2},{16,28},{... | collective-permute-start | bytes 196616 | tf_op jit(solution)/shard_map/ppermute | solution.py:294
  104.3 3.2 %collective-permute-start.13 = (f32[128,128]{1,0:T(8,128)S(1)}, f32[128,128]{1,0:T(8,128)S(1)}, u32[]{:S(2)}, u32[]{:S(2)}) collective-permute-start(f32[128,128]{1,0:T(8,128)S(1)} %add.15.one), channel_id=1, source_target_pairs={{0,32},{2,34},{4,36},{6,38},{8,40},{10,42},{12,44},{14,46},{16,48}... | collective-permute-start | bytes 196616 | tf_op jit(solution)/shard_map/ppermute | solution.py:295
  117.6 6.1 %collective-permute-start.14 = (f32[1024,128]{1,0:T(8,128)S(1)}, f32[1024,128]{1,0:T(8,128)S(1)}, u32[]{:S(2)}, u32[]{:S(2)}) collective-permute-start(f32[1024,128]{1,0:T(8,128)S(1)} %bitcast.14), channel_id=1, source_target_pairs={{0,2},{2,0},{4,6},{6,4},{8,10},{10,8},{12,14},{14,12},{16,18},{18,... | collective-permute-start | bytes 1572872 | tf_op jit(solution)/shard_map/ppermute | solution.py:306
  122.2 1.5 %copy-start = (f32[400,640]{1,0:T(8,128)S(1)}, f32[400,640]{1,0:T(8,128)}, u32[]{:S(2)}) copy-start(f32[400,640]{1,0:T(8,128)} %get-tuple-element.38.rel) | copy-start | bytes 3072004

commit v5 on v4

--- a/solution.py
+++ b/solution.py
@@ -53,14 +53,16 @@
         return one_hot(nidx[pl.ds(t * spans + c, 1), :], rows)
 
     rh, rl = split(rhs[...])
-    for c in range(spans):
-        hot_n = hot_neg(c)
+    for c in range(0, spans, 2):
+        some = range(c, min(c + 2, spans))
+        hot_n = jnp.concatenate([hot_neg(i) for i in some], axis=1)
+        at = pl.ds(c * neg, len(some) * neg)
         q = nn(rh, hot_n)
-        qh[:, nats[c]] = q.astype(BF16)
-        qht[nats[c], :] = q.T.astype(BF16)
+        qh[:, at] = q.astype(BF16)
+        qht[at, :] = q.T.astype(BF16)
         q = nn(rl, hot_n)
-        ql[:, nats[c]] = q.astype(BF16)
-        qlt[nats[c], :] = q.T.astype(BF16)
+        ql[:, at] = q.astype(BF16)
+        qlt[at, :] = q.T.astype(BF16)
     for c in range(spans):
         hot = one_hot(ridx[pl.ds(t, 1), ats[c]], rows)
         right[:, ats[c]] = nn(rh, hot) + nn(rl, hot)
@@ -94,7 +96,10 @@
         coefs.append(split(jax.nn.sigmoid(scores) * (lives[c] / neg)))
     for c in range(spans):
         ch, cl = coefs[c]
-        mixture = nn(qh[:, nats[c]], ch) + (nn(qh[:, nats[c]], cl) + nn(ql[:, nats[c]], ch))
+        high = qh[:, nats[c]]
+        mixture = nn(
+            jnp.concatenate([high, high], axis=1), jnp.concatenate([ch, cl], axis=0)
+        ) + nn(ql[:, nats[c]], ch)
         toward = pcoefs[c] * right[:, ats[c]] + mixture
         uh[:, ats[c]], ul[:, ats[c]] = split(left[:, ats[c]] * toward)
         vh[:, ats[c]], vl[:, ats[c]] = split(wts[:, ats[c]] * toward)

time: 126 us -> 125 us (level)
  no operation moved by 1% of the time
where the time goes in v5:
time: 125 us
  waiting for transfers between devices  47.2 us (38%)
  starting transfers between devices  42.1 us (34%)
  Pallas kernels  21.8 us (17%)
  blocking collectives  10 us (8%)
  local copies, waits for them, and re-layouts  2.33 us (2%)
    pallas_call x9, Pallas kernels, call(): pl.pallas_call(kernel, out_shape=[jax.ShapeDtypeStruct(o, F32) if isinsta...  21.8 us
    ppermute x4, waiting for transfers between devices, sum_over_blk(): total = total + lax.ppermute(total, 'blk', move)  21.4 us
    all_to_all x1, blocking collectives, sum_over_blk(): mine = lax.all_to_all(spread, 'blk', 0, 0, axis_index_groups=groups)  10 us
    all_to_all x2, waiting for transfers between devices, sum_over_blk(): lax.all_to_all(part.reshape(n, rows, LANES), 'blk', 0, 0, axis_index_grou...  9.56 us
    ppermute x4, starting transfers between devices, sum_over_blk(): total = total + lax.ppermute(total, 'blk', move)  8.68 us
    all_to_all x2, starting transfers between devices, sum_over_blk(): lax.all_to_all(part.reshape(n, rows, LANES), 'blk', 0, 0, axis_index_grou...  7.43 us
    all_to_all x1, waiting for transfers between devices, sum_over_blk(): mine = lax.all_to_all(spread, 'blk', 0, 0, axis_index_groups=groups)  7.41 us
    ppermute x3, starting transfers between devices, onward(): return lax.ppermute(x, ('blk', 'rel'), moves)  7.22 us
  transfers between devices with their start and end apart: 18, of which 13 were waited for; matrix products, arithmetic and copies ran while one was open for 0% of the time, Pallas kernels for 1%

profile of v5, /device:TPU:1, one launch (start us, length us, event | category | flops | bytes accessed | tf_op | source)
XLA Modules:
  0.0 124.9 jit_solution(806022246069173163)
XLA Ops:
  0.6 8.7 %shard_map.154 = (f32[400,256]{1,0:T(8,128)S(1)}, f32[408,256]{1,0:T(8,128)S(1)}, f32[1024,128]{1,0:T(8,128)S(1)}, f32[1024,128]{1,0:T(8,128)S(1)}) custom-call(s32[1]{0:T(128)} %bitcast.1.core, s32[2,1024]{1,0:T(2,128)} %bitcast.18, s32[2,1024]{1,0:T(2,128)} %bitcast.20, s32[8,128]{1,0:T(8,128)} %bitcast.24, s32[2,1024]{1,0:T(2,128)} %bitcast.22, ...), custom_call_target="tpu_custom_call" | custom-call | flops 4000000000 | bytes 8000000 | tf_op jit(solution)/shard_map/pallas_call | solution.py:236
  9.4 0.0 copy-start.2
  9.4 3.3 %collective-permute-start.4 = (f32[1024,128]{1,0:T(8,128)S(1)}, f32[1024,128]{1,0:T(8,128)S(1)}, u32[]{:S(2)}, u32[]{:S(2)}) collective-permute-start(f32[1024,128]{1,0:T(8,128)S(1)} %get-tuple-element.32), channel_id=1, source_target_pairs={{0,2},{2,0},{4,6},{6,4},{8,10},{10,8},{12,14},{14,12},{16,18},{18,... | collective-permute-start | bytes 1572872 | tf_op jit(solution)/shard_map/ppermute | solution.py:287
  12.7 1.5 %collective-permute-done.4.two = f32[1024,128]{1,0:T(8,128)S(1)} collective-permute-done((f32[1024,128]{1,0:T(8,128)S(1)}, f32[1024,128]{1,0:T(8,128)S(1)}, u32[]{:S(2)}, u32[]{:S(2)}) %collective-permute-start.4) | collective-permute-done | bytes 524320 | tf_op jit(solution)/shard_map/ppermute | solution.py:287
  14.3 0.9 shard_map.156
  15.1 3.9 %all-to-all-start = ((f32[8,128,128]{2,1,0:T(8,128)}), f32[8,128,128]{2,1,0:T(8,128)S(1)}, u32[]{:S(2)}, u32[]{:S(2)}) async-start(f32[8,128,128]{2,1,0:T(8,128)} %bitcast.8), calls=%async_computation | async-start | bytes 1048576 | tf_op jit(solution)/shard_map/all_to_all | solution.py:294
  19.1 4.7 %collective-permute-start.3 = (f32[408,256]{1,0:T(8,128)S(1)}, f32[408,256]{1,0:T(8,128)S(1)}, u32[]{:S(2)}, u32[]{:S(2)}) collective-permute-start(f32[408,256]{1,0:T(8,128)S(1)} %get-tuple-element.26), channel_id=1, source_target_pairs={{0,3},{1,2},{2,5},{3,4},{4,7},{5,6},{6,9},{7,8},{8,11},{9,10},{10,... | collective-permute-start | bytes 1253384 | tf_op jit(solution)/shard_map/ppermute | solution.py:323
  23.8 2.5 %collective-permute-start = (f32[400,256]{1,0:T(8,128)S(1)}, f32[400,256]{1,0:T(8,128)S(1)}, u32[]{:S(2)}, u32[]{:S(2)}) collective-permute-start(f32[400,256]{1,0:T(8,128)S(1)} %copy-done.12), channel_id=1, source_target_pairs={{0,2},{1,3},{2,4},{3,5},{4,6},{5,7},{6,8},{7,9},{8,10},{9,11},{10,... | collective-permute-start | bytes 1228808 | tf_op jit(solution)/shard_map/ppermute | solution.py:323
  26.3 0.2 collective-permute-start.1
  26.5 1.8 %all-to-all-done = f32[8,128,128]{2,1,0:T(8,128)S(1)} async-done(((f32[8,128,128]{2,1,0:T(8,128)}), f32[8,128,128]{2,1,0:T(8,128)S(1)}, u32[]{:S(2)}, u32[]{:S(2)}) %all-to-all-start) | async-done | bytes 524320 | tf_op jit(solution)/shard_map/all_to_all | solution.py:294
  28.4 4.7 %collective-permute-start.5 = (f32[128,128]{1,0:T(8,128)S(1)}, f32[128,128]{1,0:T(8,128)S(1)}, u32[]{:S(2)}, u32[]{:S(2)}) collective-permute-start(f32[128,128]{1,0:T(8,128)S(1)} %reduce_sum.18), channel_id=1, source_target_pairs={{0,28},{2,30},{4,8},{6,10},{8,4},{10,6},{12,16},{14,18},{16,12},{1... | collective-permute-start | bytes 196616 | tf_op jit(solution)/shard_map/ppermute | solution.py:299
  33.1 9.4 %collective-permute-done.5 = f32[128,128]{1,0:T(8,128)S(1)} collective-permute-done((f32[128,128]{1,0:T(8,128)S(1)}, f32[128,128]{1,0:T(8,128)S(1)}, u32[]{:S(2)}, u32[]{:S(2)}) %collective-permute-start.5) | collective-permute-done | bytes 65568 | tf_op jit(solution)/shard_map/ppermute | solution.py:299
  42.5 1.9 %collective-permute-start.6 = (f32[128,128]{1,0:T(8,128)S(1)}, f32[128,128]{1,0:T(8,128)S(1)}, u32[]{:S(2)}, u32[]{:S(2)}) collective-permute-start(f32[128,128]{1,0:T(8,128)S(1)} %add.12), channel_id=1, source_target_pairs={{0,12},{2,14},{4,24},{6,26},{8,20},{10,22},{12,0},{14,2},{16,28},{... | collective-permute-start | bytes 196616 | tf_op jit(solution)/shard_map/ppermute | solution.py:299
  44.5 3.4 %collective-permute-done.6 = f32[128,128]{1,0:T(8,128)S(1)} collective-permute-done((f32[128,128]{1,0:T(8,128)S(1)}, f32[128,128]{1,0:T(8,128)S(1)}, u32[]{:S(2)}, u32[]{:S(2)}) %collective-permute-start.6) | collective-permute-done | bytes 65568 | tf_op jit(solution)/shard_map/ppermute | solution.py:299
  47.8 2.6 %collective-permute-start.7 = (f32[128,128]{1,0:T(8,128)S(1)}, f32[128,128]{1,0:T(8,128)S(1)}, u32[]{:S(2)}, u32[]{:S(2)}) collective-permute-start(f32[128,128]{1,0:T(8,128)S(1)} %add.13.one), channel_id=1, source_target_pairs={{0,32},{2,34},{4,36},{6,38},{8,40},{10,42},{12,44},{14,46},{16,48}... | collective-permute-start | bytes 196616 | tf_op jit(solution)/shard_map/ppermute | solution.py:300
  50.4 0.0 collective-permute-done.rhs.rest_3_
  50.4 1.6 %collective-permute-done.7.two = f32[128,128]{1,0:T(8,128)S(1)} collective-permute-done((f32[128,128]{1,0:T(8,128)S(1)}, f32[128,128]{1,0:T(8,128)S(1)}, u32[]{:S(2)}, u32[]{:S(2)}) %collective-permute-start.7) | collective-permute-done | bytes 65568 | tf_op jit(solution)/shard_map/ppermute | solution.py:300
  52.1 0.8 shard_map.157
  52.9 4.3 %all-to-all-start.1 = ((f32[8,128,128]{2,1,0:T(8,128)}), f32[8,128,128]{2,1,0:T(8,128)S(1)}, u32[]{:S(2)}, u32[]{:S(2)}) async-start(f32[8,128,128]{2,1,0:T(8,128)} %shard_map.157), calls=%async_computation.1 | async-start | bytes 1048576 | tf_op jit(solution)/shard_map/all_to_all | solution.py:306
  57.2 0.7 copy-done.4
  57.9 1.0 copy-done.3
  58.9 0.3 shard_map.155
  59.1 7.4 %all-to-all-done.1 = f32[8,128,128]{2,1,0:T(8,128)S(1)} async-done(((f32[8,128,128]{2,1,0:T(8,128)}), f32[8,128,128]{2,1,0:T(8,128)S(1)}, u32[]{:S(2)}, u32[]{:S(2)}) %all-to-all-start.1) | async-done | bytes 524320 | tf_op jit(solution)/shard_map/all_to_all | solution.py:306
  66.6 0.0 copy-start.9
  66.6 0.0 copy-start.10
  66.6 0.0 copy-start.6
  66.6 0.1 collective-permute-start.8
  66.7 0.6 copy-done.11
  67.3 1.3 %collective-permute-done.8.gw_other = f32[1024,128]{1,0:T(8,128)S(1)} collective-permute-done((f32[1024,128]{1,0:T(8,128)S(1)}, f32[1024,128]{1,0:T(8,128)S(1)}, u32[]{:S(2)}, u32[]{:S(2)}) %collective-permute-start.8) | collective-permute-done | bytes 524320 | tf_op jit(solution)/shard_map/ppermute | solution.py:311
  68.7 7.8 %shard_map.159 = (f32[800,256]{1,0:T(8,128)S(1)}, f32[1024,128]{1,0:T(8,128)S(1)}, f32[1024,128]{1,0:T(8,128)S(1)}, f32[400,640]{1,0:T(8,128)}, f32[1,640]{1,0:T(1,128)S(1)}) custom-call(s32[2,1024]{1,0:T(2,128)S(1)} %bitcast.19, s32[2,1024]{1,0:T(2,128)S(1)} %bitcast.21, s32[2,1024]{1,0:T(2,128)S(1)} %bitcast.23, s32[8,128]{1,0:T(8,128)S(1)} %bitcast.25, ...), custom_call_target="tpu_custom_call" | custom-call | flops 4000000000 | bytes 8000000 | tf_op jit(solution)/shard_map/pallas_call | solution.py:236
  76.4 0.2 collective-permute-start.10
  76.6 1.8 %collective-permute-done.10.two = f32[1024,128]{1,0:T(8,128)S(1)} collective-permute-done((f32[1024,128]{1,0:T(8,128)S(1)}, f32[1024,128]{1,0:T(8,128)S(1)}, u32[]{:S(2)}, u32[]{:S(2)}) %collective-permute-start.10) | collective-permute-done | bytes 524320 | tf_op jit(solution)/shard_map/ppermute | solution.py:287
  78.4 0.9 shard_map.161
  79.3 3.5 %all-to-all-start.2 = ((f32[8,128,128]{2,1,0:T(8,128)}), f32[8,128,128]{2,1,0:T(8,128)S(1)}, u32[]{:S(2)}, u32[]{:S(2)}) async-start(f32[8,128,128]{2,1,0:T(8,128)} %bitcast.12), calls=%async_computation.2 | async-start | bytes 1048576 | tf_op jit(solution)/shard_map/all_to_all | solution.py:294
  82.8 2.3 %collective-permute-start.9 = (f32[800,256]{1,0:T(8,128)S(1)}, f32[800,256]{1,0:T(8,128)S(1)}, u32[]{:S(2)}, u32[]{:S(2)}) collective-permute-start(f32[800,256]{1,0:T(8,128)S(1)} %get-tuple-element.33.one), channel_id=1, source_target_pairs={{0,1},{1,0},{2,3},{3,2},{4,5},{5,4},{6,7},{7,6},{8,9},{9,8},{10,11... | collective-permute-start | bytes 2457608 | tf_op jit(solution)/shard_map/ppermute | solution.py:315
  85.1 7.8 %all-to-all-done.2 = f32[8,128,128]{2,1,0:T(8,128)S(1)} async-done(((f32[8,128,128]{2,1,0:T(8,128)}), f32[8,128,128]{2,1,0:T(8,128)S(1)}, u32[]{:S(2)}, u32[]{:S(2)}) %all-to-all-start.2) | async-done | bytes 524320 | tf_op jit(solution)/shard_map/all_to_all | solution.py:294
  92.9 1.8 %collective-permute-start.11 = (f32[128,128]{1,0:T(8,128)S(1)}, f32[128,128]{1,0:T(8,128)S(1)}, u32[]{:S(2)}, u32[]{:S(2)}) collective-permute-start(f32[128,128]{1,0:T(8,128)S(1)} %reduce_sum.19), channel_id=1, source_target_pairs={{0,28},{2,30},{4,8},{6,10},{8,4},{10,6},{12,16},{14,18},{16,12},{1... | collective-permute-start | bytes 196616 | tf_op jit(solution)/shard_map/ppermute | solution.py:299
  94.8 2.9 %collective-permute-done.11 = f32[128,128]{1,0:T(8,128)S(1)} collective-permute-done((f32[128,128]{1,0:T(8,128)S(1)}, f32[128,128]{1,0:T(8,128)S(1)}, u32[]{:S(2)}, u32[]{:S(2)}) %collective-permute-start.11) | collective-permute-done | bytes 65568 | tf_op jit(solution)/shard_map/ppermute | solution.py:299
  97.7 0.2 collective-permute-start.12
  97.8 5.8 %collective-permute-done.12 = f32[128,128]{1,0:T(8,128)S(1)} collective-permute-done((f32[128,128]{1,0:T(8,128)S(1)}, f32[128,128]{1,0:T(8,128)S(1)}, u32[]{:S(2)}, u32[]{:S(2)}) %collective-permute-start.12) | collective-permute-done | bytes 65568 | tf_op jit(solution)/shard_map/ppermute | solution.py:299
  103.6 1.2 collective-permute-start.13
  104.8 2.0 %collective-permute-done.13.two = f32[128,128]{1,0:T(8,128)S(1)} collective-permute-done((f32[128,128]{1,0:T(8,128)S(1)}, f32[128,128]{1,0:T(8,128)S(1)}, u32[]{:S(2)}, u32[]{:S(2)}) %collective-permute-start.13) | collective-permute-done | bytes 65568 | tf_op jit(solution)/shard_map/ppermute | solution.py:300
  106.9 10.0 %all_to_all.20 = f32[8,128,128]{2,1,0:T(8,128)S(1)} all-to-all(f32[8,128,128]{2,1,0:T(8,128)S(1)} %shard_map.162), channel_id=1, replica_groups={{0,4,64,68,128,132,192,196},{12,8,76,72,140,136,204,200},{16,20,80,84,1..., dimensions={0} | all-to-all | bytes 1048576 | tf_op jit(solution)/shard_map/all_to_all | solution.py:306
  116.9 4.6 %collective-permute-start.14 = (f32[1024,128]{1,0:T(8,128)S(1)}, f32[1024,128]{1,0:T(8,128)S(1)}, u32[]{:S(2)}, u32[]{:S(2)}) collective-permute-start(f32[1024,128]{1,0:T(8,128)S(1)} %bitcast.14), channel_id=1, source_target_pairs={{0,2},{2,0},{4,6},{6,4},{8,10},{10,8},{12,14},{14,12},{16,18},{18,... | collective-permute-start | bytes 1572872 | tf_op jit(solution)/shard_map/ppermute | solution.py:311
  121.5 1.0 shard_map.160
  122.5 0.5 collective-permute-done.14.gw_other
  123.0 1.3 %shard_map.163 = (f32[400,640]{1,0:T(8,128)}, f32[1,640]{1,0:T(1,128)S(1)}) custom-call(s32[1]{0:T(128)} %bitcast.1.core, f32[400,640]{1,0:T(8,128)S(1)} %copy-done, f32[1,640]{1,0:T(1,128)S(1)} %get-tuple-element.39.wacc, f32[1024,128]{1,0:T(8,128)S(1)} %bitcast.15, f32[1024,128]{1,0:T(8,128)S(1)} %collective-permute-done.14.gw_other), custom_call_target="tpu_custom_call" | custom-call | flops 1000000 | bytes 8000000 | tf_op jit(solution)/shard_map/pallas_call | solution.py:236
  124.3 0.6 reduce
  (33 shorter events, 0.2 us)
Async XLA Ops:
  9.4 16.9 %copy-start.2 = (f32[400,256]{1,0:T(8,128)}, f32[400,256]{1,0:T(8,128)S(1)}, u32[]{:S(2)}) copy-start(f32[400,256]{1,0:T(8,128)S(1)} %get-tuple-element.25.gl_a) | copy-start | bytes 1228804
  9.4 4.9 %collective-permute-start.4 = (f32[1024,128]{1,0:T(8,128)S(1)}, f32[1024,128]{1,0:T(8,128)S(1)}, u32[]{:S(2)}, u32[]{:S(2)}) collective-permute-start(f32[1024,128]{1,0:T(8,128)S(1)} %get-tuple-element.32), channel_id=1, source_target_pairs={{0,2},{2,0},{4,6},{6,4},{8,10},{10,8},{12,14},{14,12},{16,18},{18,... | collective-permute-start | bytes 1572872 | tf_op jit(solution)/shard_map/ppermute | solution.py:287
  15.1 8.7 %copy-start.12 = (f32[400,256]{1,0:T(8,128)S(1)}, f32[400,256]{1,0:T(8,128)}, u32[]{:S(2)}) copy-start(f32[400,256]{1,0:T(8,128)} %rhs_hbm.1) | copy-start | bytes 1228804
  15.1 13.2 %all-to-all-start = ((f32[8,128,128]{2,1,0:T(8,128)}), f32[8,128,128]{2,1,0:T(8,128)S(1)}, u32[]{:S(2)}, u32[]{:S(2)}) async-start(f32[8,128,128]{2,1,0:T(8,128)} %bitcast.8), calls=%async_computation | async-start | bytes 1048576 | tf_op jit(solution)/shard_map/all_to_all | solution.py:294
  19.1 31.3 %collective-permute-start.3 = (f32[408,256]{1,0:T(8,128)S(1)}, f32[408,256]{1,0:T(8,128)S(1)}, u32[]{:S(2)}, u32[]{:S(2)}) collective-permute-start(f32[408,256]{1,0:T(8,128)S(1)} %get-tuple-element.26), channel_id=1, source_target_pairs={{0,3},{1,2},{2,5},{3,4},{4,7},{5,6},{6,9},{7,8},{8,11},{9,10},{10,... | collective-permute-start | bytes 1253384 | tf_op jit(solution)/shard_map/ppermute | solution.py:323
  23.8 26.6 %collective-permute-start.2 = (f32[408,256]{1,0:T(8,128)S(1)}, f32[408,256]{1,0:T(8,128)S(1)}, u32[]{:S(2)}, u32[]{:S(2)}) collective-permute-start(f32[408,256]{1,0:T(8,128)S(1)} %get-tuple-element.26), channel_id=1, source_target_pairs={{0,2},{1,3},{2,4},{3,5},{4,6},{5,7},{6,8},{7,9},{8,10},{9,11},{10,... | collective-permute-start | bytes 1253384 | tf_op jit(solution)/shard_map/ppermute | solution.py:323
  23.8 26.6 %collective-permute-start = (f32[400,256]{1,0:T(8,128)S(1)}, f32[400,256]{1,0:T(8,128)S(1)}, u32[]{:S(2)}, u32[]{:S(2)}) collective-permute-start(f32[400,256]{1,0:T(8,128)S(1)} %copy-done.12), channel_id=1, source_target_pairs={{0,2},{1,3},{2,4},{3,5},{4,6},{5,7},{6,8},{7,9},{8,10},{9,11},{10,... | collective-permute-start | bytes 1228808 | tf_op jit(solution)/shard_map/ppermute | solution.py:323
  26.3 24.1 %collective-permute-start.1 = (f32[400,256]{1,0:T(8,128)S(1)}, f32[400,256]{1,0:T(8,128)S(1)}, u32[]{:S(2)}, u32[]{:S(2)}) collective-permute-start(f32[400,256]{1,0:T(8,128)S(1)} %get-tuple-element.25.gl_a), channel_id=1, source_target_pairs={{0,1},{1,0},{2,3},{3,2},{4,5},{5,4},{6,7},{7,6},{8,9},{9,8},{10,11... | collective-permute-start | bytes 1228808 | tf_op jit(solution)/shard_map/ppermute | solution.py:315
  28.4 14.1 %collective-permute-start.5 = (f32[128,128]{1,0:T(8,128)S(1)}, f32[128,128]{1,0:T(8,128)S(1)}, u32[]{:S(2)}, u32[]{:S(2)}) collective-permute-start(f32[128,128]{1,0:T(8,128)S(1)} %reduce_sum.18), channel_id=1, source_target_pairs={{0,28},{2,30},{4,8},{6,10},{8,4},{10,6},{12,16},{14,18},{16,12},{1... | collective-permute-start | bytes 196616 | tf_op jit(solution)/shard_map/ppermute | solution.py:299
  42.5 5.3 %collective-permute-start.6 = (f32[128,128]{1,0:T(8,128)S(1)}, f32[128,128]{1,0:T(8,128)S(1)}, u32[]{:S(2)}, u32[]{:S(2)}) collective-permute-start(f32[128,128]{1,0:T(8,128)S(1)} %add.12), channel_id=1, source_target_pairs={{0,12},{2,14},{4,24},{6,26},{8,20},{10,22},{12,0},{14,2},{16,28},{... | collective-permute-start | bytes 196616 | tf_op jit(solution)/shard_map/ppermute | solution.py:299
  47.8 4.2 %collective-permute-start.7 = (f32[128,128]{1,0:T(8,128)S(1)}, f32[128,128]{1,0:T(8,128)S(1)}, u32[]{:S(2)}, u32[]{:S(2)}) collective-permute-start(f32[128,128]{1,0:T(8,128)S(1)} %add.13.one), channel_id=1, source_target_pairs={{0,32},{2,34},{4,36},{6,38},{8,40},{10,42},{12,44},{14,46},{16,48}... | collective-permute-start | bytes 196616 | tf_op jit(solution)/shard_map/ppermute | solution.py:300
  52.9 4.3 %copy-start.1 = (f32[400,256]{1,0:T(8,128)S(1)}, f32[400,256]{1,0:T(8,128)}, u32[]{:S(2)}) copy-start(f32[400,256]{1,0:T(8,128)} %lhs.2) | copy-start | bytes 1228804
  52.9 13.7 %all-to-all-start.1 = ((f32[8,128,128]{2,1,0:T(8,128)}), f32[8,128,128]{2,1,0:T(8,128)S(1)}, u32[]{:S(2)}, u32[]{:S(2)}) async-start(f32[8,128,128]{2,1,0:T(8,128)} %shard_map.157), calls=%async_computation.1 | async-start | bytes 1048576 | tf_op jit(solution)/shard_map/all_to_all | solution.py:306
  57.2 0.7 copy-start.4
  57.9 1.0 copy-start.3
  66.6 2.1 %copy-start.5 = (f32[400,640]{1,0:T(8,128)S(1)}, f32[400,640]{1,0:T(8,128)}, u32[]{:S(2)}) copy-start(f32[400,640]{1,0:T(8,128)} %rel.1) | copy-start | bytes 3072004
  66.6 0.8 copy-start.11
  66.6 2.1 %copy-start.7 = (s32[1,1,2,1024]{3,2,1,0:T(2,128)S(1)}, s32[1,1,2,1024]{3,2,1,0:T(2,128)}, u32[]{:S(2)}) copy-start(s32[1,1,2,1024]{3,2,1,0:T(2,128)} %param.18) | copy-start | bytes 24580
  66.6 2.1 %copy-start.8 = (s32[1,1,2,1024]{3,2,1,0:T(2,128)S(1)}, s32[1,1,2,1024]{3,2,1,0:T(2,128)}, u32[]{:S(2)}) copy-start(s32[1,1,2,1024]{3,2,1,0:T(2,128)} %param.19) | copy-start | bytes 24580
  66.6 2.1 %copy-start.9 = (s32[1,1,2,4,128]{4,3,2,1,0:T(4,128)S(1)}, s32[1,1,2,4,128]{4,3,2,1,0:T(4,128)}, u32[]{:S(2)}) copy-start(s32[1,1,2,4,128]{4,3,2,1,0:T(4,128)} %param.21) | copy-start | bytes 12292
  66.6 2.1 %copy-start.10 = (s32[1,1,2]{2,1,0:T(1,128)S(1)}, s32[1,1,2]{2,1,0:T(1,128)}, u32[]{:S(2)}) copy-start(s32[1,1,2]{2,1,0:T(1,128)} %param.20) | copy-start | bytes 28
  66.6 2.0 %copy-start.6 = (s32[1,1,2,1024]{3,2,1,0:T(2,128)S(1)}, s32[1,1,2,1024]{3,2,1,0:T(2,128)}, u32[]{:S(2)}) copy-start(s32[1,1,2,1024]{3,2,1,0:T(2,128)} %param.17) | copy-start | bytes 24580
  66.6 2.0 %collective-permute-start.8 = (f32[1024,128]{1,0:T(8,128)S(1)}, f32[1024,128]{1,0:T(8,128)S(1)}, u32[]{:S(2)}, u32[]{:S(2)}) collective-permute-start(f32[1024,128]{1,0:T(8,128)S(1)} %shard_map.158.gw_mine), channel_id=1, source_target_pairs={{0,2},{2,0},{4,6},{6,4},{8,10},{10,8},{12,14},{14,12},{16,18},{18,... | collective-permute-start | bytes 1572872 | tf_op jit(solution)/shard_map/ppermute | solution.py:311
  76.4 2.0 %collective-permute-start.10 = (f32[1024,128]{1,0:T(8,128)S(1)}, f32[1024,128]{1,0:T(8,128)S(1)}, u32[]{:S(2)}, u32[]{:S(2)}) collective-permute-start(f32[1024,128]{1,0:T(8,128)S(1)} %get-tuple-element.41), channel_id=1, source_target_pairs={{0,2},{2,0},{4,6},{6,4},{8,10},{10,8},{12,14},{14,12},{16,18},{18,... | collective-permute-start | bytes 1572872 | tf_op jit(solution)/shard_map/ppermute | solution.py:287
  79.3 13.6 %all-to-all-start.2 = ((f32[8,128,128]{2,1,0:T(8,128)}), f32[8,128,128]{2,1,0:T(8,128)S(1)}, u32[]{:S(2)}, u32[]{:S(2)}) async-start(f32[8,128,128]{2,1,0:T(8,128)} %bitcast.12), calls=%async_computation.2 | async-start | bytes 1048576 | tf_op jit(solution)/shard_map/all_to_all | solution.py:294
  82.8 22.0 %collective-permute-start.9 = (f32[800,256]{1,0:T(8,128)S(1)}, f32[800,256]{1,0:T(8,128)S(1)}, u32[]{:S(2)}, u32[]{:S(2)}) collective-permute-start(f32[800,256]{1,0:T(8,128)S(1)} %get-tuple-element.33.one), channel_id=1, source_target_pairs={{0,1},{1,0},{2,3},{3,2},{4,5},{5,4},{6,7},{7,6},{8,9},{9,8},{10,11... | collective-permute-start | bytes 2457608 | tf_op jit(solution)/shard_map/ppermute | solution.py:315
  92.9 4.7 %collective-permute-start.11 = (f32[128,128]{1,0:T(8,128)S(1)}, f32[128,128]{1,0:T(8,128)S(1)}, u32[]{:S(2)}, u32[]{:S(2)}) collective-permute-start(f32[128,128]{1,0:T(8,128)S(1)} %reduce_sum.19), channel_id=1, source_target_pairs={{0,28},{2,30},{4,8},{6,10},{8,4},{10,6},{12,16},{14,18},{16,12},{1... | collective-permute-start | bytes 196616 | tf_op jit(solution)/shard_map/ppermute | solution.py:299
  97.7 6.0 %collective-permute-start.12 = (f32[128,128]{1,0:T(8,128)S(1)}, f32[128,128]{1,0:T(8,128)S(1)}, u32[]{:S(2)}, u32[]{:S(2)}) collective-permute-start(f32[128,128]{1,0:T(8,128)S(1)} %add.14), channel_id=1, source_target_pairs={{0,12},{2,14},{4,24},{6,26},{8,20},{10,22},{12,0},{14,2},{16,28},{... | collective-permute-start | bytes 196616 | tf_op jit(solution)/shard_map/ppermute | solution.py:299
  103.6 3.2 %collective-permute-start.13 = (f32[128,128]{1,0:T(8,128)S(1)}, f32[128,128]{1,0:T(8,128)S(1)}, u32[]{:S(2)}, u32[]{:S(2)}) collective-permute-start(f32[128,128]{1,0:T(8,128)S(1)} %add.15.one), channel_id=1, source_target_pairs={{0,32},{2,34},{4,36},{6,38},{8,40},{10,42},{12,44},{14,46},{16,48}... | collective-permute-start | bytes 196616 | tf_op jit(solution)/shard_map/ppermute | solution.py:300
  116.9 6.1 %collective-permute-start.14 = (f32[1024,128]{1,0:T(8,128)S(1)}, f32[1024,128]{1,0:T(8,128)S(1)}, u32[]{:S(2)}, u32[]{:S(2)}) collective-permute-start(f32[1024,128]{1,0:T(8,128)S(1)} %bitcast.14), channel_id=1, source_target_pairs={{0,2},{2,0},{4,6},{6,4},{8,10},{10,8},{12,14},{14,12},{16,18},{18,... | collective-permute-start | bytes 1572872 | tf_op jit(solution)/shard_map/ppermute | solution.py:311
  121.4 1.5 %copy-start = (f32[400,640]{1,0:T(8,128)S(1)}, f32[400,640]{1,0:T(8,128)}, u32[]{:S(2)}) copy-start(f32[400,640]{1,0:T(8,128)} %get-tuple-element.38.rel) | copy-start | bytes 3072004
